TPU v7x, 32 devices: a whole 2x2x4 slice. The times are simulated.
32 devices in a mesh: rep: 4 (over y, core), shard: 8 (over z, x).
Axes of the slice: x: 2, y: 2, z: 4, core: 2. Of those that a mesh axis runs over, the one named last changes fastest.
Arguments:
- hidden_in: bfloat16 [8192, 1024], P(('rep', 'shard')), may hold values from -6 to 6
- cotangent: bfloat16 [8192, 1024], P(('rep', 'shard')), may hold values from -6 to 6
- ln1_gain: bfloat16 [1024], P('shard'), may hold values from 0.5 to 1.5
- ln1_bias: bfloat16 [1024], P('shard'), may hold values from -3 to 3
- w_qkv: bfloat16 [1024, 3072], P('shard'), may hold values from -16 to 16
- qv_bias: bfloat16 [2048], P('shard'), may hold values from -3 to 3
- w_dense: bfloat16 [1024, 1024], P('shard'), may hold values from -0.75 to 0.75
- dense_bias: bfloat16 [1024], P('shard'), may hold values from -3 to 3
- ln2_gain: bfloat16 [1024], P('shard'), may hold values from 0.5 to 1.5
- ln2_bias: bfloat16 [1024], P('shard'), may hold values from -3 to 3
- w_up: bfloat16 [1024, 4096], P('shard'), may hold values from -0.1875 to 0.1875
- up_bias: bfloat16 [4096], P('shard'), may hold values from -3 to 3
- w_down: bfloat16 [4096, 1024], P('shard'), may hold values from -0.09375 to 0.09375
- down_bias: bfloat16 [1024], P('shard'), may hold values from -3 to 3
Outputs:
- output: bfloat16 [8192, 1024], P(('rep', 'shard'))
- input_grad: float32 [8192, 1024], P(('rep', 'shard'))
- grad_ln1_gain: float32 [1024], P('shard')
- grad_ln1_bias: float32 [1024], P('shard')
- grad_qkv: float32 [1024, 3072], P('shard')
- grad_qv_bias: float32 [2048], P('shard')
- grad_dense: float32 [1024, 1024], P('shard')
- grad_dense_bias: float32 [1024], P('shard')
- grad_ln2_gain: float32 [1024], P('shard')
- grad_ln2_bias: float32 [1024], P('shard')
- grad_up: float32 [1024, 4096], P('shard')
- grad_up_bias: float32 [4096], P('shard')
- grad_down: float32 [4096, 1024], P('shard')
- grad_down_bias: float32 [1024], P('shard')
All inputs are finite; a program needn't handle non-finite values.
Results may differ from a plain program's by a relative error of at most 0.0092.
Values may be sent and summed in bfloat16 or wider, within the bound.
No kernel may reach another device: no remote copies, remote signals or barrier semaphores. Data moves between devices by JAX's collectives and lax.ppermute only.
A program may use at most 192 MiB of HBM per device.

v0:
```python
import math

import jax
import jax.numpy as jnp
from jax import lax
from jax.sharding import PartitionSpec as P

H = 16


gelu_coef = math.sqrt(2.0 / math.pi)


def head_slopes(head_count):
    return 2.0 ** (-8.0 * (jnp.arange(head_count, dtype=jnp.float32) + 1.0) / head_count)


def layer_norm(values_in):
    centre = values_in - jnp.mean(values_in, axis=-1, keepdims=True)
    inv_std = lax.rsqrt(jnp.mean(centre * centre, axis=-1, keepdims=True) + 1e-05)
    return (centre * inv_std, inv_std)


def norm_back(grad_normed, normed, inv_std):
    return inv_std * (
        grad_normed
        - jnp.mean(grad_normed, axis=-1, keepdims=True)
        - normed * jnp.mean(grad_normed * normed, axis=-1, keepdims=True)
    )


def gelu_value(pre_gelu):
    return 0.5 * pre_gelu * (1.0 + jnp.tanh(gelu_coef * (pre_gelu + 0.044715 * pre_gelu**3)))


def gelu_slope(pre_gelu):
    tanh_part = jnp.tanh(gelu_coef * (pre_gelu + 0.044715 * pre_gelu**3))
    return 0.5 * (1.0 + tanh_part) + 0.5 * pre_gelu * (1.0 - tanh_part * tanh_part) * gelu_coef * (
        1.0 + 3.0 * 0.044715 * pre_gelu * pre_gelu
    )


def split_heads(matrix, head_count):
    return matrix.reshape(matrix.shape[0], head_count, matrix.shape[1] // head_count)


def masked_scores(query_heads, key_heads, slopes):
    block_rows = query_heads.shape[0]
    key_count = key_heads.shape[0]
    scale_factor = query_heads.shape[2] ** (-0.5)
    raw_scores = jnp.einsum(
        "qhd,khd->hqk", query_heads, key_heads, preferred_element_type=jnp.float32
    )
    query_pos = jnp.arange(block_rows)
    key_pos = jnp.arange(key_count)
    distance = (key_pos[None, :] - query_pos[:, None]).astype(jnp.float32)
    scores = raw_scores * scale_factor + slopes[:, None, None] * distance[None, :, :]
    return jnp.where((key_pos[None, :] <= query_pos[:, None])[None, :, :], scores, -1e30)


def attend(queries, key_rows, value_rows, slopes):
    head_count = slopes.shape[0]
    query_heads = split_heads(queries, head_count)
    key_heads = split_heads(key_rows, head_count)
    value_heads = split_heads(value_rows, head_count)
    length = queries.shape[0]
    block_rows = min(length, 512)
    scores = masked_scores(query_heads, key_heads, slopes)
    maximum = jnp.max(scores, axis=-1, keepdims=True)
    log_total = maximum + jnp.log(jnp.sum(jnp.exp(scores - maximum), axis=-1, keepdims=True))
    attn_probs = jnp.exp(scores - log_total).astype(jnp.bfloat16)
    context = jnp.einsum(
        "hqk,khd->qhd", attn_probs, value_heads, preferred_element_type=jnp.float32
    )
    contexts = context.reshape(block_rows, -1).astype(jnp.bfloat16)
    return (contexts, log_total)


def attend_back(queries, key_rows, value_rows, log_totals, grad_context, slopes):
    head_count = slopes.shape[0]
    query_heads = split_heads(queries, head_count)
    key_heads = split_heads(key_rows, head_count)
    value_heads = split_heads(value_rows, head_count)
    length = queries.shape[0]
    block_rows = min(length, 512)
    scale_factor = query_heads.shape[2] ** (-0.5)
    scores = masked_scores(query_heads, key_heads, slopes)
    probs_again = jnp.exp(scores - log_totals)
    grad_block = grad_context.reshape(block_rows, head_count, -1)
    grad_probs = jnp.einsum(
        "qhd,khd->hqk", grad_block, value_heads, preferred_element_type=jnp.float32
    )
    grad_scores = (
        probs_again
        * (grad_probs - jnp.sum(probs_again * grad_probs, axis=-1, keepdims=True))
        * scale_factor
    ).astype(jnp.bfloat16)
    query_parts = jnp.einsum(
        "hqk,khd->qhd", grad_scores, key_heads, preferred_element_type=jnp.float32
    ).reshape(block_rows, -1)
    grad_keys = jnp.einsum(
        "hqk,qhd->khd", grad_scores, query_heads, preferred_element_type=jnp.float32
    )
    grad_values = jnp.einsum(
        "hqk,qhd->khd",
        probs_again.astype(jnp.bfloat16),
        grad_block,
        preferred_element_type=jnp.float32,
    )
    return (query_parts, grad_keys.reshape(length, -1), grad_values.reshape(length, -1))


def forward_pass(hidden_rows, whole, slopes):
    (
        ln1_gain,
        ln1_bias,
        w_qkv,
        qv_bias,
        w_dense,
        dense_bias,
        ln2_gain,
        ln2_bias,
        w_up,
        up_bias,
        w_down,
        down_bias,
    ) = whole
    width = hidden_rows.shape[1]
    input_rows = hidden_rows.astype(jnp.float32)
    normed_one, inv_one = layer_norm(input_rows)
    normed_in = (normed_one * ln1_gain.astype(jnp.float32) + ln1_bias.astype(jnp.float32)).astype(
        jnp.bfloat16
    )
    projected = jnp.dot(normed_in, w_qkv, preferred_element_type=jnp.float32)
    queries = (projected[:, :width] + qv_bias[:width].astype(jnp.float32)).astype(jnp.bfloat16)
    key_rows = projected[:, width : 2 * width].astype(jnp.bfloat16)
    value_rows = (projected[:, 2 * width :] + qv_bias[width:].astype(jnp.float32)).astype(
        jnp.bfloat16
    )
    context, log_totals = attend(queries, key_rows, value_rows, slopes)
    residual = (
        input_rows
        + jnp.dot(context, w_dense, preferred_element_type=jnp.float32)
        + dense_bias.astype(jnp.float32)
    )
    normed_two, inv_two = layer_norm(residual)
    normed_mid = (normed_two * ln2_gain.astype(jnp.float32) + ln2_bias.astype(jnp.float32)).astype(
        jnp.bfloat16
    )
    pre_gelu = jnp.dot(normed_mid, w_up, preferred_element_type=jnp.float32) + up_bias.astype(
        jnp.float32
    )
    activated = gelu_value(pre_gelu).astype(jnp.bfloat16)
    output = (
        residual
        + jnp.dot(activated, w_down, preferred_element_type=jnp.float32)
        + down_bias.astype(jnp.float32)
    ).astype(jnp.bfloat16)
    saved = (
        normed_one,
        inv_one,
        normed_in,
        queries,
        key_rows,
        value_rows,
        context,
        log_totals,
        normed_two,
        inv_two,
        normed_mid,
        pre_gelu,
        activated,
    )
    return (output, saved)


def feedforward_back(cotangent, saved, again):
    (
        normed_one,
        inv_one,
        normed_in,
        queries,
        key_rows,
        value_rows,
        context,
        log_totals,
        normed_two,
        inv_two,
        normed_mid,
        pre_gelu,
        activated,
    ) = saved
    ln1_gain, w_qkv, w_dense, ln2_gain, w_up, w_down = again
    grad_out = cotangent.astype(jnp.float32)
    grad_down = jnp.dot(activated.T, cotangent, preferred_element_type=jnp.float32)
    grad_down_bias = jnp.sum(grad_out, axis=0)
    grad_pre = jnp.dot(cotangent, w_down.T, preferred_element_type=jnp.float32) * gelu_slope(
        pre_gelu
    )
    grad_pre_b = grad_pre.astype(jnp.bfloat16)
    grad_up = jnp.dot(normed_mid.T, grad_pre_b, preferred_element_type=jnp.float32)
    grad_up_bias = jnp.sum(grad_pre, axis=0)
    grad_mid = jnp.dot(grad_pre_b, w_up.T, preferred_element_type=jnp.float32)
    grad_ln2_gain = jnp.sum(grad_mid * normed_two, axis=0)
    grad_ln2_bias = jnp.sum(grad_mid, axis=0)
    grad_residual = grad_out + norm_back(
        grad_mid * ln2_gain.astype(jnp.float32), normed_two, inv_two
    )
    feed_grads = (grad_ln2_gain, grad_ln2_bias, grad_up, grad_up_bias, grad_down, grad_down_bias)
    return (feed_grads, grad_residual)


def attention_back(grad_residual, saved, again, slopes):
    (
        normed_one,
        inv_one,
        normed_in,
        queries,
        key_rows,
        value_rows,
        context,
        log_totals,
        normed_two,
        inv_two,
        normed_mid,
        pre_gelu,
        activated,
    ) = saved
    ln1_gain, w_qkv, w_dense, ln2_gain, w_up, w_down = again
    grad_res_b = grad_residual.astype(jnp.bfloat16)
    grad_dense = jnp.dot(context.T, grad_res_b, preferred_element_type=jnp.float32)
    grad_dense_bias = jnp.sum(grad_residual, axis=0)
    grad_context = jnp.dot(grad_res_b, w_dense.T, preferred_element_type=jnp.float32).astype(
        jnp.bfloat16
    )
    grad_queries, grad_keys, grad_values = attend_back(
        queries, key_rows, value_rows, log_totals, grad_context, slopes
    )
    grad_qv_bias = jnp.concatenate([jnp.sum(grad_queries, axis=0), jnp.sum(grad_values, axis=0)])
    grad_qkv_b = jnp.concatenate([grad_queries, grad_keys, grad_values], axis=1).astype(
        jnp.bfloat16
    )
    grad_qkv = jnp.dot(normed_in.T, grad_qkv_b, preferred_element_type=jnp.float32)
    grad_normed = jnp.dot(grad_qkv_b, w_qkv.T, preferred_element_type=jnp.float32)
    grad_ln1_gain = jnp.sum(grad_normed * normed_one, axis=0)
    grad_ln1_bias = jnp.sum(grad_normed, axis=0)
    input_grad = grad_residual + norm_back(
        grad_normed * ln1_gain.astype(jnp.float32), normed_one, inv_one
    )
    attn_grads = (grad_ln1_gain, grad_ln1_bias, grad_qkv, grad_qv_bias, grad_dense, grad_dense_bias)
    return (attn_grads, input_grad)


def on_device(
    hidden_in,
    cotangent,
    ln1_gain,
    ln1_bias,
    w_qkv,
    qv_bias,
    w_dense,
    dense_bias,
    ln2_gain,
    ln2_bias,
    w_up,
    up_bias,
    w_down,
    down_bias,
):
    slopes = head_slopes(H)
    whole = (
        lax.all_gather(ln1_gain, "shard", axis=0, tiled=True),
        lax.all_gather(ln1_bias, "shard", axis=0, tiled=True),
        lax.all_gather(w_qkv, "shard", axis=0, tiled=True),
        lax.all_gather(qv_bias, "shard", axis=0, tiled=True),
        lax.all_gather(w_dense, "shard", axis=0, tiled=True),
        lax.all_gather(dense_bias, "shard", axis=0, tiled=True),
        lax.all_gather(ln2_gain, "shard", axis=0, tiled=True),
        lax.all_gather(ln2_bias, "shard", axis=0, tiled=True),
        lax.all_gather(w_up, "shard", axis=0, tiled=True),
        lax.all_gather(up_bias, "shard", axis=0, tiled=True),
        lax.all_gather(w_down, "shard", axis=0, tiled=True),
        lax.all_gather(down_bias, "shard", axis=0, tiled=True),
    )
    output, saved = forward_pass(hidden_in, whole, slopes)
    again = (
        lax.all_gather(ln1_gain, "shard", axis=0, tiled=True),
        lax.all_gather(w_qkv, "shard", axis=0, tiled=True),
        lax.all_gather(w_dense, "shard", axis=0, tiled=True),
        lax.all_gather(ln2_gain, "shard", axis=0, tiled=True),
        lax.all_gather(w_up, "shard", axis=0, tiled=True),
        lax.all_gather(w_down, "shard", axis=0, tiled=True),
    )
    feed_grads, grad_residual = feedforward_back(cotangent, saved, again)
    attn_grads, input_grad = attention_back(grad_residual, saved, again, slopes)
    shares = (
        lax.psum_scatter(attn_grads[0], "shard", scatter_dimension=0, tiled=True),
        lax.psum_scatter(attn_grads[1], "shard", scatter_dimension=0, tiled=True),
        lax.psum_scatter(attn_grads[2], "shard", scatter_dimension=0, tiled=True),
        lax.psum_scatter(attn_grads[3], "shard", scatter_dimension=0, tiled=True),
        lax.psum_scatter(attn_grads[4], "shard", scatter_dimension=0, tiled=True),
        lax.psum_scatter(attn_grads[5], "shard", scatter_dimension=0, tiled=True),
        lax.psum_scatter(feed_grads[0], "shard", scatter_dimension=0, tiled=True),
        lax.psum_scatter(feed_grads[1], "shard", scatter_dimension=0, tiled=True),
        lax.psum_scatter(feed_grads[2], "shard", scatter_dimension=0, tiled=True),
        lax.psum_scatter(feed_grads[3], "shard", scatter_dimension=0, tiled=True),
        lax.psum_scatter(feed_grads[4], "shard", scatter_dimension=0, tiled=True),
        lax.psum_scatter(feed_grads[5], "shard", scatter_dimension=0, tiled=True),
    )
    totals = lax.psum(
        (
            shares[0],
            shares[1],
            shares[2],
            shares[3],
            shares[4],
            shares[5],
            shares[6],
            shares[7],
            shares[8],
            shares[9],
            shares[10],
            shares[11],
        ),
        "rep",
    )
    return (
        output,
        input_grad,
        totals[0],
        totals[1],
        totals[2],
        totals[3],
        totals[4],
        totals[5],
        totals[6],
        totals[7],
        totals[8],
        totals[9],
        totals[10],
        totals[11],
    )


def solution(mesh):
    placed = (
        P(("rep", "shard"), None),
        P(("rep", "shard"), None),
        P("shard"),
        P("shard"),
        P("shard", None),
        P("shard"),
        P("shard", None),
        P("shard"),
        P("shard"),
        P("shard"),
        P("shard", None),
        P("shard"),
        P("shard", None),
        P("shard"),
    )
    return jax.shard_map(
        on_device,
        mesh=mesh,
        in_specs=placed,
        out_specs=(
            P(("rep", "shard"), None),
            P(("rep", "shard"), None),
            P("shard"),
            P("shard"),
            P("shard", None),
            P("shard"),
            P("shard", None),
            P("shard"),
            P("shard"),
            P("shard"),
            P("shard", None),
            P("shard"),
            P("shard", None),
            P("shard"),
        ),
        check_vma=False,
    )
```

profile of v0, /device:TPU:1, one launch (start us, length us, event | category | flops | bytes accessed | tf_op | source)
XLA Modules:
  0.0 1433.2 jit_solution(2286575044985310103)
XLA Ops:
  8.0 0.7 all-gather.15.cloned.1.call-update
  10.0 18.1 %all-gather.3 = bf16[8,1,128]{2,1,0:T(2,128)(2,1)S(1)} all-gather(bf16[1,1,128]{2,1,0:T(2,128)(2,1)} %bitcast.87), channel_id=1, replica_groups=mesh['rep'=4,'shard'=8] {'shard'}, dimensions={0}, use_global_device_ids=true | all-gather | bytes 2304 | tf_op jit(solution)/shard_map/all_gather | solution.py:277
  28.1 13.2 all-gather.1
  41.3 14.9 %all-gather = bf16[8,1,128]{2,1,0:T(2,128)(2,1)S(1)} all-gather(bf16[1,1,128]{2,1,0:T(2,128)(2,1)} %bitcast.89), channel_id=1, replica_groups=mesh['rep'=4,'shard'=8] {'shard'}, dimensions={0}, use_global_device_ids=true | all-gather | bytes 2304 | tf_op jit(solution)/shard_map/all_gather | solution.py:272
  56.9 0.7 reshape.168
  57.6 22.9 %all-gather.6 = bf16[8,1,512]{2,1,0:T(2,128)(2,1)S(1)} all-gather(bf16[1,1,512]{2,1,0:T(2,128)(2,1)S(1)} %reshape.168), channel_id=1, replica_groups=mesh['rep'=4,'shard'=8] {'shard'}, dimensions={0}, use_global_device_ids=true | all-gather | bytes 9216 | tf_op jit(solution)/shard_map/all_gather | solution.py:281
  80.6 13.0 all-gather.5
  93.6 14.7 %all-gather.4 = bf16[8,1,128]{2,1,0:T(2,128)(2,1)S(1)} all-gather(bf16[1,1,128]{2,1,0:T(2,128)(2,1)} %bitcast.91), channel_id=1, replica_groups=mesh['rep'=4,'shard'=8] {'shard'}, dimensions={0}, use_global_device_ids=true | all-gather | bytes 2304 | tf_op jit(solution)/shard_map/all_gather | solution.py:278
  108.3 13.1 all-gather.2
  121.5 1.2 convert_reduce_fusion
  123.0 4.7 fusion.67
  128.8 1.3 fusion.73
  130.7 1.3 copy-done
  132.0 0.8 convolution_convert_fusion.1
  132.8 27.5 %all-gather.15.cloned.1.call-done = bf16[1024,1024]{1,0:T(8,128)(2,1)} async-done(((bf16[128,1024]{1,0:T(8,128)(2,1)}), bf16[1024,1024]{1,0:T(8,128)(2,1)}) %all-gather.15.cloned.1.call-update) | async-done | bytes 2097168 | tf_op jit(solution)/shard_map/all_gather | solution.py:276
  160.3 2.4 fusion.74
  163.0 123.6 %all-gather.17.cloned.1.call-done = bf16[1024,4096]{1,0:T(8,128)(2,1)} async-done(((bf16[128,4096]{1,0:T(8,128)(2,1)}), bf16[1024,4096]{1,0:T(8,128)(2,1)}) %all-gather.17.cloned.1.call-update) | async-done | bytes 8388624 | tf_op jit(solution)/shard_map/all_gather | solution.py:280
  286.7 8.0 convolution_add_fusion
  294.6 117.1 %all-gather.19.cloned.1.call-done = bf16[4096,1024]{1,0:T(8,128)(2,1)} async-done(((bf16[512,1024]{1,0:T(8,128)(2,1)}), bf16[4096,1024]{1,0:T(8,128)(2,1)}) %all-gather.19.cloned.1.call-update) | async-done | bytes 8388624 | tf_op jit(solution)/shard_map/all_gather | solution.py:282
  411.8 11.2 fusion.77
  423.1 2.7 multiply_reduce_fusion.1
  426.3 2.7 fusion.57
  429.3 3.1 convolution_convert_fusion
  432.4 2.0 copy.52
  434.4 3.8 fusion.78
  438.2 8.7 fusion.30
  446.9 9.0 fusion.71
  455.9 3.2 fusion.72
  459.1 0.8 copy-done.8
  459.9 6.6 fusion.53
  466.5 9.8 fusion.49
  476.6 0.7 copy-done.7
  477.4 10.8 fusion.69
  488.3 27.4 %reduce-scatter.7.cloned.1.call-done = f32[128,1024]{1,0:T(8,128)} async-done(((f32[1024,1024]{1,0:T(8,128)}), f32[128,1024]{1,0:T(8,128)}) %reduce-scatter.7.cloned.1.call-update) | async-done | bytes 524304 | tf_op jit(solution)/shard_map/reduce_scatter | solution.py:301
  515.7 211.1 %reduce-scatter.5.cloned.1.call-done = f32[128,3072]{1,0:T(8,128)} async-done(((f32[1024,3072]{1,0:T(8,128)}), f32[128,3072]{1,0:T(8,128)}) %reduce-scatter.5.cloned.1.call-update) | async-done | bytes 1572880 | tf_op jit(solution)/shard_map/reduce_scatter | solution.py:299
  726.8 285.3 %reduce-scatter.9.cloned.1.call-done = f32[128,4096]{1,0:T(8,128)} async-done(((f32[1024,4096]{1,0:T(8,128)}), f32[128,4096]{1,0:T(8,128)}) %reduce-scatter.9.cloned.1.call-update) | async-done | bytes 2097168 | tf_op jit(solution)/shard_map/reduce_scatter | solution.py:305
  1012.1 285.5 %reduce-scatter.11.cloned.1.call-done = f32[512,1024]{1,0:T(8,128)} async-done(((f32[4096,1024]{1,0:T(8,128)}), f32[512,1024]{1,0:T(8,128)}) %reduce-scatter.11.cloned.1.call-update) | async-done | bytes 2097168 | tf_op jit(solution)/shard_map/reduce_scatter | solution.py:307
  1297.6 14.9 %all-gather.7 = bf16[8,1,128]{2,1,0:T(2,128)(2,1)S(1)} all-gather(bf16[1,1,128]{2,1,0:T(2,128)(2,1)S(1)} %bitcast.92), channel_id=1, replica_groups=mesh['rep'=4,'shard'=8] {'shard'}, dimensions={0}, use_global_device_ids=true | all-gather | bytes 2304 | tf_op jit(solution)/shard_map/all_gather | solution.py:283
  1315.3 6.3 fusion.45
  1321.5 26.6 %all-reduce.8 = (f32[1024]{0:T(1024)S(1)}, f32[1024]{0:T(1024)S(1)}, f32[2048]{0:T(1024)S(1)}, f32[1024]{0:T(1024)S(1)}, f32[1024]{0:T(1024)S(1)}, /*index=5*/f3...) all-reduce(f32[1024]{0:T(1024)S(1)} %get-tuple-element.16, ...), channel_id=2, replica_groups=mesh['rep'=4,'shard'=8] {'shard'}, use_global_device_ids=true, to_apply=%region_12.13.clone | all-reduce | flops 12288 | bytes 98304
  1348.7 16.7 %all-reduce.9 = (f32[128]{0:T(128)}, f32[128]{0:T(128)}, f32[256]{0:T(256)}, f32[128]{0:T(128)}, f32[128]{0:T(128)}, /*index=5*/f32[128]{0:T(128)}, f32[512]{0:T(512)}, f32[128]{0:T(128)}) all-reduce(f32[128]{0:T(128)S(1)} %dynamic-slice.1, f32[128]{0:T(128)S(1)} %dynamic-slice.3, ...), channel_id=1, replica_groups=mesh['rep'=4,'shard'=8] {'rep'}, use_global_device_ids=true, to_apply=%region_13.14 | all-reduce | flops 1536 | bytes 12288 | tf_op jit(solution)/shard_map/psum | solution.py:310
  1365.4 2.7 fusion.44
  1368.1 8.6 fusion.29
  1376.7 42.6 %all-reduce.13.cloned.1.call-done = (f32[128,3072]{1,0:T(8,128)}, f32[128,1024]{1,0:T(8,128)}, f32[128,4096]{1,0:T(8,128)}, f32[512,1024]{1,0:T(8,128)}) async-done(((f32[128,3072]{1,0:T(8,128)}, f32[128,1024]{1,0:T(8,128)}, f32[128,4096]{1,0:T(8,128)}, f32[512,1024]{1,0:T(8,128)}), (f32[128,3072]{1,0:T(8,128)}, f32[128,1024]{1,0:T(8,128)}, f32[128,4096]{1,0:T(8,128)}, ...) | async-done | bytes 6291472 | tf_op jit(solution)/shard_map/psum | solution.py:310
  1419.3 2.9 copy.64
  1422.1 1.9 copy.65
  1424.0 1.3 copy.66
  1425.4 1.3 copy.67
  (96 shorter events, 7.6 us)
Async XLA Ops:
  7.2 115.5 %copy-start.1 = (bf16[256,1024]{1,0:T(8,128)(2,1)S(1)}, bf16[256,1024]{1,0:T(8,128)(2,1)}, u32[]{:S(2)}) copy-start(bf16[256,1024]{1,0:T(8,128)(2,1)} %param.14) | copy-start | bytes 1572868
  7.2 115.8 %all-gather.13.cloned.1.call-start = ((), (), s32[]{:S(2)}) async-start(), calls=%async_computation.4 | async-start | bytes 7077888 | tf_op jit(solution)/shard_map/all_gather | solution.py:274
  7.9 152.4 %all-gather.15.cloned.1.call-start = ((), (), s32[]{:S(2)}) async-start(), calls=%async_computation.5 | async-start | bytes 2359296 | tf_op jit(solution)/shard_map/all_gather | solution.py:276
  8.7 278.0 %all-gather.17.cloned.1.call-start = ((), (), s32[]{:S(2)}) async-start(), calls=%async_computation.6 | async-start | bytes 9437184 | tf_op jit(solution)/shard_map/all_gather | solution.py:280
  9.4 402.4 %all-gather.19.cloned.1.call-start = ((), (), s32[]{:S(2)}) async-start(), calls=%async_computation.7 | async-start | bytes 9437184 | tf_op jit(solution)/shard_map/all_gather | solution.py:282
  10.0 505.7 %reduce-scatter.7.cloned.1.call-start = ((), (), s32[]{:S(2)}) async-start(), calls=%async_computation.9 | async-start | bytes 4718592 | tf_op jit(solution)/shard_map/reduce_scatter | solution.py:301
  128.5 2.1 copy-start.16
  128.7 1.9 copy-start.15
  130.1 2.0 copy-start
  132.8 161.8 %copy-start.3 = (bf16[16,64,256]{2,1,0:T(8,128)(2,1)}, bf16[16,64,256]{2,1,0:T(8,128)(2,1)S(1)}, u32[]{:S(2)}) copy-start(bf16[16,64,256]{2,1,0:T(8,128)(2,1)S(1)} %convolution_convert_fusion.1) | copy-start | bytes 1572868
  286.7 125.1 %copy-start.5 = (bf16[256,1024]{1,0:T(8,128)(2,1)S(1)}, bf16[256,1024]{1,0:T(8,128)(2,1)}, u32[]{:S(2)}) copy-start(bf16[256,1024]{1,0:T(8,128)(2,1)} %param.15) | copy-start | bytes 1572868
  411.8 11.3 copy-start.18
  423.0 2.7 copy-start.12
  423.1 2.7 copy-start.6
  423.1 3.2 copy-start.4
  429.0 297.8 %reduce-scatter.5.cloned.1.call-start = ((), (), s32[]{:S(2)}) async-start(), calls=%async_computation.8 | async-start | bytes 14155776 | tf_op jit(solution)/shard_map/reduce_scatter | solution.py:299
  446.9 9.0 copy-start.2
  455.9 4.0 copy-start.13
  455.9 4.0 copy-start.14
  459.0 0.8 copy-start.8
  466.4 545.6 %reduce-scatter.9.cloned.1.call-start = ((), (), s32[]{:S(2)}) async-start(), calls=%async_computation.10 | async-start | bytes 18874368 | tf_op jit(solution)/shard_map/reduce_scatter | solution.py:305
  476.3 1.0 copy-start.7
  476.3 821.3 %reduce-scatter.11.cloned.1.call-start = ((), (), s32[]{:S(2)}) async-start(), calls=%async_computation.11 | async-start | bytes 18874368 | tf_op jit(solution)/shard_map/reduce_scatter | solution.py:307
  488.2 809.5 %copy-start.17 = (bf16[128]{0:T(256)(128)(2,1)S(1)}, bf16[128]{0:T(256)(128)(2,1)}, u32[]{:S(2)}) copy-start(bf16[128]{0:T(256)(128)(2,1)} %param.27) | copy-start | bytes 772
  488.2 824.4 %copy-start.19 = (u32[32]{0:T(128)S(1)}, u32[32]{0:T(128)}, u32[]{:S(2)}) copy-start(u32[32]{0:T(128)} %constant.40) | copy-start | bytes 388
  488.2 827.1 %copy-start.9 = (bf16[256,16,64]{0,2,1:T(8,128)(2,1)S(1)}, bf16[256,16,64]{0,2,1:T(8,128)(2,1)}, u32[]{:S(2)}) copy-start(bf16[256,16,64]{0,2,1:T(8,128)(2,1)} %copy-done.8) | copy-start | bytes 1572868
  488.2 931.1 %all-reduce.13.cloned.1.call-start = ((), (), s32[]{:S(2)}) async-start(), calls=%async_computation.12 | async-start | bytes 12582912 | tf_op jit(solution)/shard_map/psum | solution.py:310
  1419.3 4.7 copy-start.11
  1419.3 6.1 copy-start.10
Sparse Core Ops, SparseCore 0:
  10.2 101.0 all-gather.12
  113.4 46.9 all-gather.14
  162.5 124.1 all-gather.16
  288.6 123.0 all-gather.18
  429.1 86.5 reduce-scatter.6
  519.6 207.1 reduce-scatter.4
  731.0 280.9 reduce-scatter.8
  1015.8 281.7 reduce-scatter.10
  1300.4 118.8 all-reduce.12
where the time goes:
time: 1430 us
  waiting for transfers between devices  1120 us (78%)
  blocking collectives  168 us (12%)
  matrix products  104 us (7%)
  between operations  16.1 us (1%)
  local copies, waits for them, and re-layouts  15.7 us (1%)
    reduce_scatter x1, waiting for transfers between devices, on_device(): lax.psum_scatter(feed_grads[4], 'shard', scatter_dimension=0, tiled=True)  286 us
    reduce_scatter x1, waiting for transfers between devices, on_device(): lax.psum_scatter(feed_grads[2], 'shard', scatter_dimension=0, tiled=True)  285 us
    reduce_scatter x1, waiting for transfers between devices, on_device(): lax.psum_scatter(attn_grads[2], 'shard', scatter_dimension=0, tiled=True)  211 us
    all_gather x1, waiting for transfers between devices, on_device(): lax.all_gather(w_up, 'shard', axis=0, tiled=True)  124 us
    all_gather x1, waiting for transfers between devices, on_device(): lax.all_gather(w_down, 'shard', axis=0, tiled=True)  117 us
    psum x1, waiting for transfers between devices, on_device(): lax.psum((shares[0], shares[1], shares[2], shares[3], shares[4], shares[5...  42.6 us
  transfers between devices with their start and end apart: 9, of which 8 were waited for; matrix products, arithmetic and copies ran while one was open for 7% of the time, Pallas kernels for 0%

commit v1 on v0

v1 whole, which is shorter than its diff:
```python
import functools
import math

import jax
import jax.numpy as jnp
from jax import lax
from jax.sharding import PartitionSpec as P

H = 16
BF = jnp.bfloat16
F32 = jnp.float32
AXES = ("rep", "shard")
gelu_coef = math.sqrt(2.0 / math.pi)


class Place:
    def __init__(self, reps, shards):
        self.reps, self.shards = reps, shards
        self.nx = max(n for n in (1, 2, 4, 8) if shards % n == 0 and n * n <= shards)
        self.nz = shards // self.nx
        rep, shard = lax.axis_index("rep"), lax.axis_index("shard")
        self.y, self.core = rep // 2, rep % 2
        self.z, self.x = shard // self.nx, shard % self.nx
        self.shard = shard

    def _send(self, value, move):
        pairs = []
        for rep in range(self.reps):
            for shard in range(self.shards):
                y, core, z, x = move(rep // 2, rep % 2, shard // self.nx, shard % self.nx)
                pairs.append((rep * self.shards + shard, (y * 2 + core) * self.shards + z * self.nx + x))
        return lax.ppermute(value, AXES, pairs)

    def to_core(self, value):
        return self._send(value, lambda y, core, z, x: (y, 1 - core, z, x))

    def to_y(self, value):
        return self._send(value, lambda y, core, z, x: (1 - y, core, z, x))

    def to_z(self, value, k):
        return self._send(value, lambda y, core, z, x: (y, core, (z + k) % self.nz, x))

    def to_x(self, value, k):
        return self._send(value, lambda y, core, z, x: (y, core, z, (x + k) % self.nx))

    def from_shard(self, kz, kx):
        z, x = lax.rem(self.z - kz + self.nz, self.nz), lax.rem(self.x - kx + self.nx, self.nx)
        return z * self.nx + x

    def gather_slots(self, block):
        slots = {}
        for kz in range(self.nz):
            held = block if kz == 0 else self.to_z(block, kz)
            for kx in range(self.nx):
                slots[kz, kx] = held if kx == 0 else self.to_x(held, kx)
        return slots

    def assemble(self, slots):
        first = slots[0, 0]
        whole = jnp.zeros((self.shards * first.shape[0],) + first.shape[1:], first.dtype)
        for (kz, kx), block in slots.items():
            start = self.from_shard(kz, kx) * first.shape[0]
            whole = lax.dynamic_update_slice(whole, block, (start,) + (0,) * (first.ndim - 1))
        return whole

    def sum_all(self, value):
        value = value + self.to_core(value)
        value = value + self.to_y(value)
        value = sum([self.to_x(value, k) for k in range(1, self.nx)], value)
        return sum([self.to_z(value, k) for k in range(1, self.nz)], value)

    def near_first(self):
        return sorted(range(self.nz), key=lambda k: -min(k, self.nz - k))

    def _owner_sum(self, chunk_of):
        terms = []
        for k in self.near_first():
            chunk = chunk_of(k)
            mine = lax.dynamic_index_in_dim(chunk, self.x, 0, keepdims=False)
            for kx in range(1, self.nx):
                other = lax.rem(self.x + kx, self.nx)
                away = lax.dynamic_index_in_dim(chunk, other, 0, keepdims=False).astype(BF)
                mine = mine + self.to_x(away, kx).astype(F32)
            terms.append(mine if k == 0 else self.to_z(mine.astype(BF), k).astype(F32))
        return functools.reduce(lambda a, b: a + b, terms)

    def scatter_xz(self, chunk_of):
        part = lax.optimization_barrier(self._owner_sum(chunk_of).astype(BF))
        return part.astype(F32) + self.to_y(part).astype(F32)

    def scatter_yxz(self, away_of, mine_of):
        def chunk_of(k):
            return mine_of(k) + self.to_y(away_of(k).astype(BF)).astype(F32)

        part = lax.optimization_barrier(self._owner_sum(chunk_of).astype(BF))
        return part, self.to_y(part)


def head_slopes(head_count):
    return 2.0 ** (-8.0 * (jnp.arange(head_count, dtype=F32) + 1.0) / head_count)


def layer_norm(values_in):
    centre = values_in - jnp.mean(values_in, axis=-1, keepdims=True)
    inv_std = lax.rsqrt(jnp.mean(centre * centre, axis=-1, keepdims=True) + 1e-05)
    return (centre * inv_std, inv_std)


def norm_back(grad_normed, normed, inv_std):
    return inv_std * (
        grad_normed
        - jnp.mean(grad_normed, axis=-1, keepdims=True)
        - normed * jnp.mean(grad_normed * normed, axis=-1, keepdims=True)
    )


def gelu_both(u):
    t = jnp.tanh(gelu_coef * (u + 0.044715 * u * u * u))
    value = 0.5 * u * (1.0 + t)
    slope = 0.5 * (1.0 + t) + 0.5 * u * (1.0 - t * t) * gelu_coef * (1.0 + 3.0 * 0.044715 * u * u)
    return value, slope


def dot(a, b):
    return jnp.dot(a, b, preferred_element_type=F32)


def dot_tn(a, b):
    return lax.dot_general(a, b, (((0,), (0,)), ((), ())), preferred_element_type=F32)


def dot_nt(a, b):
    return lax.dot_general(a, b, (((1,), (1,)), ((), ())), preferred_element_type=F32)


def pick(pair_first, pair_second, index):
    flip = index == 1
    return jnp.where(flip, pair_second, pair_first), jnp.where(flip, pair_first, pair_second)


def on_device(
    reps,
    shards,
    hidden_in,
    cotangent,
    ln1_gain,
    ln1_bias,
    w_qkv,
    qv_bias,
    w_dense,
    dense_bias,
    ln2_gain,
    ln2_bias,
    w_up,
    up_bias,
    w_down,
    down_bias,
):
    at = Place(reps, shards)
    core, y = at.core, at.y
    rows, width = hidden_in.shape
    rd = w_qkv.shape[0]
    ff = w_up.shape[1]
    quarter = ff // shards // 4
    half = width // 2
    heads = H // 2
    hd = width // H
    slopes = lax.dynamic_slice_in_dim(head_slopes(H), core * heads, heads)

    vectors = (ln1_gain, ln1_bias, qv_bias, dense_bias, ln2_gain, ln2_bias, up_bias, down_bias)
    packed = jnp.concatenate(vectors)[None, :]
    packed = at.assemble(at.gather_slots(packed))
    whole, start = [], 0
    for v in vectors:
        whole.append(packed[:, start : start + v.shape[0]].reshape(-1).astype(F32))
        start += v.shape[0]
    gain1, bias1, qv_b, dense_b, gain2, bias2, up_b, down_b = whole

    qkv_half = lax.dynamic_index_in_dim(w_qkv.reshape(rd, 3, 2, half), core, 2, keepdims=False)
    qkv_half = qkv_half.reshape(rd, 3 * half)
    dense_half = lax.dynamic_slice_in_dim(w_dense, core * half, half, 1)
    up_quarter = w_up.reshape(rd, shards, 2, 2, quarter)
    up_quarter = lax.dynamic_index_in_dim(up_quarter, core, 2, keepdims=False)
    up_quarter = lax.dynamic_index_in_dim(up_quarter, y, 2, keepdims=False).reshape(rd, shards * quarter)
    down_quarter = lax.dynamic_slice_in_dim(w_down, (core * 2 + y) * quarter, quarter, 0)

    input_rows = hidden_in.astype(F32)
    normed_one, inv_one = layer_norm(input_rows)
    normed_in = (normed_one * gain1 + bias1).astype(BF)
    normed_in = jnp.concatenate([normed_in, at.to_core(normed_in)])
    cot = jnp.concatenate([cotangent, at.to_core(cotangent)])

    wq = at.assemble(at.gather_slots(qkv_half))
    wd = at.assemble(at.gather_slots(dense_half))
    wd_other = at.to_core(wd)
    up_slots = at.gather_slots(up_quarter)
    wu = (at.assemble(up_slots), at.assemble({k: at.to_y(v) for k, v in up_slots.items()}))
    down_slots = at.gather_slots(down_quarter)
    wo = (at.assemble(down_slots), at.assemble({k: at.to_y(v) for k, v in down_slots.items()}))
    wd = jnp.concatenate(pick(wd, wd_other, core), axis=1)

    projected = dot(normed_in, wq)
    q_b = lax.dynamic_slice_in_dim(qv_b[:width], core * half, half)
    v_b = lax.dynamic_slice_in_dim(qv_b[width:], core * half, half)
    queries = (projected[:, :half] + q_b).astype(BF).reshape(2, rows, heads, hd)
    keys = projected[:, half : 2 * half].astype(BF).reshape(2, rows, heads, hd)
    values = (projected[:, 2 * half :] + v_b).astype(BF).reshape(2, rows, heads, hd)
    raw = jnp.einsum("bqhd,bkhd->bhqk", queries, keys, preferred_element_type=F32)
    pos = jnp.arange(rows)
    distance = (pos[None, :] - pos[:, None]).astype(F32)
    scores = raw * hd ** (-0.5) + slopes[None, :, None, None] * distance
    scores = jnp.where(pos[None, :] <= pos[:, None], scores, -1e30)
    maximum = jnp.max(scores, axis=-1, keepdims=True)
    log_total = maximum + jnp.log(jnp.sum(jnp.exp(scores - maximum), axis=-1, keepdims=True))
    probs = jnp.exp(scores - log_total)
    probs_b = probs.astype(BF)
    context = jnp.einsum("bhqk,bkhd->bqhd", probs_b, values, preferred_element_type=F32)
    context = context.astype(BF).reshape(2, rows, half)
    context = jnp.concatenate(pick(context[0], at.to_core(context[1]), core), axis=1)

    residual = input_rows + dot(context, wd) + dense_b
    normed_two, inv_two = layer_norm(residual)
    normed_mid = (normed_two * gain2 + bias2).astype(BF)
    normed_mid = jnp.concatenate([normed_mid, at.to_core(normed_mid)])

    up_b4 = lax.dynamic_index_in_dim(up_b.reshape(shards, 2, 2, quarter), core, 1, keepdims=False)
    up_bs = pick(up_b4[:, 0].reshape(-1), up_b4[:, 1].reshape(-1), y)
    acts, slope_of = [], []
    for w, b in zip(wu, up_bs):
        value, slope = gelu_both(dot(normed_mid, w) + b)
        acts.append(value.astype(BF))
        slope_of.append(slope)
    part = dot(acts[0], wo[0]) + dot(acts[1], wo[1])
    output = (residual + part[:rows] + at.to_core(part[rows:]) + down_b).astype(BF)

    nz, nx = at.nz, at.nx

    def owner_cols(matrix, k, per):
        z = lax.rem(at.z + k, nz)
        return lax.dynamic_slice_in_dim(matrix, z * nx * per, nx * per, 1)

    def down_terms(i):
        return lambda k: dot_tn(owner_cols(acts[i], k, quarter), cot).reshape(nx, quarter, width)

    down_own, down_other = at.scatter_yxz(down_terms(1), down_terms(0))
    grad_down_bias = jnp.sum(cotangent.astype(F32), axis=0)
    grad_pre = [dot_nt(cot, w) * s for w, s in zip(wo, slope_of)]
    grad_pre_b = [g.astype(BF) for g in grad_pre]
    grad_up_bias = [jnp.sum(g, axis=0) for g in grad_pre]
    both_pre = jnp.concatenate(grad_pre_b, axis=1)

    def up_terms(k):
        return dot_tn(owner_cols(normed_mid, k, rd), both_pre).reshape(nx, rd, 2 * shards * quarter)

    def up_terms_by_y(k):
        terms = up_terms(k).reshape(nx, rd, 2, shards * quarter)
        return jnp.concatenate(pick(terms[:, :, 0], terms[:, :, 1], y), axis=-1)

    up_total = at.scatter_xz(up_terms_by_y)
    gmid = dot_nt(grad_pre_b[0], wu[0]) + dot_nt(grad_pre_b[1], wu[1])
    grad_mid = gmid[:rows] + at.to_core(gmid[rows:])
    grad_ln2_gain = jnp.sum(grad_mid * normed_two, axis=0)
    grad_ln2_bias = jnp.sum(grad_mid, axis=0)
    grad_residual = cotangent.astype(F32) + norm_back(grad_mid * gain2, normed_two, inv_two)
    grad_res_b = grad_residual.astype(BF)
    grad_dense_bias = jnp.sum(grad_residual, axis=0)

    context_t = context
    res_halves = grad_res_b.reshape(rows, 2, half)
    res_keep = lax.dynamic_index_in_dim(res_halves, core, 1, keepdims=False)
    res_give = lax.dynamic_index_in_dim(res_halves, 1 - core, 1, keepdims=False)
    dense_sum = dot_tn(context_t, res_keep) + at.to_core(dot_tn(context_t, res_give).astype(BF)).astype(F32)

    def dense_terms(k):
        z = lax.rem(at.z + k, nz)
        return lax.dynamic_slice_in_dim(dense_sum, z * nx * rd, nx * rd, 0).reshape(nx, rd, half)

    dense_total = at.scatter_xz(dense_terms)

    grad_context = dot_nt(grad_res_b, wd).astype(BF).reshape(rows, 2, half)
    gc_keep = lax.dynamic_index_in_dim(grad_context, core, 1, keepdims=False)
    gc_give = lax.dynamic_index_in_dim(grad_context, 1 - core, 1, keepdims=False)
    grad_ctx = jnp.stack([gc_keep, at.to_core(gc_give)]).reshape(2, rows, heads, hd)
    grad_probs = jnp.einsum("bqhd,bkhd->bhqk", grad_ctx, values, preferred_element_type=F32)
    grad_scores = probs * (grad_probs - jnp.sum(probs * grad_probs, axis=-1, keepdims=True)) * hd ** (-0.5)
    grad_scores = grad_scores.astype(BF)
    grad_q = jnp.einsum("bhqk,bkhd->bqhd", grad_scores, keys, preferred_element_type=F32).reshape(2 * rows, half)
    grad_k = jnp.einsum("bhqk,bqhd->bkhd", grad_scores, queries, preferred_element_type=F32).reshape(2 * rows, half)
    grad_v = jnp.einsum("bhqk,bqhd->bkhd", probs_b, grad_ctx, preferred_element_type=F32).reshape(2 * rows, half)
    grad_q_bias, grad_v_bias = jnp.sum(grad_q, axis=0), jnp.sum(grad_v, axis=0)
    grad_qkv_b = jnp.concatenate([grad_q, grad_k, grad_v], axis=1).astype(BF)

    cols = 3 * half // 2
    pre_y = lax.dynamic_slice_in_dim(grad_qkv_b, y * cols, cols, 1)
    pre_n = lax.dynamic_slice_in_dim(grad_qkv_b, (1 - y) * cols, cols, 1)

    def qkv_terms(columns):
        return lambda k: dot_tn(owner_cols(normed_in, k, rd), columns).reshape(nx, rd, cols)

    qkv_own, qkv_other = at.scatter_yxz(qkv_terms(pre_n), qkv_terms(pre_y))
    gnorm = dot_nt(grad_qkv_b, wq)
    grad_normed = gnorm[:rows] + at.to_core(gnorm[rows:])
    grad_ln1_gain = jnp.sum(grad_normed * normed_one, axis=0)
    grad_ln1_bias = jnp.sum(grad_normed, axis=0)
    input_grad = grad_residual + norm_back(grad_normed * gain1, normed_one, inv_one)

    down_y = jnp.concatenate(pick(down_own, down_other, y), axis=0)
    grad_down = jnp.concatenate(pick(down_y, at.to_core(down_y), core), axis=0).astype(F32)
    up_c = up_total.reshape(rd, 2, shards, quarter).transpose(0, 2, 1, 3).reshape(rd, shards, 1, 2 * quarter)
    grad_up = jnp.concatenate(pick(up_c, at.to_core(up_c), core), axis=2).reshape(rd, ff)
    grad_dense = jnp.concatenate(pick(dense_total, at.to_core(dense_total), core), axis=1)
    qkv_c = jnp.concatenate(pick(qkv_own, qkv_other, y), axis=1).reshape(rd, 3, 1, half)
    grad_qkv = jnp.concatenate(pick(qkv_c, at.to_core(qkv_c), core), axis=2).reshape(rd, 3 * width).astype(F32)

    up_y = jnp.stack([g.reshape(shards, quarter) for g in pick(grad_up_bias[0], grad_up_bias[1], y)], axis=1)
    on_core = jnp.arange(2) == core
    up_bias_all = jnp.where(on_core[None, :, None, None], up_y[:, None], 0.0).reshape(-1)
    feed = jnp.concatenate([grad_ln2_gain, grad_ln2_bias, up_bias_all, grad_down_bias, grad_dense_bias])
    feed = at.sum_all(feed[None, :])[0]
    qv_all = jnp.stack([grad_q_bias, grad_v_bias])
    qv_all = jnp.where(on_core[None, :, None], qv_all[:, None], 0.0).reshape(-1)
    attn = jnp.concatenate([grad_ln1_gain, grad_ln1_bias, qv_all])
    attn = at.sum_all(attn[None, :])[0]

    def own(vector, start, size):
        per = size // shards
        return lax.dynamic_slice_in_dim(vector, start + at.shard * per, per)

    return (
        output,
        input_grad,
        own(attn, 0, width),
        own(attn, width, width),
        grad_qkv,
        own(attn, 2 * width, 2 * width),
        grad_dense,
        own(feed, 3 * width + ff, width),
        own(feed, 0, width),
        own(feed, width, width),
        grad_up,
        own(feed, 2 * width, ff),
        grad_down,
        own(feed, 2 * width + ff, width),
    )


def solution(mesh):
    both, rows, vector = P(("rep", "shard"), None), P("shard", None), P("shard")
    weights = (vector, vector, rows, vector, rows, vector, vector, vector, rows, vector, rows, vector)
    return jax.shard_map(
        functools.partial(on_device, mesh.shape["rep"], mesh.shape["shard"]),
        mesh=mesh,
        in_specs=(both, both) + weights,
        out_specs=(both, both) + weights,
        check_vma=False,
    )
```

time: 1430 us -> 644 us (0.45)
  waiting for transfers between devices: 1120 us -> 172 us
  blocking collectives: 168 us -> 0 us
  local copies, waits for them, and re-layouts: 15.7 us -> 171 us
  starting transfers between devices: 0.84 us -> 149 us
  other arithmetic: 5.88 us -> 47.6 us
    reduce_scatter x4 -> x0, waiting for transfers between devices: 809 us -> none  [the longest x1 286 us: on_device(): lax.psum_scatter(feed_grads[4], 'shard', scatter_dimension=0, tiled=True)]
    all_gather x4 -> x0, waiting for transfers between devices: 268 us -> none  [the longest x1 124 us: on_device(): lax.all_gather(w_up, 'shard', axis=0, tiled=True)]
    ppermute x0 -> x117, waiting for transfers between devices: none -> 172 us  [_send(): return lax.ppermute(value, AXES, pairs)]
    ppermute x0 -> x117, starting transfers between devices: none -> 149 us  [_send(): return lax.ppermute(value, AXES, pairs)]
    all_gather x8 -> x0, blocking collectives: 125 us -> none  [the longest x1 22.9 us: on_device(): lax.all_gather(up_bias, 'shard', axis=0, tiled=True)]
    dynamic_update_slice x0 -> x56, local copies, waits for them, and re-layouts: none -> 55.3 us  [assemble(): lax.dynamic_update_slice(whole, block, (start,) + (0,) * (first.ndim - 1))]
    psum x1 -> x0, waiting for transfers between devices: 42.6 us -> none  [on_device(): lax.psum((shares[0], shares[1], shares[2], shares[3], shares[4], shares[5...]
    unnamed x1 -> x0, blocking collectives: 26.6 us -> none
  transfers between devices with their start and end apart: 9 -> 117, of which waited for: 8 -> 31; matrix products, arithmetic and copies ran while one was open for 7% -> 44% of each run, Pallas kernels for 0% -> 0%
where the time goes in v1:
time: 644 us; the launch traced here: 637 us
  waiting for transfers between devices  172 us (27%)
  local copies, waits for them, and re-layouts  171 us (27%)
  starting transfers between devices  149 us (23%)
  matrix products  94.3 us (15%)
  other arithmetic  47.6 us (7%)
    ppermute x117, waiting for transfers between devices, _send(): return lax.ppermute(value, AXES, pairs)  172 us
    ppermute x117, starting transfers between devices, _send(): return lax.ppermute(value, AXES, pairs)  149 us
    dynamic_update_slice x56, local copies, waits for them, and re-layouts, assemble(): lax.dynamic_update_slice(whole, block, (start,) + (0,) * (first.ndim - 1))  55.3 us
    dot_general x22, matrix products, dot_tn(): lax.dot_general(a, b, (((0,), (0,)), ((), ())), preferred_element_type=F32)  29.4 us
    dot_general x6, matrix products, dot_nt(): lax.dot_general(a, b, (((1,), (1,)), ((), ())), preferred_element_type=F32)  20.3 us
    dot_general x6, matrix products, dot(): return jnp.dot(a, b, preferred_element_type=F32)  18.9 us
    ppermute x16, local copies, waits for them, and re-layouts, _send(): return lax.ppermute(value, AXES, pairs)  18.5 us
    unnamed x193, local copies, waits for them, and re-layouts  17.2 us
  transfers between devices with their start and end apart: 117, of which 31 were waited for; matrix products, arithmetic and copies ran while one was open for 44% of the time, Pallas kernels for 0%

profile of v1, /device:TPU:1, one launch (start us, length us, event | category | flops | bytes accessed | tf_op | source)
XLA Modules:
  0.0 637.1 jit_solution(404746651348438243)
XLA Ops:
  7.5 4.2 collective-permute-start.5
  65.2 7.2 %collective-permute-done.19 = bf16[128,512]{1,0:T(8,128)(2,1)} collective-permute-done((bf16[128,512]{1,0:T(8,128)(2,1)}, bf16[128,512]{1,0:T(8,128)(2,1)}, u32[]{:S(2)}, u32[]{:S(2)}) %collective-permute-start.19) | collective-permute-done | bytes 131104 | tf_op jit(solution)/shard_map/ppermute | solution.py:32
  79.9 8.6 %collective-permute-start.21 = (bf16[128,512]{1,0:T(8,128)(2,1)}, bf16[128,512]{1,0:T(8,128)(2,1)S(1)}, u32[]{:S(2)}, u32[]{:S(2)}) collective-permute-start(bf16[128,512]{1,0:T(8,128)(2,1)} %get-tuple-element.41), channel_id=1, source_target_pairs={{0,6},{1,7},{2,0},{3,1},{4,2},{5,3},{6,4},{7,5},{8,14},{9,15},{10,... | collective-permute-start | bytes 393224 | tf_op jit(solution)/shard_map/ppermute | solution.py:32
  94.5 6.6 %collective-permute-done.22 = bf16[128,512]{1,0:T(8,128)(2,1)S(1)} collective-permute-done((bf16[128,512]{1,0:T(8,128)(2,1)S(1)}, bf16[128,512]{1,0:T(8,128)(2,1)S(1)}, u32[]{:S(2)}, u32[]{:S(2)}) %collective-permute-start.22) | collective-permute-done | bytes 131104 | tf_op jit(solution)/shard_map/ppermute | solution.py:32
  114.7 6.0 collective-permute-done.34
  122.8 3.5 collective-permute-done.36
  132.6 3.3 collective-permute-start.30
  156.9 4.0 collective-permute-done.51
  166.1 13.9 %collective-permute-start.13 = (bf16[128,1536]{0,1:T(8,128)(2,1)S(1)}, bf16[128,1536]{0,1:T(8,128)(2,1)}, u32[]{:S(2)}, u32[]{:S(2)}) collective-permute-start(bf16[128,1536]{0,1:T(8,128)(2,1)S(1)} %bitcast.344), channel_id=1, source_target_pairs={{0,6},{1,7},{2,0},{3,1},{4,2},{5,3},{6,4},{7,5},{8,14},{9,15},{10,... | collective-permute-start | bytes 1179656 | tf_op jit(solution)/shard_map/ppermute | solution.py:32
  181.1 4.9 collective-permute-start.7
  196.5 5.5 collective-permute-done.12
  205.6 5.6 collective-permute-done.14
  212.2 3.7 fusion.55
  247.5 10.2 %collective-permute-done.42 = bf16[128,1024]{0,1:T(8,128)(2,1)S(1)} collective-permute-done((bf16[128,1024]{0,1:T(8,128)(2,1)}, bf16[128,1024]{0,1:T(8,128)(2,1)S(1)}, u32[]{:S(2)}, u32[]{:S(2)}) %collective-permute-start.42) | collective-permute-done | bytes 262176 | tf_op jit(solution)/shard_map/ppermute | solution.py:32
  265.1 3.5 multiply_convert_fusion.1
  271.2 3.4 multiply_convert_fusion.2
  287.5 4.3 fusion.225
  291.8 3.2 fusion.233
  295.1 3.9 fusion.224
  299.0 4.6 convolution_add_fusion.1
  312.1 4.1 reshape_reshape.13
  316.2 5.6 fusion.221
  323.9 4.1 reshape_reshape.14
  328.0 5.6 fusion.222
  335.7 4.0 reshape_reshape.12
  339.7 3.7 fusion.132
  343.4 4.0 reshape_reshape.15
  347.4 4.3 fusion.223
  366.9 6.9 %collective-permute-done.97 = bf16[128,2048]{1,0:T(8,128)(2,1)S(1)} collective-permute-done((bf16[128,2048]{1,0:T(8,128)(2,1)S(1)}, bf16[128,2048]{1,0:T(8,128)(2,1)S(1)}, u32[]{:S(2)}, u32[]{:S(2)}) %collective-permute-start.97) | collective-permute-done | bytes 524320 | tf_op jit(solution)/shard_map/ppermute | solution.py:32
  375.9 9.1 %collective-permute-done.99 = bf16[128,2048]{1,0:T(8,128)(2,1)S(1)} collective-permute-done((bf16[128,2048]{1,0:T(8,128)(2,1)S(1)}, bf16[128,2048]{1,0:T(8,128)(2,1)S(1)}, u32[]{:S(2)}, u32[]{:S(2)}) %collective-permute-start.99) | collective-permute-done | bytes 524320 | tf_op jit(solution)/shard_map/ppermute | solution.py:32
  388.7 18.8 %collective-permute-done.111 = bf16[128,1024]{1,0:T(8,128)(2,1)S(1)} collective-permute-done((bf16[128,1024]{1,0:T(8,128)(2,1)S(1)}, bf16[128,1024]{1,0:T(8,128)(2,1)S(1)}, u32[]{:S(2)}, u32[]{:S(2)}) %collective-permute-start.111) | collective-permute-done | bytes 262176 | tf_op jit(solution)/shard_map/ppermute | solution.py:32
  408.8 4.3 collective-permute-done.105
  414.8 4.0 collective-permute-done.108
  424.2 14.3 %collective-permute-done.106 = bf16[128,1024]{1,0:T(8,128)(2,1)S(1)} collective-permute-done((bf16[128,1024]{1,0:T(8,128)(2,1)S(1)}, bf16[128,1024]{1,0:T(8,128)(2,1)S(1)}, u32[]{:S(2)}, u32[]{:S(2)}) %collective-permute-start.106) | collective-permute-done | bytes 262176 | tf_op jit(solution)/shard_map/ppermute | solution.py:32
  438.5 3.3 collective-permute-start.100
  450.3 3.1 constant_dynamic-slice_fusion.10
  456.6 5.8 collective-permute-done.100
  462.4 24.2 %collective-permute-done.96 = bf16[128,2048]{1,0:T(8,128)(2,1)} collective-permute-done((bf16[128,2048]{1,0:T(8,128)(2,1)}, bf16[128,2048]{1,0:T(8,128)(2,1)}, u32[]{:S(2)}, u32[]{:S(2)}) %collective-permute-start.96) | collective-permute-done | bytes 524320 | tf_op jit(solution)/shard_map/ppermute | solution.py:32
  502.0 3.1 fusion.227
  507.8 8.5 %fusion.43 = bf16[2,256,8,64]{1,3,2,0:T(8,128)(2,1)} fusion(bf16[2,256,8,64]{1,3,2,0:T(8,128)(2,1)S(1)} %copy-done.29, f32[2,8,256,256]{2,3,1,0:T(8,128)} %fusion.117, f32[2,8,256,256]{2,3,1,0:T(8,128)} %copy-done.2, f32[2,8,256]{2,1,0:T(8,128)S(1)} %log_add_fusion), kind=kOutput, calls=%fused_computation.101 | convolution fusion | flops 141824256 | bytes 9453568 | tf_op jit(solution)/shard_map/bhqk,bqhd->bkhd/dot_general | solution.py:288
  516.3 7.7 %fusion.226 = (f32[8,64]{1,0:T(8,128)S(1)}, bf16[2,256,8,64]{1,3,2,0:T(8,128)(2,1)S(1)}) fusion(bf16[2,256,8,64]{1,3,2,0:T(8,128)(2,1)S(1)} %copy-done.30, f32[2,8,256,256]{2,3,1,0:T(8,128)} %fusion.117, f32[2,8,256,256]{2,3,1,0:T(8,128)} %copy-done.2, f32[2,8,256]{2,1,0:T(8,128)S(1)} %log_add_fusion), kind=kOutput, calls=%fused_computation.462 | convolution fusion | flops 142085888 | bytes 9455616 | tf_op jit(solution)/shard_map/bhqk,bkhd->bqhd/dot_general | solution.py:287
  539.4 5.2 fusion.234
  556.0 3.4 collective-permute-done.72
  560.5 7.2 %collective-permute-done.69 = bf16[2,128,768]{1,2,0:T(8,128)(2,1)S(1)} collective-permute-done((bf16[2,128,768]{1,2,0:T(8,128)(2,1)S(1)}, bf16[2,128,768]{1,2,0:T(8,128)(2,1)S(1)}, u32[]{:S(2)}, u32[]{:S(2)}) %collective-permute-start.69) | collective-permute-done | bytes 393248 | tf_op jit(solution)/shard_map/ppermute | solution.py:32
  573.4 3.7 collective-permute-done.70
  578.2 3.0 collective-permute-done.73
  593.0 4.9 collective-permute-start.83
  601.3 6.4 %collective-permute-start.60 = (f32[1,4096]{1,0:T(1,128)S(1)}, f32[1,4096]{1,0:T(1,128)S(1)}, u32[]{:S(2)}, u32[]{:S(2)}) collective-permute-start(f32[1,4096]{1,0:T(1,128)S(1)} %bitcast.357), channel_id=1, source_target_pairs={{0,8},{1,9},{2,10},{3,11},{4,12},{5,13},{6,14},{7,15},{8,0},{9,1},... | collective-permute-start | bytes 49160 | tf_op jit(solution)/shard_map/ppermute | solution.py:32
  (659 shorter events, 341.5 us)
Async XLA Ops:
  7.5 28.0 %collective-permute-start.5 = (bf16[1,1536]{1,0:T(2,128)(2,1)S(1)}, bf16[1,1536]{1,0:T(2,128)(2,1)}, u32[]{:S(2)}, u32[]{:S(2)}) collective-permute-start(bf16[1,1536]{1,0:T(2,128)(2,1)S(1)} %broadcast_in_dim.54), channel_id=1, source_target_pairs={{0,6},{1,7},{2,0},{3,1},{4,2},{5,3},{6,4},{7,5},{8,14},{9,15},{10,... | collective-permute-start | bytes 9224 | tf_op jit(solution)/shard_map/ppermute | solution.py:32
  11.7 22.6 %collective-permute-start.3 = (bf16[1,1536]{1,0:T(2,128)(2,1)S(1)}, bf16[1,1536]{1,0:T(2,128)(2,1)}, u32[]{:S(2)}, u32[]{:S(2)}) collective-permute-start(bf16[1,1536]{1,0:T(2,128)(2,1)S(1)} %broadcast_in_dim.54), channel_id=1, source_target_pairs={{0,4},{1,5},{2,6},{3,7},{4,0},{5,1},{6,2},{7,3},{8,12},{9,13},{10,... | collective-permute-start | bytes 9224 | tf_op jit(solution)/shard_map/ppermute | solution.py:32
  11.7 22.3 %collective-permute-start.1 = (bf16[1,1536]{1,0:T(2,128)(2,1)S(1)}, bf16[1,1536]{1,0:T(2,128)(2,1)}, u32[]{:S(2)}, u32[]{:S(2)}) collective-permute-start(bf16[1,1536]{1,0:T(2,128)(2,1)S(1)} %broadcast_in_dim.54), channel_id=1, source_target_pairs={{0,2},{1,3},{2,4},{3,5},{4,6},{5,7},{6,0},{7,1},{8,10},{9,11},{10,... | collective-permute-start | bytes 9224 | tf_op jit(solution)/shard_map/ppermute | solution.py:32
  12.2 23.7 %collective-permute-start = (bf16[1,1536]{1,0:T(2,128)(2,1)S(1)}, bf16[1,1536]{1,0:T(2,128)(2,1)}, u32[]{:S(2)}, u32[]{:S(2)}) collective-permute-start(bf16[1,1536]{1,0:T(2,128)(2,1)S(1)} %broadcast_in_dim.54), channel_id=1, source_target_pairs={{0,1},{1,0},{2,3},{3,2},{4,5},{5,4},{6,7},{7,6},{8,9},{9,8},{10,11... | collective-permute-start | bytes 9224 | tf_op jit(solution)/shard_map/ppermute | solution.py:32
  13.4 48.1 %collective-permute-start.47 = (bf16[128,1024]{1,0:T(8,128)(2,1)S(1)}, bf16[128,1024]{1,0:T(8,128)(2,1)}, u32[]{:S(2)}, u32[]{:S(2)}) collective-permute-start(bf16[128,1024]{1,0:T(8,128)(2,1)S(1)} %constant_dynamic-slice_fusion.16), channel_id=1, source_target_pairs={{0,16},{1,17},{2,18},{3,19},{4,20},{5,21},{6,22},{7,23},{8,24},{9,... | collective-permute-start | bytes 786440 | tf_op jit(solution)/shard_map/ppermute | solution.py:32
  48.4 53.3 %collective-permute-start.37 = (bf16[128,1024]{1,0:T(8,128)(2,1)S(1)}, bf16[128,1024]{1,0:T(8,128)(2,1)}, u32[]{:S(2)}, u32[]{:S(2)}) collective-permute-start(bf16[128,1024]{1,0:T(8,128)(2,1)S(1)} %constant_dynamic-slice_fusion.16), channel_id=1, source_target_pairs={{0,6},{1,7},{2,0},{3,1},{4,2},{5,3},{6,4},{7,5},{8,14},{9,15},{10,... | collective-permute-start | bytes 786440 | tf_op jit(solution)/shard_map/ppermute | solution.py:32
  52.9 52.4 %collective-permute-start.35 = (bf16[128,1024]{1,0:T(8,128)(2,1)S(1)}, bf16[128,1024]{1,0:T(8,128)(2,1)}, u32[]{:S(2)}, u32[]{:S(2)}) collective-permute-start(bf16[128,1024]{1,0:T(8,128)(2,1)S(1)} %constant_dynamic-slice_fusion.16), channel_id=1, source_target_pairs={{0,4},{1,5},{2,6},{3,7},{4,0},{5,1},{6,2},{7,3},{8,12},{9,13},{10,... | collective-permute-start | bytes 786440 | tf_op jit(solution)/shard_map/ppermute | solution.py:32
  61.5 27.7 %collective-permute-start.39 = (bf16[128,1024]{0,1:T(8,128)(2,1)S(1)}, bf16[128,1024]{0,1:T(8,128)(2,1)S(1)}, u32[]{:S(2)}, u32[]{:S(2)}) collective-permute-start(bf16[128,1024]{0,1:T(8,128)(2,1)S(1)} %bitcast.351), channel_id=1, source_target_pairs={{0,16},{1,17},{2,18},{3,19},{4,20},{5,21},{6,22},{7,23},{8,24},{9,... | collective-permute-start | bytes 786440 | tf_op jit(solution)/shard_map/ppermute | solution.py:32
  89.2 20.5 %collective-permute-start.8 = (bf16[128,1536]{0,1:T(8,128)(2,1)S(1)}, bf16[128,1536]{0,1:T(8,128)(2,1)}, u32[]{:S(2)}, u32[]{:S(2)}) collective-permute-start(bf16[128,1536]{0,1:T(8,128)(2,1)S(1)} %bitcast.341), channel_id=1, source_target_pairs={{0,1},{1,0},{2,3},{3,2},{4,5},{5,4},{6,7},{7,6},{8,9},{9,8},{10,11... | collective-permute-start | bytes 1179656 | tf_op jit(solution)/shard_map/ppermute | solution.py:32
  101.7 64.4 %collective-permute-start.56 = (bf16[256,1024]{1,0:T(8,128)(2,1)S(1)}, bf16[256,1024]{1,0:T(8,128)(2,1)}, u32[]{:S(2)}, u32[]{:S(2)}) collective-permute-start(bf16[256,1024]{1,0:T(8,128)(2,1)S(1)} %copy-done.34), channel_id=1, source_target_pairs={{0,8},{1,9},{2,10},{3,11},{4,12},{5,13},{6,14},{7,15},{8,0},{9,1},... | collective-permute-start | bytes 1572872 | tf_op jit(solution)/shard_map/ppermute | solution.py:32
  105.3 31.8 %collective-permute-start.28 = (bf16[128,1024]{0,1:T(8,128)(2,1)S(1)}, bf16[128,1024]{0,1:T(8,128)(2,1)}, u32[]{:S(2)}, u32[]{:S(2)}) collective-permute-start(bf16[128,1024]{0,1:T(8,128)(2,1)S(1)} %bitcast.354), channel_id=1, source_target_pairs={{0,4},{1,5},{2,6},{3,7},{4,0},{5,1},{6,2},{7,3},{8,12},{9,13},{10,... | collective-permute-start | bytes 786440 | tf_op jit(solution)/shard_map/ppermute | solution.py:32
  107.1 22.1 %collective-permute-start.38 = (bf16[128,1024]{1,0:T(8,128)(2,1)}, bf16[128,1024]{1,0:T(8,128)(2,1)}, u32[]{:S(2)}, u32[]{:S(2)}) collective-permute-start(bf16[128,1024]{1,0:T(8,128)(2,1)} %collective-permute-done.37), channel_id=1, source_target_pairs={{0,1},{1,0},{2,3},{3,2},{4,5},{5,4},{6,7},{7,6},{8,9},{9,8},{10,11... | collective-permute-start | bytes 786440 | tf_op jit(solution)/shard_map/ppermute | solution.py:32
  151.6 29.4 %collective-permute-start.52 = (bf16[128,1024]{1,0:T(8,128)(2,1)}, bf16[128,1024]{1,0:T(8,128)(2,1)}, u32[]{:S(2)}, u32[]{:S(2)}) collective-permute-start(bf16[128,1024]{1,0:T(8,128)(2,1)} %collective-permute-done.36), channel_id=1, source_target_pairs={{0,16},{1,17},{2,18},{3,19},{4,20},{5,21},{6,22},{7,23},{8,24},{9,... | collective-permute-start | bytes 786440 | tf_op jit(solution)/shard_map/ppermute | solution.py:32
  155.3 32.5 %collective-permute-start.50 = (bf16[128,1024]{1,0:T(8,128)(2,1)}, bf16[128,1024]{1,0:T(8,128)(2,1)}, u32[]{:S(2)}, u32[]{:S(2)}) collective-permute-start(bf16[128,1024]{1,0:T(8,128)(2,1)} %collective-permute-done.34), channel_id=1, source_target_pairs={{0,16},{1,17},{2,18},{3,19},{4,20},{5,21},{6,22},{7,23},{8,24},{9,... | collective-permute-start | bytes 786440 | tf_op jit(solution)/shard_map/ppermute | solution.py:32
  160.9 29.6 %collective-permute-start.11 = (bf16[128,1536]{0,1:T(8,128)(2,1)S(1)}, bf16[128,1536]{0,1:T(8,128)(2,1)}, u32[]{:S(2)}, u32[]{:S(2)}) collective-permute-start(bf16[128,1536]{0,1:T(8,128)(2,1)S(1)} %bitcast.343), channel_id=1, source_target_pairs={{0,4},{1,5},{2,6},{3,7},{4,0},{5,1},{6,2},{7,3},{8,12},{9,13},{10,... | collective-permute-start | bytes 1179656 | tf_op jit(solution)/shard_map/ppermute | solution.py:32
  161.6 30.2 %collective-permute-start.10 = (bf16[128,1536]{0,1:T(8,128)(2,1)}, bf16[128,1536]{0,1:T(8,128)(2,1)}, u32[]{:S(2)}, u32[]{:S(2)}) collective-permute-start(bf16[128,1536]{0,1:T(8,128)(2,1)} %collective-permute-done.9), channel_id=1, source_target_pairs={{0,1},{1,0},{2,3},{3,2},{4,5},{5,4},{6,7},{7,6},{8,9},{9,8},{10,11... | collective-permute-start | bytes 1179656 | tf_op jit(solution)/shard_map/ppermute | solution.py:32
  166.1 30.3 %collective-permute-start.13 = (bf16[128,1536]{0,1:T(8,128)(2,1)S(1)}, bf16[128,1536]{0,1:T(8,128)(2,1)}, u32[]{:S(2)}, u32[]{:S(2)}) collective-permute-start(bf16[128,1536]{0,1:T(8,128)(2,1)S(1)} %bitcast.344), channel_id=1, source_target_pairs={{0,6},{1,7},{2,0},{3,1},{4,2},{5,3},{6,4},{7,5},{8,14},{9,15},{10,... | collective-permute-start | bytes 1179656 | tf_op jit(solution)/shard_map/ppermute | solution.py:32
  181.1 31.1 %collective-permute-start.7 = (bf16[256,1024]{1,0:T(8,128)(2,1)S(1)}, bf16[256,1024]{1,0:T(8,128)(2,1)S(1)}, u32[]{:S(2)}, u32[]{:S(2)}) collective-permute-start(bf16[256,1024]{1,0:T(8,128)(2,1)S(1)} %fusion.48), channel_id=1, source_target_pairs={{0,8},{1,9},{2,10},{3,11},{4,12},{5,13},{6,14},{7,15},{8,0},{9,1},... | collective-permute-start | bytes 1572872 | tf_op jit(solution)/shard_map/ppermute | solution.py:32
  187.8 54.7 %collective-permute-start.23 = (bf16[1024,512]{1,0:T(8,128)(2,1)}, bf16[1024,512]{1,0:T(8,128)(2,1)}, u32[]{:S(2)}, u32[]{:S(2)}) collective-permute-start(bf16[1024,512]{1,0:T(8,128)(2,1)} %constant_dynamic-update-slice_fusion.32), channel_id=1, source_target_pairs={{0,8},{1,9},{2,10},{3,11},{4,12},{5,13},{6,14},{7,15},{8,0},{9,1},... | collective-permute-start | bytes 3145736 | tf_op jit(solution)/shard_map/ppermute | solution.py:32
  190.5 71.2 %collective-permute-start.45 = (bf16[128,1024]{0,1:T(8,128)(2,1)}, bf16[128,1024]{0,1:T(8,128)(2,1)}, u32[]{:S(2)}, u32[]{:S(2)}) collective-permute-start(bf16[128,1024]{0,1:T(8,128)(2,1)} %copy-done.61), channel_id=1, source_target_pairs={{0,16},{1,17},{2,18},{3,19},{4,20},{5,21},{6,22},{7,23},{8,24},{9,... | collective-permute-start | bytes 786440 | tf_op jit(solution)/shard_map/ppermute | solution.py:32
  196.4 62.8 %collective-permute-start.43 = (bf16[128,1024]{0,1:T(8,128)(2,1)}, bf16[128,1024]{0,1:T(8,128)(2,1)}, u32[]{:S(2)}, u32[]{:S(2)}) collective-permute-start(bf16[128,1024]{0,1:T(8,128)(2,1)} %collective-permute-done.28), channel_id=1, source_target_pairs={{0,16},{1,17},{2,18},{3,19},{4,20},{5,21},{6,22},{7,23},{8,24},{9,... | collective-permute-start | bytes 786440 | tf_op jit(solution)/shard_map/ppermute | solution.py:32
  211.3 27.1 %collective-permute-start.54 = (bf16[128,1024]{1,0:T(8,128)(2,1)}, bf16[128,1024]{1,0:T(8,128)(2,1)}, u32[]{:S(2)}, u32[]{:S(2)}) collective-permute-start(bf16[128,1024]{1,0:T(8,128)(2,1)} %collective-permute-done.38), channel_id=1, source_target_pairs={{0,16},{1,17},{2,18},{3,19},{4,20},{5,21},{6,22},{7,23},{8,24},{9,... | collective-permute-start | bytes 786440 | tf_op jit(solution)/shard_map/ppermute | solution.py:32
  238.3 25.1 %collective-permute-start.46 = (bf16[128,1024]{0,1:T(8,128)(2,1)}, bf16[128,1024]{0,1:T(8,128)(2,1)}, u32[]{:S(2)}, u32[]{:S(2)}) collective-permute-start(bf16[128,1024]{0,1:T(8,128)(2,1)} %collective-permute-done.31), channel_id=1, source_target_pairs={{0,16},{1,17},{2,18},{3,19},{4,20},{5,21},{6,22},{7,23},{8,24},{9,... | collective-permute-start | bytes 786440 | tf_op jit(solution)/shard_map/ppermute | solution.py:32
  281.7 82.7 %collective-permute-start.104 = (bf16[2,128,1024]{2,1,0:T(8,128)(2,1)}, bf16[2,128,1024]{2,1,0:T(8,128)(2,1)}, u32[]{:S(2)}, u32[]{:S(2)}) collective-permute-start(bf16[2,128,1024]{2,1,0:T(8,128)(2,1)} %bitcast.85), channel_id=1, source_target_pairs={{0,16},{1,17},{2,18},{3,19},{4,20},{5,21},{6,22},{7,23},{8,24},{9,... | collective-permute-start | bytes 1572872 | tf_op jit(solution)/shard_map/ppermute | solution.py:32
  283.0 104.1 %collective-permute-start.107 = (bf16[2,128,1024]{2,1,0:T(8,128)(2,1)}, bf16[2,128,1024]{2,1,0:T(8,128)(2,1)}, u32[]{:S(2)}, u32[]{:S(2)}) collective-permute-start(bf16[2,128,1024]{2,1,0:T(8,128)(2,1)} %bitcast.89), channel_id=1, source_target_pairs={{0,16},{1,17},{2,18},{3,19},{4,20},{5,21},{6,22},{7,23},{8,24},{9,... | collective-permute-start | bytes 1572872 | tf_op jit(solution)/shard_map/ppermute | solution.py:32
  283.1 79.5 %collective-permute-start.110 = (bf16[2,128,1024]{2,1,0:T(8,128)(2,1)}, bf16[2,128,1024]{2,1,0:T(8,128)(2,1)}, u32[]{:S(2)}, u32[]{:S(2)}) collective-permute-start(bf16[2,128,1024]{2,1,0:T(8,128)(2,1)} %bitcast.93), channel_id=1, source_target_pairs={{0,16},{1,17},{2,18},{3,19},{4,20},{5,21},{6,22},{7,23},{8,24},{9,... | collective-permute-start | bytes 1572872 | tf_op jit(solution)/shard_map/ppermute | solution.py:32
  284.5 75.7 %collective-permute-start.113 = (bf16[2,128,1024]{2,1,0:T(8,128)(2,1)}, bf16[2,128,1024]{2,1,0:T(8,128)(2,1)}, u32[]{:S(2)}, u32[]{:S(2)}) collective-permute-start(bf16[2,128,1024]{2,1,0:T(8,128)(2,1)} %bitcast.97), channel_id=1, source_target_pairs={{0,16},{1,17},{2,18},{3,19},{4,20},{5,21},{6,22},{7,23},{8,24},{9,... | collective-permute-start | bytes 1572872 | tf_op jit(solution)/shard_map/ppermute | solution.py:32
  308.8 133.1 %collective-permute-start.57 = (f32[256,1024]{1,0:T(8,128)}, f32[256,1024]{1,0:T(8,128)}, u32[]{:S(2)}, u32[]{:S(2)}) collective-permute-start(f32[256,1024]{1,0:T(8,128)} %slice.155), channel_id=1, source_target_pairs={{0,8},{1,9},{2,10},{3,11},{4,12},{5,13},{6,14},{7,15},{8,0},{9,1},... | collective-permute-start | bytes 3145736 | tf_op jit(solution)/shard_map/ppermute | solution.py:32
  362.7 22.3 %collective-permute-start.99 = (bf16[128,2048]{1,0:T(8,128)(2,1)S(1)}, bf16[128,2048]{1,0:T(8,128)(2,1)S(1)}, u32[]{:S(2)}, u32[]{:S(2)}) collective-permute-start(bf16[128,2048]{1,0:T(8,128)(2,1)S(1)} %fusion.93), channel_id=1, source_target_pairs={{0,1},{1,0},{2,3},{3,2},{4,5},{5,4},{6,7},{7,6},{8,9},{9,8},{10,11... | collective-permute-start | bytes 1572872 | tf_op jit(solution)/shard_map/ppermute | solution.py:32
  364.4 54.6 %collective-permute-start.95 = (bf16[128,2048]{1,0:T(8,128)(2,1)S(1)}, bf16[128,2048]{1,0:T(8,128)(2,1)S(1)}, u32[]{:S(2)}, u32[]{:S(2)}) collective-permute-start(bf16[128,2048]{1,0:T(8,128)(2,1)S(1)} %fusion.91), channel_id=1, source_target_pairs={{0,1},{1,0},{2,3},{3,2},{4,5},{5,4},{6,7},{7,6},{8,9},{9,8},{10,11... | collective-permute-start | bytes 1572872 | tf_op jit(solution)/shard_map/ppermute | solution.py:32
  373.8 47.9 %collective-permute-start.114 = (bf16[128,1024]{1,0:T(8,128)(2,1)S(1)}, bf16[128,1024]{1,0:T(8,128)(2,1)S(1)}, u32[]{:S(2)}, u32[]{:S(2)}) collective-permute-start(bf16[128,1024]{1,0:T(8,128)(2,1)S(1)} %fusion.121), channel_id=1, source_target_pairs={{0,1},{1,0},{2,3},{3,2},{4,5},{5,4},{6,7},{7,6},{8,9},{9,8},{10,11... | collective-permute-start | bytes 786440 | tf_op jit(solution)/shard_map/ppermute | solution.py:32
  385.0 22.5 %collective-permute-start.111 = (bf16[128,1024]{1,0:T(8,128)(2,1)S(1)}, bf16[128,1024]{1,0:T(8,128)(2,1)S(1)}, u32[]{:S(2)}, u32[]{:S(2)}) collective-permute-start(bf16[128,1024]{1,0:T(8,128)(2,1)S(1)} %fusion.120), channel_id=1, source_target_pairs={{0,1},{1,0},{2,3},{3,2},{4,5},{5,4},{6,7},{7,6},{8,9},{9,8},{10,11... | collective-permute-start | bytes 786440 | tf_op jit(solution)/shard_map/ppermute | solution.py:32
  387.1 26.0 %collective-permute-start.105 = (bf16[128,1024]{1,0:T(8,128)(2,1)S(1)}, bf16[128,1024]{1,0:T(8,128)(2,1)S(1)}, u32[]{:S(2)}, u32[]{:S(2)}) collective-permute-start(bf16[128,1024]{1,0:T(8,128)(2,1)S(1)} %fusion.118), channel_id=1, source_target_pairs={{0,1},{1,0},{2,3},{3,2},{4,5},{5,4},{6,7},{7,6},{8,9},{9,8},{10,11... | collective-permute-start | bytes 786440 | tf_op jit(solution)/shard_map/ppermute | solution.py:32
  421.7 22.3 %collective-permute-start.55 = (f32[256,1024]{1,0:T(8,128)S(1)}, f32[256,1024]{1,0:T(8,128)S(1)}, u32[]{:S(2)}, u32[]{:S(2)}) collective-permute-start(f32[256,1024]{1,0:T(8,128)S(1)} %slice.152), channel_id=1, source_target_pairs={{0,8},{1,9},{2,10},{3,11},{4,12},{5,13},{6,14},{7,15},{8,0},{9,1},... | collective-permute-start | bytes 3145736 | tf_op jit(solution)/shard_map/ppermute | solution.py:32
  423.0 30.7 %collective-permute-start.101 = (bf16[128,2048]{1,0:T(8,128)(2,1)}, bf16[128,2048]{1,0:T(8,128)(2,1)}, u32[]{:S(2)}, u32[]{:S(2)}) collective-permute-start(bf16[128,2048]{1,0:T(8,128)(2,1)} %fusion.94), channel_id=1, source_target_pairs={{0,1},{1,0},{2,3},{3,2},{4,5},{5,4},{6,7},{7,6},{8,9},{9,8},{10,11... | collective-permute-start | bytes 1572872 | tf_op jit(solution)/shard_map/ppermute | solution.py:32
  438.5 23.9 %collective-permute-start.100 = (bf16[128,2048]{1,0:T(8,128)(2,1)}, bf16[128,2048]{1,0:T(8,128)(2,1)}, u32[]{:S(2)}, u32[]{:S(2)}) collective-permute-start(bf16[128,2048]{1,0:T(8,128)(2,1)} %fusion.68), channel_id=1, source_target_pairs={{0,6},{1,7},{2,0},{3,1},{4,2},{5,3},{6,4},{7,5},{8,14},{9,15},{10,... | collective-permute-start | bytes 1572872 | tf_op jit(solution)/shard_map/ppermute | solution.py:32
  442.0 44.5 %collective-permute-start.96 = (bf16[128,2048]{1,0:T(8,128)(2,1)}, bf16[128,2048]{1,0:T(8,128)(2,1)}, u32[]{:S(2)}, u32[]{:S(2)}) collective-permute-start(bf16[128,2048]{1,0:T(8,128)(2,1)} %fusion.80), channel_id=1, source_target_pairs={{0,4},{1,5},{2,6},{3,7},{4,0},{5,1},{6,2},{7,3},{8,12},{9,13},{10,... | collective-permute-start | bytes 1572872 | tf_op jit(solution)/shard_map/ppermute | solution.py:32
  453.5 43.9 %collective-permute-start.115 = (bf16[128,1024]{1,0:T(8,128)(2,1)S(1)}, bf16[128,1024]{1,0:T(8,128)(2,1)}, u32[]{:S(2)}, u32[]{:S(2)}) collective-permute-start(bf16[128,1024]{1,0:T(8,128)(2,1)S(1)} %fusion.96), channel_id=1, source_target_pairs={{0,16},{1,17},{2,18},{3,19},{4,20},{5,21},{6,22},{7,23},{8,24},{9,... | collective-permute-start | bytes 786440 | tf_op jit(solution)/shard_map/ppermute | solution.py:32
  453.8 47.1 %collective-permute-start.58 = (bf16[256,512]{1,0:T(8,128)(2,1)S(1)}, bf16[256,512]{1,0:T(8,128)(2,1)}, u32[]{:S(2)}, u32[]{:S(2)}) collective-permute-start(bf16[256,512]{1,0:T(8,128)(2,1)S(1)} %bitcast.356), channel_id=1, source_target_pairs={{0,8},{1,9},{2,10},{3,11},{4,12},{5,13},{6,14},{7,15},{8,0},{9,1},... | collective-permute-start | bytes 786440 | tf_op jit(solution)/shard_map/ppermute | solution.py:32
  455.6 34.1 %collective-permute-start.91 = (f32[1,8192]{1,0:T(1,128)S(1)}, f32[1,8192]{1,0:T(1,128)S(1)}, u32[]{:S(2)}, u32[]{:S(2)}) collective-permute-start(f32[1,8192]{1,0:T(1,128)S(1)} %add.922), channel_id=1, source_target_pairs={{0,1},{1,0},{2,3},{3,2},{4,5},{5,4},{6,7},{7,6},{8,9},{9,8},{10,11... | collective-permute-start | bytes 98312 | tf_op jit(solution)/shard_map/ppermute | solution.py:32
  493.1 89.6 %collective-permute-start.79 = (bf16[1024,512]{1,0:T(8,128)(2,1)}, bf16[1024,512]{1,0:T(8,128)(2,1)}, u32[]{:S(2)}, u32[]{:S(2)}) collective-permute-start(bf16[1024,512]{1,0:T(8,128)(2,1)} %convolution_convert_fusion), channel_id=1, source_target_pairs={{0,8},{1,9},{2,10},{3,11},{4,12},{5,13},{6,14},{7,15},{8,0},{9,1},... | collective-permute-start | bytes 3145736 | tf_op jit(solution)/shard_map/ppermute | solution.py:32
  494.9 53.8 %collective-permute-start.102 = (bf16[128,2048]{1,0:T(8,128)(2,1)}, bf16[128,2048]{1,0:T(8,128)(2,1)}, u32[]{:S(2)}, u32[]{:S(2)}) collective-permute-start(bf16[128,2048]{1,0:T(8,128)(2,1)} %fusion.62), channel_id=1, source_target_pairs={{0,16},{1,17},{2,18},{3,19},{4,20},{5,21},{6,22},{7,23},{8,24},{9,... | collective-permute-start | bytes 1572872 | tf_op jit(solution)/shard_map/ppermute | solution.py:32
  499.3 69.6 %collective-permute-start.116 = (bf16[256,1024]{1,0:T(8,128)(2,1)}, bf16[256,1024]{1,0:T(8,128)(2,1)}, u32[]{:S(2)}, u32[]{:S(2)}) collective-permute-start(bf16[256,1024]{1,0:T(8,128)(2,1)} %pad_maximum_fusion.15), channel_id=1, source_target_pairs={{0,8},{1,9},{2,10},{3,11},{4,12},{5,13},{6,14},{7,15},{8,0},{9,1},... | collective-permute-start | bytes 1572872 | tf_op jit(solution)/shard_map/ppermute | solution.py:32
  553.6 47.0 %collective-permute-start.59 = (f32[256,1024]{1,0:T(8,128)S(1)}, f32[256,1024]{1,0:T(8,128)S(1)}, u32[]{:S(2)}, u32[]{:S(2)}) collective-permute-start(f32[256,1024]{1,0:T(8,128)S(1)} %slice.157), channel_id=1, source_target_pairs={{0,8},{1,9},{2,10},{3,11},{4,12},{5,13},{6,14},{7,15},{8,0},{9,1},... | collective-permute-start | bytes 3145736 | tf_op jit(solution)/shard_map/ppermute | solution.py:32
  592.0 24.5 %collective-permute-start.86 = (bf16[128,512]{1,0:T(8,128)(2,1)S(1)}, bf16[128,512]{1,0:T(8,128)(2,1)S(1)}, u32[]{:S(2)}, u32[]{:S(2)}) collective-permute-start(bf16[128,512]{1,0:T(8,128)(2,1)S(1)} %fusion.162), channel_id=1, source_target_pairs={{0,1},{1,0},{2,3},{3,2},{4,5},{5,4},{6,7},{7,6},{8,9},{9,8},{10,11... | collective-permute-start | bytes 393224 | tf_op jit(solution)/shard_map/ppermute | solution.py:32
  593.0 23.7 %collective-permute-start.83 = (bf16[128,512]{1,0:T(8,128)(2,1)S(1)}, bf16[128,512]{1,0:T(8,128)(2,1)S(1)}, u32[]{:S(2)}, u32[]{:S(2)}) collective-permute-start(bf16[128,512]{1,0:T(8,128)(2,1)S(1)} %fusion.141), channel_id=1, source_target_pairs={{0,2},{1,3},{2,4},{3,5},{4,6},{5,7},{6,0},{7,1},{8,10},{9,11},{10,... | collective-permute-start | bytes 393224 | tf_op jit(solution)/shard_map/ppermute | solution.py:32
  597.9 21.3 %collective-permute-start.85 = (bf16[128,512]{1,0:T(8,128)(2,1)S(1)}, bf16[128,512]{1,0:T(8,128)(2,1)S(1)}, u32[]{:S(2)}, u32[]{:S(2)}) collective-permute-start(bf16[128,512]{1,0:T(8,128)(2,1)S(1)} %fusion.140), channel_id=1, source_target_pairs={{0,6},{1,7},{2,0},{3,1},{4,2},{5,3},{6,4},{7,5},{8,14},{9,15},{10,... | collective-permute-start | bytes 393224 | tf_op jit(solution)/shard_map/ppermute | solution.py:32
  598.0 21.2 %collective-permute-start.81 = (bf16[128,512]{1,0:T(8,128)(2,1)S(1)}, bf16[128,512]{1,0:T(8,128)(2,1)S(1)}, u32[]{:S(2)}, u32[]{:S(2)}) collective-permute-start(bf16[128,512]{1,0:T(8,128)(2,1)S(1)} %fusion.142), channel_id=1, source_target_pairs={{0,4},{1,5},{2,6},{3,7},{4,0},{5,1},{6,2},{7,3},{8,12},{9,13},{10,... | collective-permute-start | bytes 393224 | tf_op jit(solution)/shard_map/ppermute | solution.py:32
  (152 other events, 1538.3 us)

commit v2 on v1

v2 whole, which is shorter than its diff:
```python
import functools
import math

import jax
import jax.numpy as jnp
import numpy as np
from jax import lax
from jax.experimental import pallas as pl
from jax.experimental.pallas import tpu as pltpu
from jax.sharding import PartitionSpec as P

H = 16
BF = jnp.bfloat16
F32 = jnp.float32
AXES = ("rep", "shard")
gelu_coef = math.sqrt(2.0 / math.pi)
VMEM_LIMIT = 60 * 2**20


class Place:
    def __init__(self, reps, shards):
        self.reps, self.shards = reps, shards
        self.nx = max(n for n in (1, 2, 4, 8) if shards % n == 0 and n * n <= shards)
        self.nz = nz = shards // self.nx
        rep, shard = lax.axis_index("rep"), lax.axis_index("shard")
        self.shard = shard
        self.slots = [(kz, kx) for kz in range(nz) for kx in range(self.nx)]
        table = np.zeros((reps * shards, 4 + 2 * shards), np.int32)
        for r in range(reps):
            for s in range(shards):
                y, core, z, x = r // 2, r % 2, s // self.nx, s % self.nx
                source = [(z - kz) % nz * self.nx + (x - kx) % self.nx for kz, kx in self.slots]
                in_half = [v - core * shards // 2 if v * 2 // shards == core else -1 for v in source]
                table[r * shards + s] = [y, core, z, x] + source + in_half
        row = lax.dynamic_slice_in_dim(jnp.asarray(table), rep * shards + shard, 1, 0)
        self.info = row[0]
        self.y, self.core, self.x = self.info[0], self.info[1], self.info[3]

    def _send(self, value, move, among=None):
        pairs = []
        for rep in range(self.reps):
            for shard in range(self.shards):
                here = (rep // 2, rep % 2, shard // self.nx, shard % self.nx)
                if among is None or among(*here):
                    y, core, z, x = move(*here)
                    pairs.append((rep * self.shards + shard, (y * 2 + core) * self.shards + z * self.nx + x))
        return lax.ppermute(value, AXES, pairs)

    def to_core(self, value):
        return self._send(value, lambda y, core, z, x: (y, 1 - core, z, x))

    def to_y(self, value):
        return self._send(value, lambda y, core, z, x: (1 - y, core, z, x))

    def to_z(self, value, k, among=None):
        return self._send(value, lambda y, core, z, x: (y, core, (z + k) % self.nz, x), among)

    def to_x(self, value, k, among=None):
        return self._send(value, lambda y, core, z, x: (y, core, z, (x + k) % self.nx), among)

    def gather(self, block, half=False):
        held_by_core = lambda core, z: z * 2 // self.nz == core
        held = [block] + [
            self.to_z(block, k, (lambda y, core, z, x: held_by_core(core, z)) if half else None)
            for k in range(1, self.nz)
        ]
        out = []
        for kz, value in enumerate(held):
            among = (lambda y, core, z, x, kz=kz: held_by_core(core, (z - kz) % self.nz)) if half else None
            out += [value] + [self.to_x(value, kx, among) for kx in range(1, self.nx)]
        return out

    def sum_all(self, value):
        value = value + self.to_core(value)
        value = value + self.to_y(value)
        value = sum([self.to_x(value, k) for k in range(1, self.nx)], value)
        return sum([self.to_z(value, k) for k in range(1, self.nz)], value)

    def z_groups(self):
        order = sorted(range(self.nz), key=lambda k: -min(k, self.nz - k))
        return order[: self.nz // 2], order[self.nz // 2 :]


def vmem():
    return pl.BlockSpec(memory_space=pltpu.VMEM)


def call(body, outs, ins, kinds, scratch=(), flops=0, name=None):
    spec = {
        "v": vmem(),
        "a": pl.BlockSpec(memory_space=pl.ANY),
        "s": pl.BlockSpec(memory_space=pltpu.SMEM),
    }
    moved = sum(v.size * v.dtype.itemsize for v in ins) + sum(math.prod(s) * jnp.dtype(t).itemsize for s, t in outs)
    return pl.pallas_call(
        body,
        out_shape=[jax.ShapeDtypeStruct(s, t) for s, t in outs],
        in_specs=[spec[k] for k in kinds],
        out_specs=[vmem() for _ in outs],
        scratch_shapes=list(scratch),
        compiler_params=pltpu.CompilerParams(vmem_limit_bytes=VMEM_LIMIT),
        cost_estimate=pl.CostEstimate(flops=flops, bytes_accessed=moved, transcendentals=0),
        name=name,
    )(*ins)


def dot(a, b):
    return jnp.dot(a, b, preferred_element_type=F32)


def dot_tn(a, b):
    return lax.dot_general(a, b, (((0,), (0,)), ((), ())), preferred_element_type=F32)


def dot_nt(a, b):
    return lax.dot_general(a, b, (((1,), (1,)), ((), ())), preferred_element_type=F32)


def layer_norm(values_in):
    centre = values_in - jnp.mean(values_in, axis=-1, keepdims=True)
    inv_std = lax.rsqrt(jnp.mean(centre * centre, axis=-1, keepdims=True) + 1e-05)
    return (centre * inv_std, inv_std)


def norm_back(grad_normed, normed, inv_std):
    return inv_std * (
        grad_normed
        - jnp.mean(grad_normed, axis=-1, keepdims=True)
        - normed * jnp.mean(grad_normed * normed, axis=-1, keepdims=True)
    )


def aligned(value, step):
    return pl.multiple_of(value, step) if step % 8 == 0 else value


def load_slots(slots, info, base, rows, target, sem, start):
    for i, slot in enumerate(slots):
        at = aligned(info[base + i] * rows, rows)
        copy = pltpu.make_async_copy(slot, target.at[pl.ds(at, rows), :], sem.at[i])
        if start:
            copy.start()
        else:
            copy.wait()


def load_half(slots, info, base, rows, target, sem, start):
    for i, slot in enumerate(slots):
        place = info[base + i]

        @pl.when(place >= 0)
        def _(i=i, slot=slot, place=place):
            at = aligned(place * rows, rows)
            copy = pltpu.make_async_copy(slot, target.at[pl.ds(at, rows), :], sem.at[i])
            if start:
                copy.start()
            else:
                copy.wait()


def load_down(slots, info, base, rows, target, sem, start):
    total = target.shape[0] // 2
    for i, slot in enumerate(slots):
        for part in range(2):
            half = jnp.bitwise_xor(info[0], part)
            at = aligned(half * total + info[base + i] * rows, rows)
            copy = pltpu.make_async_copy(
                slot.at[pl.ds(part * rows, rows), :], target.at[pl.ds(at, rows), :], sem.at[2 * i + part]
            )
            if start:
                copy.start()
            else:
                copy.wait()


def attention_kernel(n, rd, *refs):
    info, slopes, own, other, gain, bias, qv, *rest = refs
    slots, (nin_ref, qkv_ref, ctx_ref, probs_ref, wq, sem) = rest[:n], rest[n:]
    load_slots(slots, info, 4, rd, wq, sem, True)
    rows, width = own.shape
    half = width // 2
    for i, ref in enumerate((own, other)):
        normed, _ = layer_norm(ref[...].astype(F32))
        nin_ref[i * rows : (i + 1) * rows, :] = (normed * gain[...] + bias[...]).astype(BF)
    load_slots(slots, info, 4, rd, wq, sem, False)
    tile = 256

    @pl.loop(0, 3 * half // tile)
    def _(t):
        cols = pl.ds(pl.multiple_of(t * tile, tile), tile)
        qkv_ref[:, cols] = (dot(nin_ref[...], wq[:, cols]) + qv[:, cols]).astype(BF)

    hd = width // H
    lane = lax.broadcasted_iota(jnp.int32, (rows, 2 * hd), 1)
    first = lane < hd
    q_pos = lax.broadcasted_iota(jnp.int32, (rows, rows), 0)
    k_pos = lax.broadcasted_iota(jnp.int32, (rows, rows), 1)
    distance = (k_pos - q_pos).astype(F32)
    seen = k_pos <= q_pos
    pairs = half // (2 * hd)

    @pl.loop(0, 2 * pairs)
    def _(step):
        seq, pair = step // pairs, step % pairs
        at = pl.ds(pl.multiple_of(seq * rows, rows), rows)
        lanes = [pl.ds(pl.multiple_of(part * half + pair * 2 * hd, 2 * hd), 2 * hd) for part in range(3)]
        q, k, v = (qkv_ref[at, where] for where in lanes)
        out = []
        for i in range(2):
            mine = first if i == 0 else jnp.logical_not(first)
            scores = dot_nt(jnp.where(mine, q, jnp.zeros_like(q)), k) * hd ** (-0.5) + slopes[pair * 2 + i] * distance
            scores = jnp.where(seen, scores, -1e30)
            e = jnp.exp(scores - jnp.max(scores, axis=-1, keepdims=True))
            probs = (e * (1.0 / jnp.sum(e, axis=-1, keepdims=True))).astype(BF)
            probs_ref[step * 2 + i] = probs
            out.append(dot(probs, v))
        ctx_ref[at, lanes[0]] = jnp.where(first, out[0], out[1]).astype(BF)


def dense_kernel(n, rd, *refs):
    info, ctx, *rest = refs
    slots, (out_ref, wd, sem) = rest[:n], rest[n:]
    load_half(slots, info, 4 + n, rd, wd, sem, True)
    load_half(slots, info, 4 + n, rd, wd, sem, False)
    out_ref[...] = dot(ctx[...], wd[...])


def middle_kernel(own, other, part, recv, dense_b, gain, bias, res_ref, mid_ref):
    rows = own.shape[0]
    for i, ref in enumerate((own, other)):
        here, there = slice(i * rows, (i + 1) * rows), slice((1 - i) * rows, (2 - i) * rows)
        residual = ref[...].astype(F32) + (part[here, :] + recv[there, :]) + dense_b[...]
        res_ref[here, :] = residual
        normed, _ = layer_norm(residual)
        mid_ref[here, :] = (normed * gain[...] + bias[...]).astype(BF)


def up_kernel(n, rd, *refs):
    info, mid, up_b, *rest = refs
    slots, (act_ref, slope_ref, wu, sem) = rest[: 2 * n], rest[2 * n :]
    cols = slots[0].shape[1]
    for start in (True, False):
        for j in range(2):
            load_slots(
                slots[j * n : (j + 1) * n], info, 4, rd, wu.at[:, pl.ds(j * cols, cols)], sem.at[pl.ds(j * n, n)], start
            )
    tile = 256

    @pl.loop(0, 2 * cols // tile)
    def _(t):
        at = pl.ds(pl.multiple_of(t * tile, tile), tile)
        u = dot(mid[...], wu[:, at]) + up_b[:, at]
        t_ = jnp.tanh(gelu_coef * (u + 0.044715 * u * u * u))
        act_ref[:, at] = (0.5 * u * (1.0 + t_)).astype(BF)
        slope_ref[:, at] = 0.5 * (1.0 + t_) + 0.5 * u * (1.0 - t_ * t_) * gelu_coef * (
            1.0 + 3.0 * 0.044715 * u * u
        )


def feed_back_kernel(n, rd, quarter, *refs):
    info, own, other, slope, *rest = refs
    up_slots, down_slots, (gp_ref, gb_ref, gmid_ref, wu, wo, sem, sem2) = rest[: 2 * n], rest[2 * n : 3 * n], rest[3 * n :]
    cols = up_slots[0].shape[1]
    for start in (True, False):
        load_down(down_slots, info, 4, quarter, wo, sem2, start)
        for j in range(2):
            load_slots(
                up_slots[j * n : (j + 1) * n],
                info,
                4,
                rd,
                wu.at[:, pl.ds(j * cols, cols)],
                sem.at[pl.ds(j * n, n)],
                start,
            )
    rows = own.shape[0]
    tile = 256

    @pl.loop(0, 2 * cols // tile)
    def _(t):
        at = pl.ds(pl.multiple_of(t * tile, tile), tile)
        total = jnp.zeros((1, tile), F32)
        for i, ref in enumerate((own, other)):
            here = slice(i * rows, (i + 1) * rows)
            grad_pre = dot_nt(ref[...], wo[at, :]) * slope[here, at]
            gp_ref[here, at] = grad_pre.astype(BF)
            total = total + jnp.sum(grad_pre, axis=0, keepdims=True)
        gb_ref[:, at] = total

    width = own.shape[1]

    @pl.loop(0, width // tile)
    def _(t):
        at = pl.ds(pl.multiple_of(t * tile, tile), tile)
        gmid_ref[:, at] = dot_nt(gp_ref[...], wu[at, :])


def output_kernel(n, quarter, *refs):
    info, act, *rest = refs
    slots, (own_ref, other_ref, wo, sem) = rest[:n], rest[n:]
    for start in (True, False):
        load_down(slots, info, 4, quarter, wo, sem, start)
    rows, width = own_ref.shape
    tile = 256

    @pl.loop(0, width // tile)
    def _(t):
        at = pl.ds(pl.multiple_of(t * tile, tile), tile)
        both = dot(act[...], wo[:, at])
        own_ref[:, at] = both[:rows]
        other_ref[:, at] = both[rows:]


def owner_lanes(info, k, nz, size, base=0):
    return pl.ds(pl.multiple_of(base + lax.rem(info[2] + k, nz) * size, 128), size)


def grad_y_kernel(groups, nz, size, bases, by_y, info, left, *refs):
    right, outs = refs[: -2 * len(groups)], refs[-2 * len(groups) :]
    rows = right[0].shape[0]
    for g, ks in enumerate(groups):
        for j, k in enumerate(ks):
            for which in range(2):
                out = outs[2 * g + which]
                total = None
                for i, ref in enumerate(right):
                    here = slice(i * rows, (i + 1) * rows)
                    if by_y:
                        cols = out.shape[-1]
                        y = info[0] if which == 1 else 1 - info[0]
                        value = ref[:, pl.ds(pl.multiple_of(y * cols, 128), cols)]
                        lhs = left[here, owner_lanes(info, k, nz, size)]
                    else:
                        value = ref[...]
                        lhs = left[here, owner_lanes(info, k, nz, size, bases[1 - which])]
                    term = dot_tn(lhs, value)
                    total = term if total is None else total + term
                out[j] = total.astype(BF)


def grad_x_kernel(ks_groups, nz, nx, per, swap, info, left, right, *outs):
    size = nx * per
    for g, ks in enumerate(ks_groups):
        for j, k in enumerate(ks):
            for kx in range(nx):
                x = lax.rem(info[3] + kx, nx)
                out = outs[g * nx + kx]
                if nx * per % 128 == 0 and per % 128 == 0:
                    lanes = pl.ds(pl.multiple_of(lax.rem(info[2] + k, nz) * size + x * per, 128), per)
                    lhs = left[:, lanes]
                    rows = slice(None)
                else:
                    lhs = left[:, owner_lanes(info, k, nz, size)]
                    rows = None
                cols = right.shape[1] // 2
                for half in range(2):
                    value = dot_tn(lhs, right[:, half * cols : (half + 1) * cols]).astype(BF)
                    if rows is None:
                        picked = value[:per]
                        for v in range(1, nx):
                            picked = jnp.where(x == v, value[v * per : (v + 1) * per], picked)
                        value = picked
                    at = jnp.bitwise_xor(info[0], half) if swap else half
                    out[j, :, pl.ds(pl.multiple_of(at * cols, 128), cols)] = value


def fold_y_kernel(nx, per, info, mine, recv, *outs):
    for kx in range(nx):
        x = lax.rem(info[3] + kx, nx)
        at = pl.ds(aligned(x * per, per), per)
        outs[kx][...] = (mine[:, at, :].astype(F32) + recv[:, at, :].astype(F32)).astype(BF)


def fold_x_kernel(count, *refs):
    ins, outs = refs[:count], refs[count:]
    for j, out in enumerate(outs):
        out[...] = sum(ref[j].astype(F32) for ref in ins).astype(BF)


def sum_kernel(*refs):
    refs[-1][...] = sum(ref[...].astype(F32) for ref in refs[:-1]).astype(BF)


def attention_back_kernel(n, rd, *refs):
    info, part, recv, residual, own, other, gain, qkv, probs, *rest = refs
    slots, outs = rest[:n], rest[n:]
    res_ref, resb_ref, sums_ref, dqkv_ref, qvb_ref, wd, gctx, sem = outs
    load_half(slots, info, 4 + n, rd, wd, sem, True)
    rows, width = own.shape
    half = width // 2
    hd = width // H
    for i, ref in enumerate((own, other)):
        here, there = slice(i * rows, (i + 1) * rows), slice((1 - i) * rows, (2 - i) * rows)
        grad_mid = part[here, :] + recv[there, :]
        normed, inv_std = layer_norm(residual[here, :])
        grad_res = ref[...].astype(F32) + norm_back(grad_mid * gain[...], normed, inv_std)
        resb_ref[here, :] = grad_res.astype(BF)
        if i == 0:
            res_ref[...] = grad_res
            sums_ref[0:1, :] = jnp.sum(grad_mid * normed, axis=0, keepdims=True)
            sums_ref[1:2, :] = jnp.sum(grad_mid, axis=0, keepdims=True)
            sums_ref[2:3, :] = jnp.sum(grad_res, axis=0, keepdims=True)
    load_half(slots, info, 4 + n, rd, wd, sem, False)
    gctx[...] = dot_nt(resb_ref[...], wd[...]).astype(BF)

    lane = lax.broadcasted_iota(jnp.int32, (rows, 2 * hd), 1)
    first = lane < hd
    pairs = half // (2 * hd)
    qvb_ref[...] = jnp.zeros_like(qvb_ref)

    @pl.loop(0, 2 * pairs)
    def _(step):
        seq, pair = step // pairs, step % pairs
        at = pl.ds(pl.multiple_of(seq * rows, rows), rows)
        lanes = [pl.ds(pl.multiple_of(p * half + pair * 2 * hd, 2 * hd), 2 * hd) for p in range(3)]
        q, k, v = (qkv[at, where] for where in lanes)
        g = gctx[at, lanes[0]]
        dq, dk, dv = 0.0, 0.0, 0.0
        for i in range(2):
            mine = first if i == 0 else jnp.logical_not(first)
            g_i = jnp.where(mine, g, jnp.zeros_like(g))
            prob = probs[step * 2 + i]
            prob_f = prob.astype(F32)
            grad_probs = dot_nt(g_i, v)
            delta = jnp.sum(prob_f * grad_probs, axis=-1, keepdims=True)
            grad_scores = (prob_f * (grad_probs - delta) * hd ** (-0.5)).astype(BF)
            dq = dq + dot(grad_scores, jnp.where(mine, k, jnp.zeros_like(k)))
            dk = dk + dot_tn(grad_scores, jnp.where(mine, q, jnp.zeros_like(q)))
            dv = dv + dot_tn(prob, g_i)
        for where, value in zip(lanes, (dq, dk, dv)):
            dqkv_ref[at, where] = value.astype(BF)
        for row, value in ((0, dq), (1, dv)):
            qvb_ref[row : row + 1, lanes[0]] = qvb_ref[row : row + 1, lanes[0]] + jnp.sum(value, axis=0, keepdims=True)


def normed_kernel(n, rd, *refs):
    info, dqkv, *rest = refs
    slots, (own_ref, other_ref, wq, sem) = rest[:n], rest[n:]
    for start in (True, False):
        load_slots(slots, info, 4, rd, wq, sem, start)
    rows, width = own_ref.shape
    tile = 256

    @pl.loop(0, width // tile)
    def _(t):
        at = pl.ds(pl.multiple_of(t * tile, tile), tile)
        both = dot_nt(dqkv[...], wq[at, :])
        own_ref[:, at] = both[:rows]
        other_ref[:, at] = both[rows:]


def input_kernel(own, recv, hidden, grad_res, gain, in_ref, sums_ref):
    grad_normed = own[...] + recv[...]
    normed, inv_std = layer_norm(hidden[...].astype(F32))
    sums_ref[0:1, :] = jnp.sum(grad_normed * normed, axis=0, keepdims=True)
    sums_ref[1:2, :] = jnp.sum(grad_normed, axis=0, keepdims=True)
    in_ref[...] = grad_res[...] + norm_back(grad_normed * gain[...], normed, inv_std)


def pick(pair_first, pair_second, index):
    flip = index == 1
    return jnp.where(flip, pair_second, pair_first), jnp.where(flip, pair_first, pair_second)


def on_device(
    reps,
    shards,
    hidden_in,
    cotangent,
    ln1_gain,
    ln1_bias,
    w_qkv,
    qv_bias,
    w_dense,
    dense_bias,
    ln2_gain,
    ln2_bias,
    w_up,
    up_bias,
    w_down,
    down_bias,
):
    at = Place(reps, shards)
    info, core, y = at.info, at.core, at.y
    nz, nx, n = at.nz, at.nx, shards
    rows, width = hidden_in.shape
    rd = w_qkv.shape[0]
    ff = w_up.shape[1]
    quarter = ff // shards // 4
    half = width // 2
    heads = H // 2
    hd = width // H
    fq = shards * quarter
    dma = pltpu.SemaphoreType.DMA
    slopes = jnp.asarray(2.0 ** (-8.0 * (np.arange(H) + 1.0) / H), F32)
    slopes = lax.dynamic_slice_in_dim(slopes, core * heads, heads)

    qkv_half = lax.dynamic_index_in_dim(w_qkv.reshape(rd, 3, 2, half), core, 2, keepdims=False)
    qkv_slots = at.gather(qkv_half.reshape(rd, 3 * half))
    hidden_other = at.to_core(hidden_in)

    vectors = (ln1_gain, ln1_bias, qv_bias, dense_bias, ln2_gain, ln2_bias, up_bias, down_bias)
    packed = jnp.concatenate(vectors).astype(F32)[None, :]
    held = jnp.concatenate([packed] + [at.to_z(packed, k) for k in range(1, nz)])
    held = jnp.stack([held] + [at.to_x(held, k) for k in range(1, nx)], axis=1).reshape(n, -1)
    placed = info[4 : 4 + n][None, :] == jnp.arange(n)[:, None]
    packed = jnp.sum(jnp.where(placed[:, :, None], held[None], 0.0), axis=1)
    whole, start = [], 0
    for v in vectors:
        whole.append(packed[:, start : start + v.shape[0]].reshape(1, -1))
        start += v.shape[0]
    gain1, bias1, qv_b, dense_b, gain2, bias2, up_b, down_b = whole
    qv_half = lax.dynamic_index_in_dim(qv_b.reshape(2, 2, half), core, 1, keepdims=False)
    qkv_bias = jnp.concatenate([qv_half[:1], jnp.zeros((1, half), F32), qv_half[1:]], axis=1)
    up_b4 = lax.dynamic_index_in_dim(up_b.reshape(n, 2, 2, quarter), core, 1, keepdims=False)
    up_halves = jnp.concatenate(pick(up_b4[:, 0].reshape(1, -1), up_b4[:, 1].reshape(1, -1), y), axis=1)

    dense_slots = at.gather(w_dense, half=True)
    up_quarter = w_up.reshape(rd, n, 4, quarter)
    up_quarter = lax.dynamic_index_in_dim(up_quarter, core * 2 + y, 2, keepdims=False).reshape(rd, fq)
    up_slots = at.gather(up_quarter)
    up_slots = up_slots + [at.to_y(v) for v in up_slots]
    down_slots = at.gather(lax.dynamic_slice_in_dim(w_down, core * 2 * quarter, 2 * quarter, 0))
    cot_other = at.to_core(cotangent)

    mac = 2 * 2 * rows * width
    nin, qkv, ctx, probs = call(
        functools.partial(attention_kernel, n, rd),
        [((2 * rows, width), BF), ((2 * rows, 3 * half), BF), ((2 * rows, half), BF), ((2 * heads, rows, rows), BF)],
        [info, slopes, hidden_in, hidden_other, gain1, bias1, qkv_bias] + qkv_slots,
        "ss" + "v" * 5 + "a" * n,
        [pltpu.VMEM((width, 3 * half), BF), dma((n,))],
        mac * 4 * half,
        "attn",
    )
    (part,) = call(
        functools.partial(dense_kernel, n, rd),
        [((2 * rows, width), F32)],
        [info, ctx] + dense_slots,
        "sv" + "a" * n,
        [pltpu.VMEM((half, width), BF), dma((n,))],
        mac * half,
        "dense",
    )
    residual, mid = call(
        middle_kernel,
        [((2 * rows, width), F32), ((2 * rows, width), BF)],
        [hidden_in, hidden_other, part, at.to_core(part), dense_b, gain2, bias2],
        "v" * 7,
        name="middle",
    )
    act, slope = call(
        functools.partial(up_kernel, n, rd),
        [((2 * rows, 2 * fq), BF), ((2 * rows, 2 * fq), F32)],
        [info, mid, up_halves] + up_slots,
        "svv" + "a" * 2 * n,
        [pltpu.VMEM((width, 2 * fq), BF), dma((2 * n,))],
        mac * 2 * fq,
        "up",
    )

    groups = at.z_groups()

    def scatter_y(left, right, per, cols, bases, by_y, name):
        outs = [((len(ks), nx * per, cols), BF) for ks in groups for _ in range(2)]
        terms = call(
            functools.partial(grad_y_kernel, groups, nz, nx * per, bases, by_y),
            outs,
            [info, left] + right,
            "sv" + "v" * len(right),
            flops=mac * n * per * cols // width * 2,
            name=name,
        )
        sent = []
        for g, ks in enumerate(groups):
            away, mine = terms[2 * g], terms[2 * g + 1]
            parts = call(
                functools.partial(fold_y_kernel, nx, per),
                [((len(ks), per, cols), BF)] * nx,
                [info, mine, at.to_y(away)],
                "svv",
                name=name + "_y",
            )
            sent.append(parts)
        own = over_xz(sent, per, cols, name)
        return own, at.to_y(own)

    def over_xz(parts_of, per, cols, name):
        terms = []
        for ks, parts in zip(groups, parts_of):
            ins = [parts[0]] + [at.to_x(parts[kx], kx) for kx in range(1, nx)]
            sums = call(
                functools.partial(fold_x_kernel, nx),
                [((per, cols), BF)] * len(ks),
                ins,
                "v" * nx,
                name=name + "_x",
            )
            terms += [v if k == 0 else at.to_z(v, k) for k, v in zip(ks, sums)]
        return call(sum_kernel, [((per, cols), BF)], terms, "v" * nz, name=name + "_z")[0]

    def terms_x(left, right, per, cols, swap, name):
        outs = [((len(ks), per, cols), BF) for ks in groups for _ in range(nx)]
        terms = call(
            functools.partial(grad_x_kernel, groups, nz, nx, per, swap),
            outs,
            [info, left, right],
            "svv",
            flops=mac * n * per * cols // width,
            name=name,
        )
        return [terms[g * nx : (g + 1) * nx] for g in range(len(groups))]

    down_own, down_other = scatter_y(act, [cotangent, cot_other], quarter, width, (0, fq), False, "gdown")

    gpre, gpre_sums, gmid = call(
        functools.partial(feed_back_kernel, n, rd, quarter),
        [((2 * rows, 2 * fq), BF), ((1, 2 * fq), F32), ((2 * rows, width), F32)],
        [info, cotangent, cot_other, slope] + up_slots + down_slots,
        "svvv" + "a" * 3 * n,
        [pltpu.VMEM((width, 2 * fq), BF), pltpu.VMEM((2 * fq, width), BF), dma((2 * n,)), dma((2 * n,))],
        mac * 4 * fq,
        "feed_back",
    )
    gmid_recv = at.to_core(gmid)
    up_part = over_xz(terms_x(mid, gpre, rd, 2 * fq, True, "gup"), rd, 2 * fq, "gup")
    up_recv = at.to_y(up_part)

    grad_res, grad_res_b, sums2, dqkv, qv_sums = call(
        functools.partial(attention_back_kernel, n, rd),
        [
            ((rows, width), F32),
            ((2 * rows, width), BF),
            ((3, width), F32),
            ((2 * rows, 3 * half), BF),
            ((2, half), F32),
        ],
        [info, gmid, gmid_recv, residual, cotangent, cot_other, gain2, qkv, probs] + dense_slots,
        "s" + "v" * 8 + "a" * n,
        [pltpu.VMEM((half, width), BF), pltpu.VMEM((2 * rows, half), BF), dma((n,))],
        mac * 3 * half,
        "attn_back",
    )
    qkv_own, qkv_other = scatter_y(nin, [dqkv], rd, 3 * half // 2, None, True, "gqkv")

    def dense_terms(info_, left, right, *outs):
        for j in range(nz // 2):
            for kx in range(nx):
                x = lax.rem(info_[3] + kx, nx)
                if rd % 128 == 0:
                    lhs = left[:, pl.ds(pl.multiple_of((j * nx + x) * rd, 128), rd)]
                    outs[kx][j] = dot_tn(lhs, right[...]).astype(BF)
                else:
                    value = dot_tn(left[:, j * nx * rd : (j + 1) * nx * rd], right[...]).astype(BF)
                    picked = value[:rd]
                    for v in range(1, nx):
                        picked = jnp.where(x == v, value[v * rd : (v + 1) * rd], picked)
                    outs[kx][j] = picked

    dparts = call(
        dense_terms,
        [((nz // 2, rd, width), BF)] * nx,
        [info, ctx, grad_res_b],
        "svv",
        flops=mac * half,
        name="gdense",
    )
    dins = [dparts[0]] + [at.to_x(dparts[kx], kx) for kx in range(1, nx)]

    def dense_fold(info_, *refs):
        ins, outs = refs[:nx], refs[nx:]
        for k, out in enumerate(outs):
            place = lax.rem(info_[2] + k, nz) - info_[1] * (nz // 2)
            safe = jnp.clip(place, 0, nz // 2 - 1)
            out[...] = sum(ref[safe].astype(F32) for ref in ins).astype(BF)

    dsums = call(dense_fold, [((rd, width), BF)] * nz, [info] + dins, "s" + "v" * nx, name="gdense_x")
    toward = lambda k: lambda y, core, z, x: ((z + k) % nz) * 2 // nz == core
    dterms = [dsums[0]] + [at.to_z(dsums[k], k, toward(k)) for k in range(1, nz)]
    (dense_part,) = call(sum_kernel, [((rd, width), BF)], dterms, "v" * nz, name="gdense_z")
    dense_mine = dense_part.astype(F32) + at.to_y(dense_part).astype(F32)
    dense_recv = at.to_core(dense_mine)
    grad_dense = jnp.where(info[2] * 2 // nz == core, dense_mine, dense_recv)

    out_own, out_other = call(
        functools.partial(output_kernel, n, quarter),
        [((rows, width), F32), ((rows, width), F32)],
        [info, act] + down_slots,
        "sv" + "a" * n,
        [pltpu.VMEM((2 * fq, width), BF), dma((2 * n,))],
        mac * 2 * fq,
        "output",
    )
    output = (residual[:rows] + (out_own + at.to_core(out_other)) + down_b).astype(BF)

    norm_own, norm_other = call(
        functools.partial(normed_kernel, n, rd),
        [((rows, width), F32), ((rows, width), F32)],
        [info, dqkv] + qkv_slots,
        "sv" + "a" * n,
        [pltpu.VMEM((width, 3 * half), BF), dma((n,))],
        mac * 3 * half,
        "gnorm",
    )
    input_grad, sums1 = call(
        input_kernel,
        [((rows, width), F32), ((2, width), F32)],
        [norm_own, at.to_core(norm_other), hidden_in, grad_res, gain1],
        "v" * 5,
        name="input_grad",
    )

    down_y = jnp.concatenate(pick(down_own, down_other, y), axis=0)
    grad_down = jnp.concatenate(pick(down_y, at.to_core(down_y), core), axis=0).astype(F32)
    up_total = up_part.astype(F32) + up_recv.astype(F32)
    up_c = up_total.reshape(rd, 2, n, quarter).transpose(0, 2, 1, 3).reshape(rd, n, 1, 2 * quarter)
    grad_up = jnp.concatenate(pick(up_c, at.to_core(up_c), core), axis=2).reshape(rd, ff)
    qkv_c = jnp.concatenate(pick(qkv_own, qkv_other, y), axis=1).reshape(rd, 3, 1, half)
    grad_qkv = jnp.concatenate(pick(qkv_c, at.to_core(qkv_c), core), axis=2).reshape(rd, 3 * width).astype(F32)

    grad_down_bias = jnp.sum(cotangent.astype(F32), axis=0)
    up_y = jnp.stack([g.reshape(n, quarter) for g in pick(gpre_sums[0, :fq], gpre_sums[0, fq:], y)], axis=1)
    on_core = jnp.arange(2) == core
    up_bias_all = jnp.where(on_core[None, :, None, None], up_y[:, None], 0.0).reshape(-1)
    qv_all = jnp.where(on_core[None, :, None], qv_sums[:, None], 0.0).reshape(-1)
    feed = jnp.concatenate([sums2.reshape(-1), grad_down_bias, up_bias_all, sums1.reshape(-1), qv_all])
    feed = at.sum_all(feed[None, :])[0]

    def own(start, size):
        per = size // n
        return lax.dynamic_slice_in_dim(feed, start + at.shard * per, per)

    return (
        output,
        input_grad,
        own(4 * width + ff, width),
        own(5 * width + ff, width),
        grad_qkv,
        own(6 * width + ff, 2 * width),
        grad_dense,
        own(2 * width, width),
        own(0, width),
        own(width, width),
        grad_up,
        own(4 * width, ff),
        grad_down,
        own(3 * width, width),
    )


def solution(mesh):
    both, rows, vector = P(("rep", "shard"), None), P("shard", None), P("shard")
    weights = (vector, vector, rows, vector, rows, vector, vector, vector, rows, vector, rows, vector)
    return jax.shard_map(
        functools.partial(on_device, mesh.shape["rep"], mesh.shape["shard"]),
        mesh=mesh,
        in_specs=(both, both) + weights,
        out_specs=(both, both) + weights,
        check_vma=False,
    )
```

time: 644 us -> 497 us (0.77)
  local copies, waits for them, and re-layouts: 171 us -> 31.2 us
  Pallas kernels: 0 us -> 135 us
  matrix products: 94.3 us -> 0 us
  other arithmetic: 47.6 us -> 11.6 us
  starting transfers between devices: 149 us -> 121 us
  waiting for transfers between devices: 172 us -> 185 us
    pallas_call x0 -> x28, Pallas kernels: none -> 135 us  [call(): pl.pallas_call(body, out_shape=[jax.ShapeDtypeStruct(s, t) for s, t in ou...]
    dot_general x40 -> x0, matrix products: 94.3 us -> none  [the longest x22 29.4 us: dot_tn(): lax.dot_general(a, b, (((0,), (0,)), ((), ())), preferred_element_type=F32)]
    dynamic_update_slice x56 -> x0, local copies, waits for them, and re-layouts: 55.3 us -> none  [assemble(): lax.dynamic_update_slice(whole, block, (start,) + (0,) * (first.ndim - 1))]
    ppermute x117 -> x83, starting transfers between devices: 149 us -> 121 us  [_send(): return lax.ppermute(value, AXES, pairs)]
    another operation x12 -> x4, local copies, waits for them, and re-layouts: 23.8 us -> 0.06 us  [the longest x2 0.04 us: on_device(): jnp.stack([held] + [at.to_x(held, k) for k in range(1, nx)], axis=1)]
    slice x9 -> x4, local copies, waits for them, and re-layouts: 19.5 us -> 0.6 us  [the longest x1 0.58 us: on_device(): grad_dense = jnp.where(info[2] * 2 // nz == core, dense_mine, dense_recv)]
    ppermute x16 -> x0, local copies, waits for them, and re-layouts: 18.5 us -> none  [_send(): return lax.ppermute(value, AXES, pairs)]
    reshape x13 -> x3, local copies, waits for them, and re-layouts: 18.8 us -> 2.8 us  [the longest x1 1.85 us: on_device(): up_quarter = w_up.reshape(rd, n, 4, quarter)]
  transfers between devices with their start and end apart: 117 -> 83, of which waited for: 31 -> 27; matrix products, arithmetic and copies ran while one was open for 44% -> 6% of each run, Pallas kernels for 0% -> 23%
where the time goes in v2:
time: 497 us; the launch traced here: 493 us
  waiting for transfers between devices  185 us (37%)
  Pallas kernels  135 us (27%)
  starting transfers between devices  121 us (24%)
  local copies, waits for them, and re-layouts  31.2 us (6%)
  other arithmetic  11.6 us (2%)
  between operations  8.72 us (2%)
    ppermute x83, waiting for transfers between devices, _send(): return lax.ppermute(value, AXES, pairs)  185 us
    pallas_call x28, Pallas kernels, call(): pl.pallas_call(body, out_shape=[jax.ShapeDtypeStruct(s, t) for s, t in ou...  135 us
    ppermute x83, starting transfers between devices, _send(): return lax.ppermute(value, AXES, pairs)  121 us
    unnamed x103, local copies, waits for them, and re-layouts  19.1 us
  transfers between devices with their start and end apart: 83, of which 27 were waited for; matrix products, arithmetic and copies ran while one was open for 6% of the time, Pallas kernels for 23%

profile of v2, /device:TPU:1, one launch (start us, length us, event | category | flops | bytes accessed | tf_op | source)
XLA Modules:
  0.0 493.3 jit_solution(15552964545952122376)
XLA Ops:
  6.2 4.2 collective-permute-start.3
  20.3 6.9 %collective-permute-start.10 = (bf16[128,1536]{1,0:T(8,128)(2,1)}, bf16[128,1536]{1,0:T(8,128)(2,1)}, u32[]{:S(2)}, u32[]{:S(2)}) collective-permute-start(bf16[128,1536]{1,0:T(8,128)(2,1)} %copy.66.refs_7_.refs_2_), channel_id=1, source_target_pairs={{0,6},{1,7},{2,0},{3,1},{4,2},{5,3},{6,4},{7,5},{8,14},{9,15},{10,... | collective-permute-start | bytes 1179656 | tf_op jit(solution)/shard_map/ppermute | solution.py:47
  37.3 27.1 %collective-permute-done.8.refs_11_.refs_6_ = bf16[128,1536]{1,0:T(8,128)(2,1)} collective-permute-done((bf16[128,1536]{1,0:T(8,128)(2,1)}, bf16[128,1536]{1,0:T(8,128)(2,1)}, u32[]{:S(2)}, u32[]{:S(2)}) %collective-permute-start.8) | collective-permute-done | bytes 393248 | tf_op jit(solution)/shard_map/ppermute | solution.py:47
  68.2 3.1 collective-permute-start.16
  74.0 3.1 collective-permute-start.14
  77.8 4.7 collective-permute-done.7.refs_10_.refs_5_
  82.5 14.7 %attn.1 = (bf16[512,1024]{1,0:T(8,128)(2,1)}, bf16[512,1536]{1,0:T(8,128)(2,1)}, bf16[512,512]{1,0:T(8,128)(2,1)}, bf16[16,256,256]{2,1,0:T(8,128)(2,1)}) custom-call(s32[20]{0:T(128)} %get-tuple-element.187.refs_0_.info.info_, f32[8]{0:T(128)} %dynamic_slice.66.refs_1_, bf16[256,1024]{1,0:T(8,128)(2,1)} %hidden.1, bf16[256,1024]{1,0:T(8,128)(2,1)} %copy-done.20, ...), custom_call_target="tpu_custom_call" | custom-call | flops 2147483648 | bytes 9451632 | tf_op jit(solution)/shard_map/attn/pallas_call | solution.py:95
  98.2 4.3 dense.1.part
  102.6 4.1 collective-permute-start.19
  115.9 3.7 collective-permute-done.27.refs_11_.refs_12_
  120.5 11.2 %collective-permute-start.38 = (bf16[256,1024]{1,0:T(8,128)(2,1)S(1)}, bf16[256,1024]{1,0:T(8,128)(2,1)S(1)}, u32[]{:S(2)}, u32[]{:S(2)}) collective-permute-start(bf16[256,1024]{1,0:T(8,128)(2,1)S(1)} %constant_dynamic-slice_fusion.9.refs_2_.refs_20_), channel_id=1, source_target_pairs={{0,4},{1,5},{2,6},{3,7},{4,0},{5,1},{6,2},{7,3},{8,12},{9,13},{10,... | collective-permute-start | bytes 1572872 | tf_op jit(solution)/shard_map/ppermute | solution.py:47
  131.6 6.6 %collective-permute-done.23.refs_7_.refs_8_ = bf16[128,1024]{1,0:T(8,128)(2,1)} collective-permute-done((bf16[128,1024]{1,0:T(8,128)(2,1)S(1)}, bf16[128,1024]{1,0:T(8,128)(2,1)}, u32[]{:S(2)}, u32[]{:S(2)}) %collective-permute-start.23) | collective-permute-done | bytes 262176 | tf_op jit(solution)/shard_map/ppermute | solution.py:47
  139.5 4.9 collective-permute-done.20.refs_4_.refs_5_
  145.8 37.3 %collective-permute-done.38.refs_6_.refs_24_ = bf16[256,1024]{1,0:T(8,128)(2,1)S(1)} collective-permute-done((bf16[256,1024]{1,0:T(8,128)(2,1)S(1)}, bf16[256,1024]{1,0:T(8,128)(2,1)S(1)}, u32[]{:S(2)}, u32[]{:S(2)}) %collective-permute-start.38) | collective-permute-done | bytes 524320 | tf_op jit(solution)/shard_map/ppermute | solution.py:47
  186.0 4.1 collective-permute-done.31.refs_15_.refs_16_
  191.6 4.1 collective-permute-done.29.refs_13_.refs_14_
  197.9 3.5 collective-permute-done.28.refs_12_.refs_13_
  202.5 4.4 collective-permute-done.34.refs_18_.refs_19_
  206.9 3.7 collective-permute-start.43
  213.8 4.4 collective-permute-done.30.refs_14_.refs_15_
  220.2 4.6 middle.1
  224.9 11.8 %up.1 = (bf16[512,2048]{1,0:T(8,128)(2,1)}, f32[512,2048]{1,0:T(8,128)}) custom-call(s32[20]{0:T(128)} %get-tuple-element.187.refs_0_.info.info_, bf16[512,1024]{1,0:T(8,128)(2,1)} %get-tuple-element.76.refs_1_.left, f32[1,2048]{1,0:T(1,128)} %pad_maximum_fusion.5.refs_2_, bf16[128,1024]{1,0:T(8,128)(2,1)} %bitcast.94, ...), custom_call_target="tpu_custom_call" | custom-call | flops 2147483648 | bytes 11542608 | tf_op jit(solution)/shard_map/up/pallas_call | solution.py:95
  236.8 8.1 %collective-permute-done.37.refs_5_.refs_23_ = bf16[256,1024]{1,0:T(8,128)(2,1)} collective-permute-done((bf16[256,1024]{1,0:T(8,128)(2,1)S(1)}, bf16[256,1024]{1,0:T(8,128)(2,1)}, u32[]{:S(2)}, u32[]{:S(2)}) %collective-permute-start.37) | collective-permute-done | bytes 524320 | tf_op jit(solution)/shard_map/ppermute | solution.py:47
  244.9 14.5 %feed_back.1 = (bf16[512,2048]{1,0:T(8,128)(2,1)}, f32[1,2048]{1,0:T(1,128)}, f32[512,1024]{1,0:T(8,128)}) custom-call(s32[20]{0:T(128)} %get-tuple-element.187.refs_0_.info.info_, bf16[256,1024]{1,0:T(8,128)(2,1)} %refs_0_.1, bf16[256,1024]{1,0:T(8,128)(2,1)} %copy-done.19, f32[512,2048]{1,0:T(8,128)} %get-tuple-element.80.refs_3_, ...), custom_call_target="tpu_custom_call" | custom-call | flops 4294967296 | bytes 17834064 | tf_op jit(solution)/shard_map/feed_back/pallas_call | solution.py:95
  259.4 5.4 %gup.1 = (bf16[2,128,2048]{2,1,0:T(8,128)(2,1)}, bf16[2,128,2048]{2,1,0:T(8,128)(2,1)}, bf16[2,128,2048]{2,1,0:T(8,128)(2,1)}, bf16[2,128,2048]{2,1,0:T(8,128)(2,1)}) custom-call(s32[20]{0:T(128)} %get-tuple-element.187.refs_0_.info.info_, bf16[512,1024]{1,0:T(8,128)(2,1)} %get-tuple-element.76.refs_1_.left, bf16[512,2048]{1,0:T(8,128)(2,1)} %get-tuple-element.113.right), custom_call_target="tpu_custom_call" | custom-call | flops 2147483648 | bytes 7340112 | tf_op jit(solution)/shard_map/gup/pallas_call | solution.py:95
  266.3 5.3 %gdown.1 = (bf16[2,256,1024]{2,1,0:T(8,128)(2,1)}, bf16[2,256,1024]{2,1,0:T(8,128)(2,1)}, bf16[2,256,1024]{2,1,0:T(8,128)(2,1)}, bf16[2,256,1024]{2,1,0:T(8,128)(2,1)}) custom-call(s32[20]{0:T(128)} %get-tuple-element.187.refs_0_.info.info_, bf16[512,2048]{1,0:T(8,128)(2,1)} %get-tuple-element.77.refs_1_.left, bf16[256,1024]{1,0:T(8,128)(2,1)} %refs_0_.1, ...), custom_call_target="tpu_custom_call" | custom-call | flops 2147483648 | bytes 7340112 | tf_op jit(solution)/shard_map/gdown/pallas_call | solution.py:95
  273.1 5.7 %collective-permute-start.44 = (f32[512,1024]{1,0:T(8,128)}, f32[512,1024]{1,0:T(8,128)}, u32[]{:S(2)}, u32[]{:S(2)}) collective-permute-start(f32[512,1024]{1,0:T(8,128)} %get-tuple-element.81.refs_1_), channel_id=1, source_target_pairs={{0,8},{1,9},{2,10},{3,11},{4,12},{5,13},{6,14},{7,15},{8,0},{9,1},... | collective-permute-start | bytes 6291464 | tf_op jit(solution)/shard_map/ppermute | solution.py:47
  278.8 6.4 %collective-permute-done.67.refs_1_ = bf16[2,128,2048]{2,1,0:T(8,128)(2,1)} collective-permute-done((bf16[2,128,2048]{2,1,0:T(8,128)(2,1)}, bf16[2,128,2048]{2,1,0:T(8,128)(2,1)}, u32[]{:S(2)}, u32[]{:S(2)}) %collective-permute-start.67) | collective-permute-done | bytes 1048608 | tf_op jit(solution)/shard_map/ppermute | solution.py:47
  287.9 19.8 %collective-permute-done.70.refs_1_ = bf16[2,128,2048]{2,1,0:T(8,128)(2,1)S(1)} collective-permute-done((bf16[2,128,2048]{2,1,0:T(8,128)(2,1)}, bf16[2,128,2048]{2,1,0:T(8,128)(2,1)S(1)}, u32[]{:S(2)}, u32[]{:S(2)}) %collective-permute-start.70) | collective-permute-done | bytes 1048608 | tf_op jit(solution)/shard_map/ppermute | solution.py:47
  308.7 8.1 %output.1 = (f32[256,1024]{1,0:T(8,128)}, f32[256,1024]{1,0:T(8,128)}) custom-call(s32[20]{0:T(128)} %get-tuple-element.187.refs_0_.info.info_, bf16[512,2048]{1,0:T(8,128)(2,1)} %get-tuple-element.77.refs_1_.left, bf16[256,1024]{1,0:T(8,128)(2,1)} %copy-done.25, bf16[256,1024]{1,0:T(8,128)(2,1)} %collective-permute-done.35.refs_3_.refs_21_, ...), custom_call_target="tpu_custom_call" | custom-call | flops 2147483648 | bytes 8388688 | tf_op jit(solution)/shard_map/output/pallas_call | solution.py:95
  316.8 5.5 %collective-permute-start.42 = (f32[256,1024]{1,0:T(8,128)}, f32[256,1024]{1,0:T(8,128)}, u32[]{:S(2)}, u32[]{:S(2)}) collective-permute-start(f32[256,1024]{1,0:T(8,128)} %get-tuple-element.79), channel_id=1, source_target_pairs={{0,8},{1,9},{2,10},{3,11},{4,12},{5,13},{6,14},{7,15},{8,0},{9,1},... | collective-permute-start | bytes 3145736 | tf_op jit(solution)/shard_map/ppermute | solution.py:47
  324.9 2.8 collective-permute-start.71
  330.5 2.7 gdown_y.2
  342.7 6.2 %collective-permute-done.75.refs_1_ = bf16[2,128,1024]{2,1,0:T(8,128)(2,1)S(1)} collective-permute-done((bf16[2,128,1024]{2,1,0:T(8,128)(2,1)}, bf16[2,128,1024]{2,1,0:T(8,128)(2,1)S(1)}, u32[]{:S(2)}, u32[]{:S(2)}) %collective-permute-start.75) | collective-permute-done | bytes 524320 | tf_op jit(solution)/shard_map/ppermute | solution.py:47
  351.7 8.4 %collective-permute-done.79.refs_1_ = bf16[2,128,1024]{2,1,0:T(8,128)(2,1)S(1)} collective-permute-done((bf16[2,128,1024]{2,1,0:T(8,128)(2,1)}, bf16[2,128,1024]{2,1,0:T(8,128)(2,1)S(1)}, u32[]{:S(2)}, u32[]{:S(2)}) %collective-permute-start.79) | collective-permute-done | bytes 524320 | tf_op jit(solution)/shard_map/ppermute | solution.py:47
  368.4 8.1 %collective-permute-done.80.refs_2_ = bf16[128,1024]{1,0:T(8,128)(2,1)S(1)} collective-permute-done((bf16[128,1024]{1,0:T(8,128)(2,1)}, bf16[128,1024]{1,0:T(8,128)(2,1)S(1)}, u32[]{:S(2)}, u32[]{:S(2)}) %collective-permute-start.80) | collective-permute-done | bytes 262176 | tf_op jit(solution)/shard_map/ppermute | solution.py:47
  380.7 13.3 %attn_back.1 = (f32[256,1024]{1,0:T(8,128)}, bf16[512,1024]{1,0:T(8,128)(2,1)}, f32[3,1024]{1,0:T(4,128)}, bf16[512,1536]{1,0:T(8,128)(2,1)}, f32[2,512]{1,0:T(2,128)}) custom-call(s32[20]{0:T(128)} %get-tuple-element.187.refs_0_.info.info_, f32[512,1024]{1,0:T(8,128)} %get-tuple-element.81.refs_1_, f32[512,1024]{1,0:T(8,128)} %collective-permute-done.44.refs_2_, ...), custom_call_target="tpu_custom_call" | custom-call | flops 1610612736 | bytes 16797776 | tf_op jit(solution)/shard_map/attn_back/pallas_call | solution.py:95
  394.0 7.0 %gnorm.1 = (f32[256,1024]{1,0:T(8,128)}, f32[256,1024]{1,0:T(8,128)}) custom-call(s32[20]{0:T(128)} %get-tuple-element.187.refs_0_.info.info_, bf16[512,1536]{1,0:T(8,128)(2,1)} %get-tuple-element.84.refs_1_.refs_0_, bf16[128,1536]{1,0:T(8,128)(2,1)} %copy.66.refs_7_.refs_2_, bf16[128,1536]{1,0:T(8,128)(2,1)} %collective-permute-done.5.refs_8_.refs_3_, ...), custom_call_target="tpu_custom_call" | custom-call | flops 1610612736 | bytes 6815824 | tf_op jit(solution)/shard_map/gnorm/pallas_call | solution.py:95
  402.5 3.0 gdense.1
  406.7 4.9 %gqkv.1 = (bf16[2,256,768]{2,1,0:T(8,128)(2,1)}, bf16[2,256,768]{2,1,0:T(8,128)(2,1)}, bf16[2,256,768]{2,1,0:T(8,128)(2,1)}, bf16[2,256,768]{2,1,0:T(8,128)(2,1)}) custom-call(s32[20]{0:T(128)} %get-tuple-element.187.refs_0_.info.info_, bf16[512,1024]{1,0:T(8,128)(2,1)} %get-tuple-element.93.left, bf16[512,1536]{1,0:T(8,128)(2,1)} %get-tuple-element.84.refs_1_.refs_0_), custom_call_target="tpu_custom_call" | custom-call | flops 1610612736 | bytes 5767248 | tf_op jit(solution)/shard_map/gqkv/pallas_call | solution.py:95
  413.1 6.3 %collective-permute-done.61.refs_1_ = bf16[2,128,1024]{2,1,0:T(8,128)(2,1)} collective-permute-done((bf16[2,128,1024]{2,1,0:T(8,128)(2,1)}, bf16[2,128,1024]{2,1,0:T(8,128)(2,1)}, u32[]{:S(2)}, u32[]{:S(2)}) %collective-permute-start.61) | collective-permute-done | bytes 524320 | tf_op jit(solution)/shard_map/ppermute | solution.py:47
  425.7 5.1 %collective-permute-done.52.recv = bf16[2,256,768]{2,1,0:T(8,128)(2,1)} collective-permute-done((bf16[2,256,768]{2,1,0:T(8,128)(2,1)}, bf16[2,256,768]{2,1,0:T(8,128)(2,1)}, u32[]{:S(2)}, u32[]{:S(2)}) %collective-permute-start.52) | collective-permute-done | bytes 786464 | tf_op jit(solution)/shard_map/ppermute | solution.py:47
  430.9 3.6 collective-permute-start.63
  437.1 3.8 input_grad.1
  461.4 2.9 copy.74
  471.2 6.0 %collective-permute-start.66 = (f32[128,1024]{1,0:T(8,128)S(1)}, f32[128,1024]{1,0:T(8,128)S(1)}, u32[]{:S(2)}, u32[]{:S(2)}) collective-permute-start(f32[128,1024]{1,0:T(8,128)S(1)} %convert_add_fusion), channel_id=1, source_target_pairs={{0,8},{1,9},{2,10},{3,11},{4,12},{5,13},{6,14},{7,15},{8,0},{9,1},... | collective-permute-start | bytes 1572872 | tf_op jit(solution)/shard_map/ppermute | solution.py:47
  481.8 2.8 collective-permute-done.59
  485.8 3.6 collective-permute-start.60
  (311 shorter events, 138.6 us)
Async XLA Ops:
  10.4 16.9 %collective-permute-start.1 = (f32[1,1536]{1,0:T(1,128)S(1)}, f32[1,1536]{1,0:T(1,128)S(1)}, u32[]{:S(2)}, u32[]{:S(2)}) collective-permute-start(f32[1,1536]{1,0:T(1,128)S(1)} %convert_element_type.37), channel_id=1, source_target_pairs={{0,2},{1,3},{2,4},{3,5},{4,6},{5,7},{6,0},{7,1},{8,10},{9,11},{10,... | collective-permute-start | bytes 18440 | tf_op jit(solution)/shard_map/ppermute | solution.py:47
  10.8 21.2 %collective-permute-start.17 = (bf16[128,1024]{1,0:T(8,128)(2,1)}, bf16[128,1024]{1,0:T(8,128)(2,1)S(1)}, u32[]{:S(2)}, u32[]{:S(2)}) collective-permute-start(bf16[128,1024]{1,0:T(8,128)(2,1)} %refs_9_.1), channel_id=1, source_target_pairs={{0,6},{1,7},{2,0},{3,1},{12,10},{13,11},{14,12},{15,13},{16,22},{1... | collective-permute-start | bytes 786440 | tf_op jit(solution)/shard_map/ppermute | solution.py:47
  11.5 21.7 %collective-permute-start.15 = (bf16[128,1024]{1,0:T(8,128)(2,1)}, bf16[128,1024]{1,0:T(8,128)(2,1)}, u32[]{:S(2)}, u32[]{:S(2)}) collective-permute-start(bf16[128,1024]{1,0:T(8,128)(2,1)} %refs_9_.1), channel_id=1, source_target_pairs={{0,4},{1,5},{2,6},{3,7},{12,8},{13,9},{14,10},{15,11},{16,20},{17,... | collective-permute-start | bytes 786440 | tf_op jit(solution)/shard_map/ppermute | solution.py:47
  30.0 34.4 %collective-permute-start.8 = (bf16[128,1536]{1,0:T(8,128)(2,1)}, bf16[128,1536]{1,0:T(8,128)(2,1)}, u32[]{:S(2)}, u32[]{:S(2)}) collective-permute-start(bf16[128,1536]{1,0:T(8,128)(2,1)} %copy.66.refs_7_.refs_2_), channel_id=1, source_target_pairs={{0,4},{1,5},{2,6},{3,7},{4,0},{5,1},{6,2},{7,3},{8,12},{9,13},{10,... | collective-permute-start | bytes 1179656 | tf_op jit(solution)/shard_map/ppermute | solution.py:47
  32.1 33.8 %collective-permute-start.6 = (bf16[128,1536]{1,0:T(8,128)(2,1)}, bf16[128,1536]{1,0:T(8,128)(2,1)}, u32[]{:S(2)}, u32[]{:S(2)}) collective-permute-start(bf16[128,1536]{1,0:T(8,128)(2,1)} %copy.66.refs_7_.refs_2_), channel_id=1, source_target_pairs={{0,2},{1,3},{2,4},{3,5},{4,6},{5,7},{6,0},{7,1},{8,10},{9,11},{10,... | collective-permute-start | bytes 1179656 | tf_op jit(solution)/shard_map/ppermute | solution.py:47
  33.2 34.3 %collective-permute-start = (bf16[256,1024]{1,0:T(8,128)(2,1)S(1)}, bf16[256,1024]{1,0:T(8,128)(2,1)S(1)}, u32[]{:S(2)}, u32[]{:S(2)}) collective-permute-start(bf16[256,1024]{1,0:T(8,128)(2,1)S(1)} %copy-done.6), channel_id=1, source_target_pairs={{0,8},{1,9},{2,10},{3,11},{4,12},{5,13},{6,14},{7,15},{8,0},{9,1},... | collective-permute-start | bytes 1572872 | tf_op jit(solution)/shard_map/ppermute | solution.py:47
  35.3 31.5 %collective-permute-start.5 = (bf16[128,1536]{1,0:T(8,128)(2,1)}, bf16[128,1536]{1,0:T(8,128)(2,1)}, u32[]{:S(2)}, u32[]{:S(2)}) collective-permute-start(bf16[128,1536]{1,0:T(8,128)(2,1)} %copy.66.refs_7_.refs_2_), channel_id=1, source_target_pairs={{0,1},{1,0},{2,3},{3,2},{4,5},{5,4},{6,7},{7,6},{8,9},{9,8},{10,11... | collective-permute-start | bytes 1179656 | tf_op jit(solution)/shard_map/ppermute | solution.py:47
  36.6 31.6 %collective-permute-start.11 = (bf16[128,1536]{1,0:T(8,128)(2,1)}, bf16[128,1536]{1,0:T(8,128)(2,1)}, u32[]{:S(2)}, u32[]{:S(2)}) collective-permute-start(bf16[128,1536]{1,0:T(8,128)(2,1)} %collective-permute-done.10.refs_13_.refs_8_), channel_id=1, source_target_pairs={{0,1},{1,0},{2,3},{3,2},{4,5},{5,4},{6,7},{7,6},{8,9},{9,8},{10,11... | collective-permute-start | bytes 1179656 | tf_op jit(solution)/shard_map/ppermute | solution.py:47
  66.8 30.4 %collective-permute-start.12 = (bf16[128,1024]{1,0:T(8,128)(2,1)S(1)}, bf16[128,1024]{1,0:T(8,128)(2,1)S(1)}, u32[]{:S(2)}, u32[]{:S(2)}) collective-permute-start(bf16[128,1024]{1,0:T(8,128)(2,1)S(1)} %copy-done.8), channel_id=1, source_target_pairs={{0,1},{1,0},{2,3},{3,2},{12,13},{13,12},{14,15},{15,14},{16,17},{1... | collective-permute-start | bytes 786440 | tf_op jit(solution)/shard_map/ppermute | solution.py:47
  67.5 29.8 %collective-permute-start.18 = (bf16[128,1024]{1,0:T(8,128)(2,1)S(1)}, bf16[128,1024]{1,0:T(8,128)(2,1)S(1)}, u32[]{:S(2)}, u32[]{:S(2)}) collective-permute-start(bf16[128,1024]{1,0:T(8,128)(2,1)S(1)} %collective-permute-done.17.refs_8_.refs_15_), channel_id=1, source_target_pairs={{0,1},{1,0},{6,7},{7,6},{10,11},{11,10},{12,13},{13,12},{16,17},{1... | collective-permute-start | bytes 786440 | tf_op jit(solution)/shard_map/ppermute | solution.py:47
  68.2 29.1 %collective-permute-start.16 = (bf16[128,1024]{1,0:T(8,128)(2,1)}, bf16[128,1024]{1,0:T(8,128)(2,1)S(1)}, u32[]{:S(2)}, u32[]{:S(2)}) collective-permute-start(bf16[128,1024]{1,0:T(8,128)(2,1)} %collective-permute-done.15.refs_6_.refs_13_), channel_id=1, source_target_pairs={{4,5},{5,4},{6,7},{7,6},{8,9},{9,8},{10,11},{11,10},{20,21},{21,20... | collective-permute-start | bytes 786440 | tf_op jit(solution)/shard_map/ppermute | solution.py:47
  74.0 23.3 %collective-permute-start.14 = (bf16[128,1024]{1,0:T(8,128)(2,1)S(1)}, bf16[128,1024]{1,0:T(8,128)(2,1)S(1)}, u32[]{:S(2)}, u32[]{:S(2)}) collective-permute-start(bf16[128,1024]{1,0:T(8,128)(2,1)S(1)} %collective-permute-done.13.refs_4_.refs_11_), channel_id=1, source_target_pairs={{2,3},{3,2},{4,5},{5,4},{8,9},{9,8},{14,15},{15,14},{18,19},{19,18... | collective-permute-start | bytes 786440 | tf_op jit(solution)/shard_map/ppermute | solution.py:47
  102.6 116.8 %collective-permute-start.19 = (f32[512,1024]{1,0:T(8,128)}, f32[512,1024]{1,0:T(8,128)}, u32[]{:S(2)}, u32[]{:S(2)}) collective-permute-start(f32[512,1024]{1,0:T(8,128)} %dense.1.part), channel_id=1, source_target_pairs={{0,8},{1,9},{2,10},{3,11},{4,12},{5,13},{6,14},{7,15},{8,0},{9,1},... | collective-permute-start | bytes 6291464 | tf_op jit(solution)/shard_map/ppermute | solution.py:47
  112.8 25.5 %collective-permute-start.23 = (bf16[128,1024]{1,0:T(8,128)(2,1)S(1)}, bf16[128,1024]{1,0:T(8,128)(2,1)}, u32[]{:S(2)}, u32[]{:S(2)}) collective-permute-start(bf16[128,1024]{1,0:T(8,128)(2,1)S(1)} %bitcast.91), channel_id=1, source_target_pairs={{0,4},{1,5},{2,6},{3,7},{4,0},{5,1},{6,2},{7,3},{8,12},{9,13},{10,... | collective-permute-start | bytes 786440 | tf_op jit(solution)/shard_map/ppermute | solution.py:47
  115.1 23.1 %collective-permute-start.21 = (bf16[128,1024]{1,0:T(8,128)(2,1)S(1)}, bf16[128,1024]{1,0:T(8,128)(2,1)}, u32[]{:S(2)}, u32[]{:S(2)}) collective-permute-start(bf16[128,1024]{1,0:T(8,128)(2,1)S(1)} %bitcast.92), channel_id=1, source_target_pairs={{0,2},{1,3},{2,4},{3,5},{4,6},{5,7},{6,0},{7,1},{8,10},{9,11},{10,... | collective-permute-start | bytes 786440 | tf_op jit(solution)/shard_map/ppermute | solution.py:47
  119.6 25.0 %collective-permute-start.40 = (bf16[256,1024]{1,0:T(8,128)(2,1)S(1)}, bf16[256,1024]{1,0:T(8,128)(2,1)S(1)}, u32[]{:S(2)}, u32[]{:S(2)}) collective-permute-start(bf16[256,1024]{1,0:T(8,128)(2,1)S(1)} %constant_dynamic-slice_fusion.9.refs_2_.refs_20_), channel_id=1, source_target_pairs={{0,6},{1,7},{2,0},{3,1},{4,2},{5,3},{6,4},{7,5},{8,14},{9,15},{10,... | collective-permute-start | bytes 1572872 | tf_op jit(solution)/shard_map/ppermute | solution.py:47
  120.5 62.6 %collective-permute-start.38 = (bf16[256,1024]{1,0:T(8,128)(2,1)S(1)}, bf16[256,1024]{1,0:T(8,128)(2,1)S(1)}, u32[]{:S(2)}, u32[]{:S(2)}) collective-permute-start(bf16[256,1024]{1,0:T(8,128)(2,1)S(1)} %constant_dynamic-slice_fusion.9.refs_2_.refs_20_), channel_id=1, source_target_pairs={{0,4},{1,5},{2,6},{3,7},{4,0},{5,1},{6,2},{7,3},{8,12},{9,13},{10,... | collective-permute-start | bytes 1572872 | tf_op jit(solution)/shard_map/ppermute | solution.py:47
  138.2 45.1 %collective-permute-start.36 = (bf16[256,1024]{1,0:T(8,128)(2,1)S(1)}, bf16[256,1024]{1,0:T(8,128)(2,1)S(1)}, u32[]{:S(2)}, u32[]{:S(2)}) collective-permute-start(bf16[256,1024]{1,0:T(8,128)(2,1)S(1)} %constant_dynamic-slice_fusion.9.refs_2_.refs_20_), channel_id=1, source_target_pairs={{0,2},{1,3},{2,4},{3,5},{4,6},{5,7},{6,0},{7,1},{8,10},{9,11},{10,... | collective-permute-start | bytes 1572872 | tf_op jit(solution)/shard_map/ppermute | solution.py:47
  144.3 40.2 %collective-permute-start.33 = (bf16[128,1024]{1,0:T(8,128)(2,1)}, bf16[128,1024]{1,0:T(8,128)(2,1)}, u32[]{:S(2)}, u32[]{:S(2)}) collective-permute-start(bf16[128,1024]{1,0:T(8,128)(2,1)} %collective-permute-done.25.refs_9_.refs_10_), channel_id=1, source_target_pairs={{0,16},{1,17},{2,18},{3,19},{4,20},{5,21},{6,22},{7,23},{8,24},{9,... | collective-permute-start | bytes 786440 | tf_op jit(solution)/shard_map/ppermute | solution.py:47
  144.6 41.2 %collective-permute-start.26 = (bf16[128,1024]{1,0:T(8,128)(2,1)}, bf16[128,1024]{1,0:T(8,128)(2,1)}, u32[]{:S(2)}, u32[]{:S(2)}) collective-permute-start(bf16[128,1024]{1,0:T(8,128)(2,1)} %collective-permute-done.25.refs_9_.refs_10_), channel_id=1, source_target_pairs={{0,1},{1,0},{2,3},{3,2},{4,5},{5,4},{6,7},{7,6},{8,9},{9,8},{10,11... | collective-permute-start | bytes 786440 | tf_op jit(solution)/shard_map/ppermute | solution.py:47
  190.3 16.6 %collective-permute-start.34 = (bf16[128,1024]{1,0:T(8,128)(2,1)}, bf16[128,1024]{1,0:T(8,128)(2,1)}, u32[]{:S(2)}, u32[]{:S(2)}) collective-permute-start(bf16[128,1024]{1,0:T(8,128)(2,1)} %collective-permute-done.26.refs_10_.refs_11_), channel_id=1, source_target_pairs={{0,16},{1,17},{2,18},{3,19},{4,20},{5,21},{6,22},{7,23},{8,24},{9,... | collective-permute-start | bytes 786440 | tf_op jit(solution)/shard_map/ppermute | solution.py:47
  195.7 16.9 %collective-permute-start.32 = (bf16[128,1024]{1,0:T(8,128)(2,1)}, bf16[128,1024]{1,0:T(8,128)(2,1)}, u32[]{:S(2)}, u32[]{:S(2)}) collective-permute-start(bf16[128,1024]{1,0:T(8,128)(2,1)} %collective-permute-done.24.refs_8_.refs_9_), channel_id=1, source_target_pairs={{0,16},{1,17},{2,18},{3,19},{4,20},{5,21},{6,22},{7,23},{8,24},{9,... | collective-permute-start | bytes 786440 | tf_op jit(solution)/shard_map/ppermute | solution.py:47
  195.9 22.2 %collective-permute-start.30 = (bf16[128,1024]{1,0:T(8,128)(2,1)}, bf16[128,1024]{1,0:T(8,128)(2,1)}, u32[]{:S(2)}, u32[]{:S(2)}) collective-permute-start(bf16[128,1024]{1,0:T(8,128)(2,1)} %collective-permute-done.22.refs_6_.refs_7_), channel_id=1, source_target_pairs={{0,16},{1,17},{2,18},{3,19},{4,20},{5,21},{6,22},{7,23},{8,24},{9,... | collective-permute-start | bytes 786440 | tf_op jit(solution)/shard_map/ppermute | solution.py:47
  201.3 35.4 %collective-permute-start.35 = (bf16[256,1024]{1,0:T(8,128)(2,1)S(1)}, bf16[256,1024]{1,0:T(8,128)(2,1)}, u32[]{:S(2)}, u32[]{:S(2)}) collective-permute-start(bf16[256,1024]{1,0:T(8,128)(2,1)S(1)} %constant_dynamic-slice_fusion.9.refs_2_.refs_20_), channel_id=1, source_target_pairs={{0,1},{1,0},{2,3},{3,2},{4,5},{5,4},{6,7},{7,6},{8,9},{9,8},{10,11... | collective-permute-start | bytes 1572872 | tf_op jit(solution)/shard_map/ppermute | solution.py:47
  206.9 29.8 %collective-permute-start.43 = (bf16[256,1024]{1,0:T(8,128)(2,1)S(1)}, bf16[256,1024]{1,0:T(8,128)(2,1)S(1)}, u32[]{:S(2)}, u32[]{:S(2)}) collective-permute-start(bf16[256,1024]{1,0:T(8,128)(2,1)S(1)} %copy-done.4), channel_id=1, source_target_pairs={{0,8},{1,9},{2,10},{3,11},{4,12},{5,13},{6,14},{7,15},{8,0},{9,1},... | collective-permute-start | bytes 1572872 | tf_op jit(solution)/shard_map/ppermute | solution.py:47
  212.6 24.2 %collective-permute-start.41 = (bf16[256,1024]{1,0:T(8,128)(2,1)S(1)}, bf16[256,1024]{1,0:T(8,128)(2,1)}, u32[]{:S(2)}, u32[]{:S(2)}) collective-permute-start(bf16[256,1024]{1,0:T(8,128)(2,1)S(1)} %collective-permute-done.40.refs_8_.refs_26_), channel_id=1, source_target_pairs={{0,1},{1,0},{2,3},{3,2},{4,5},{5,4},{6,7},{7,6},{8,9},{9,8},{10,11... | collective-permute-start | bytes 1572872 | tf_op jit(solution)/shard_map/ppermute | solution.py:47
  218.2 18.6 %collective-permute-start.39 = (bf16[256,1024]{1,0:T(8,128)(2,1)S(1)}, bf16[256,1024]{1,0:T(8,128)(2,1)}, u32[]{:S(2)}, u32[]{:S(2)}) collective-permute-start(bf16[256,1024]{1,0:T(8,128)(2,1)S(1)} %collective-permute-done.38.refs_6_.refs_24_), channel_id=1, source_target_pairs={{0,1},{1,0},{2,3},{3,2},{4,5},{5,4},{6,7},{7,6},{8,9},{9,8},{10,11... | collective-permute-start | bytes 1572872 | tf_op jit(solution)/shard_map/ppermute | solution.py:47
  219.4 25.5 %collective-permute-start.37 = (bf16[256,1024]{1,0:T(8,128)(2,1)S(1)}, bf16[256,1024]{1,0:T(8,128)(2,1)}, u32[]{:S(2)}, u32[]{:S(2)}) collective-permute-start(bf16[256,1024]{1,0:T(8,128)(2,1)S(1)} %collective-permute-done.36.refs_4_.refs_22_), channel_id=1, source_target_pairs={{0,1},{1,0},{2,3},{3,2},{4,5},{5,4},{6,7},{7,6},{8,9},{9,8},{10,11... | collective-permute-start | bytes 1572872 | tf_op jit(solution)/shard_map/ppermute | solution.py:47
  264.9 20.4 %collective-permute-start.67 = (bf16[2,128,2048]{2,1,0:T(8,128)(2,1)}, bf16[2,128,2048]{2,1,0:T(8,128)(2,1)}, u32[]{:S(2)}, u32[]{:S(2)}) collective-permute-start(bf16[2,128,2048]{2,1,0:T(8,128)(2,1)} %get-tuple-element.115), channel_id=1, source_target_pairs={{0,1},{1,0},{2,3},{3,2},{4,5},{5,4},{6,7},{7,6},{8,9},{9,8},{10,11... | collective-permute-start | bytes 3145736 | tf_op jit(solution)/shard_map/ppermute | solution.py:47
  266.1 41.6 %collective-permute-start.70 = (bf16[2,128,2048]{2,1,0:T(8,128)(2,1)}, bf16[2,128,2048]{2,1,0:T(8,128)(2,1)S(1)}, u32[]{:S(2)}, u32[]{:S(2)}) collective-permute-start(bf16[2,128,2048]{2,1,0:T(8,128)(2,1)} %get-tuple-element.119), channel_id=1, source_target_pairs={{0,1},{1,0},{2,3},{3,2},{4,5},{5,4},{6,7},{7,6},{8,9},{9,8},{10,11... | collective-permute-start | bytes 3145736 | tf_op jit(solution)/shard_map/ppermute | solution.py:47
  271.6 45.2 %collective-permute-start.74 = (bf16[2,256,1024]{2,1,0:T(8,128)(2,1)}, bf16[2,256,1024]{2,1,0:T(8,128)(2,1)S(1)}, u32[]{:S(2)}, u32[]{:S(2)}) collective-permute-start(bf16[2,256,1024]{2,1,0:T(8,128)(2,1)} %get-tuple-element.123), channel_id=1, source_target_pairs={{0,16},{1,17},{2,18},{3,19},{4,20},{5,21},{6,22},{7,23},{8,24},{9,... | collective-permute-start | bytes 3145736 | tf_op jit(solution)/shard_map/ppermute | solution.py:47
  271.9 53.1 %collective-permute-start.78 = (bf16[2,256,1024]{2,1,0:T(8,128)(2,1)}, bf16[2,256,1024]{2,1,0:T(8,128)(2,1)S(1)}, u32[]{:S(2)}, u32[]{:S(2)}) collective-permute-start(bf16[2,256,1024]{2,1,0:T(8,128)(2,1)} %get-tuple-element.129), channel_id=1, source_target_pairs={{0,16},{1,17},{2,18},{3,19},{4,20},{5,21},{6,22},{7,23},{8,24},{9,... | collective-permute-start | bytes 3145736 | tf_op jit(solution)/shard_map/ppermute | solution.py:47
  273.1 107.6 %collective-permute-start.44 = (f32[512,1024]{1,0:T(8,128)}, f32[512,1024]{1,0:T(8,128)}, u32[]{:S(2)}, u32[]{:S(2)}) collective-permute-start(f32[512,1024]{1,0:T(8,128)} %get-tuple-element.81.refs_1_), channel_id=1, source_target_pairs={{0,8},{1,9},{2,10},{3,11},{4,12},{5,13},{6,14},{7,15},{8,0},{9,1},... | collective-permute-start | bytes 6291464 | tf_op jit(solution)/shard_map/ppermute | solution.py:47
  287.9 48.0 %collective-permute-start.68 = (bf16[128,2048]{1,0:T(8,128)(2,1)}, bf16[128,2048]{1,0:T(8,128)(2,1)}, u32[]{:S(2)}, u32[]{:S(2)}) collective-permute-start(bf16[128,2048]{1,0:T(8,128)(2,1)} %get-tuple-element.116), channel_id=1, source_target_pairs={{0,4},{1,5},{2,6},{3,7},{4,0},{5,1},{6,2},{7,3},{8,12},{9,13},{10,... | collective-permute-start | bytes 1572872 | tf_op jit(solution)/shard_map/ppermute | solution.py:47
  307.7 29.4 %collective-permute-start.69 = (bf16[128,2048]{1,0:T(8,128)(2,1)}, bf16[128,2048]{1,0:T(8,128)(2,1)}, u32[]{:S(2)}, u32[]{:S(2)}) collective-permute-start(bf16[128,2048]{1,0:T(8,128)(2,1)} %get-tuple-element.117), channel_id=1, source_target_pairs={{0,2},{1,3},{2,4},{3,5},{4,6},{5,7},{6,0},{7,1},{8,10},{9,11},{10,... | collective-permute-start | bytes 1572872 | tf_op jit(solution)/shard_map/ppermute | solution.py:47
  316.8 46.1 %collective-permute-start.42 = (f32[256,1024]{1,0:T(8,128)}, f32[256,1024]{1,0:T(8,128)}, u32[]{:S(2)}, u32[]{:S(2)}) collective-permute-start(f32[256,1024]{1,0:T(8,128)} %get-tuple-element.79), channel_id=1, source_target_pairs={{0,8},{1,9},{2,10},{3,11},{4,12},{5,13},{6,14},{7,15},{8,0},{9,1},... | collective-permute-start | bytes 3145736 | tf_op jit(solution)/shard_map/ppermute | solution.py:47
  337.1 23.0 %collective-permute-start.79 = (bf16[2,128,1024]{2,1,0:T(8,128)(2,1)}, bf16[2,128,1024]{2,1,0:T(8,128)(2,1)S(1)}, u32[]{:S(2)}, u32[]{:S(2)}) collective-permute-start(bf16[2,128,1024]{2,1,0:T(8,128)(2,1)} %get-tuple-element.131), channel_id=1, source_target_pairs={{0,1},{1,0},{2,3},{3,2},{4,5},{5,4},{6,7},{7,6},{8,9},{9,8},{10,11... | collective-permute-start | bytes 1572872 | tf_op jit(solution)/shard_map/ppermute | solution.py:47
  342.4 37.1 %collective-permute-start.72 = (bf16[128,2048]{1,0:T(8,128)(2,1)}, bf16[128,2048]{1,0:T(8,128)(2,1)S(1)}, u32[]{:S(2)}, u32[]{:S(2)}) collective-permute-start(bf16[128,2048]{1,0:T(8,128)(2,1)} %gup_z.1), channel_id=1, source_target_pairs={{0,16},{1,17},{2,18},{3,19},{4,20},{5,21},{6,22},{7,23},{8,24},{9,... | collective-permute-start | bytes 1572872 | tf_op jit(solution)/shard_map/ppermute | solution.py:47
  379.3 21.9 %collective-permute-start.81 = (bf16[128,1024]{1,0:T(8,128)(2,1)}, bf16[128,1024]{1,0:T(8,128)(2,1)S(1)}, u32[]{:S(2)}, u32[]{:S(2)}) collective-permute-start(bf16[128,1024]{1,0:T(8,128)(2,1)} %gdown_z.1), channel_id=1, source_target_pairs={{0,16},{1,17},{2,18},{3,19},{4,20},{5,21},{6,22},{7,23},{8,24},{9,... | collective-permute-start | bytes 786440 | tf_op jit(solution)/shard_map/ppermute | solution.py:47
  379.8 79.0 %collective-permute-start.73 = (f32[128,8,1,256]{3,1,0,2:T(8,128)S(1)}, f32[128,8,1,256]{3,1,0,2:T(8,128)S(1)}, u32[]{:S(2)}, u32[]{:S(2)}) collective-permute-start(f32[128,8,1,256]{3,1,0,2:T(8,128)S(1)} %bitcast.82), channel_id=1, source_target_pairs={{0,8},{1,9},{2,10},{3,11},{4,12},{5,13},{6,14},{7,15},{8,0},{9,1},... | collective-permute-start | bytes 3145736 | tf_op jit(solution)/shard_map/ppermute | solution.py:47
  401.0 35.8 %collective-permute-start.45 = (f32[256,1024]{1,0:T(8,128)}, f32[256,1024]{1,0:T(8,128)}, u32[]{:S(2)}, u32[]{:S(2)}) collective-permute-start(f32[256,1024]{1,0:T(8,128)} %get-tuple-element.86), channel_id=1, source_target_pairs={{0,8},{1,9},{2,10},{3,11},{4,12},{5,13},{6,14},{7,15},{8,0},{9,1},... | collective-permute-start | bytes 3145736 | tf_op jit(solution)/shard_map/ppermute | solution.py:47
  402.0 21.0 %collective-permute-start.82 = (bf16[256,1024]{1,0:T(8,128)(2,1)}, bf16[256,1024]{1,0:T(8,128)(2,1)S(1)}, u32[]{:S(2)}, u32[]{:S(2)}) collective-permute-start(bf16[256,1024]{1,0:T(8,128)(2,1)} %pad_maximum_fusion.1), channel_id=1, source_target_pairs={{0,8},{1,9},{2,10},{3,11},{4,12},{5,13},{6,14},{7,15},{8,0},{9,1},... | collective-permute-start | bytes 1572872 | tf_op jit(solution)/shard_map/ppermute | solution.py:47
  411.7 19.2 %collective-permute-start.52 = (bf16[2,256,768]{2,1,0:T(8,128)(2,1)}, bf16[2,256,768]{2,1,0:T(8,128)(2,1)}, u32[]{:S(2)}, u32[]{:S(2)}) collective-permute-start(bf16[2,256,768]{2,1,0:T(8,128)(2,1)} %get-tuple-element.95), channel_id=1, source_target_pairs={{0,16},{1,17},{2,18},{3,19},{4,20},{5,21},{6,22},{7,23},{8,24},{9,... | collective-permute-start | bytes 2359304 | tf_op jit(solution)/shard_map/ppermute | solution.py:47
  419.3 30.6 %collective-permute-start.56 = (bf16[2,256,768]{2,1,0:T(8,128)(2,1)}, bf16[2,256,768]{2,1,0:T(8,128)(2,1)}, u32[]{:S(2)}, u32[]{:S(2)}) collective-permute-start(bf16[2,256,768]{2,1,0:T(8,128)(2,1)} %get-tuple-element.101), channel_id=1, source_target_pairs={{0,16},{1,17},{2,18},{3,19},{4,20},{5,21},{6,22},{7,23},{8,24},{9,... | collective-permute-start | bytes 2359304 | tf_op jit(solution)/shard_map/ppermute | solution.py:47
  423.8 17.8 %collective-permute-start.62 = (bf16[128,1024]{1,0:T(8,128)(2,1)}, bf16[128,1024]{1,0:T(8,128)(2,1)S(1)}, u32[]{:S(2)}, u32[]{:S(2)}) collective-permute-start(bf16[128,1024]{1,0:T(8,128)(2,1)} %get-tuple-element.110), channel_id=1, source_target_pairs={{0,2},{1,3},{6,0},{7,1},{10,12},{11,13},{12,14},{13,15},{16,18},{1... | collective-permute-start | bytes 786440 | tf_op jit(solution)/shard_map/ppermute | solution.py:47
  436.9 17.0 %collective-permute-start.53 = (bf16[2,128,768]{2,1,0:T(8,128)(2,1)}, bf16[2,128,768]{2,1,0:T(8,128)(2,1)S(1)}, u32[]{:S(2)}, u32[]{:S(2)}) collective-permute-start(bf16[2,128,768]{2,1,0:T(8,128)(2,1)} %get-tuple-element.97), channel_id=1, source_target_pairs={{0,1},{1,0},{2,3},{3,2},{4,5},{5,4},{6,7},{7,6},{8,9},{9,8},{10,11... | collective-permute-start | bytes 1179656 | tf_op jit(solution)/shard_map/ppermute | solution.py:47
  448.7 21.7 %collective-permute-start.65 = (bf16[128,1024]{1,0:T(8,128)(2,1)}, bf16[128,1024]{1,0:T(8,128)(2,1)S(1)}, u32[]{:S(2)}, u32[]{:S(2)}) collective-permute-start(bf16[128,1024]{1,0:T(8,128)(2,1)} %gdense_z.1), channel_id=1, source_target_pairs={{0,16},{1,17},{2,18},{3,19},{4,20},{5,21},{6,22},{7,23},{8,24},{9,... | collective-permute-start | bytes 786440 | tf_op jit(solution)/shard_map/ppermute | solution.py:47
  471.2 19.3 %collective-permute-start.66 = (f32[128,1024]{1,0:T(8,128)S(1)}, f32[128,1024]{1,0:T(8,128)S(1)}, u32[]{:S(2)}, u32[]{:S(2)}) collective-permute-start(f32[128,1024]{1,0:T(8,128)S(1)} %convert_add_fusion), channel_id=1, source_target_pairs={{0,8},{1,9},{2,10},{3,11},{4,12},{5,13},{6,14},{7,15},{8,0},{9,1},... | collective-permute-start | bytes 1572872 | tf_op jit(solution)/shard_map/ppermute | solution.py:47
  (78 other events, 1424.2 us)

commit v3 on v2

v3 whole, which is shorter than its diff:
```python
import functools
import math

import jax
import jax.numpy as jnp
import numpy as np
from jax import lax
from jax.experimental import pallas as pl
from jax.experimental.pallas import tpu as pltpu
from jax.sharding import PartitionSpec as P

H = 16
BF = jnp.bfloat16
F32 = jnp.float32
AXES = ("rep", "shard")
gelu_coef = math.sqrt(2.0 / math.pi)
VMEM_LIMIT = 60 * 2**20


class Place:
    def __init__(self, reps, shards):
        self.reps, self.shards = reps, shards
        self.nx = max(n for n in (1, 2, 4, 8) if shards % n == 0 and n * n <= shards)
        self.nz = shards // self.nx
        rep, shard = lax.axis_index("rep"), lax.axis_index("shard")
        self.shard, self.waits = shard, [[]]
        table = [
            [r // 2, r % 2, v // self.nx, v % self.nx] for r in range(reps) for v in range(shards)
        ]
        row = lax.dynamic_slice_in_dim(jnp.asarray(np.array(table, np.int32)), rep * shards + shard, 1, 0)
        self.info = row[0]
        self.y, self.core, self.x = self.info[0], self.info[1], self.info[3]

    def _send(self, value, move):
        pairs = []
        for rep in range(self.reps):
            for shard in range(self.shards):
                y, core, z, x = move(rep // 2, rep % 2, shard // self.nx, shard % self.nx)
                pairs.append((rep * self.shards + shard, (y * 2 + core) * self.shards + z * self.nx + x))
        return lax.ppermute(value, AXES, pairs)

    def to_core(self, value):
        return self._send(value, lambda y, core, z, x: (y, 1 - core, z, x))

    def to_y(self, value):
        return self._send(value, lambda y, core, z, x: (1 - y, core, z, x))

    def to_z(self, value, k):
        return self._send(value, lambda y, core, z, x: (y, core, (z + k) % self.nz, x))

    def to_x(self, value, k):
        return self._send(value, lambda y, core, z, x: (y, core, z, (x + k) % self.nx))

    def swap_z(self, value):
        along = [[z * self.nx + x for z in range(self.nz)] for x in range(self.nx)]
        return lax.all_to_all(value, "shard", 0, 0, axis_index_groups=along, tiled=True)

    def gather(self, block, over_y=False):
        block = jnp.broadcast_to(block[None], (self.nz,) + block.shape)
        held = self.swap_z(after(block, self.waits.pop(0)))
        out = [held] + [self.to_x(held, kx) for kx in range(1, self.nx)]
        for i, values in enumerate(([held], out[1:])):
            self.hold(i, values)
        if over_y:
            out = out + [self.to_y(v) for v in out]
        return out

    def hold(self, steps, values):
        while len(self.waits) <= steps + 2:
            self.waits.append([])
        self.waits[steps] += values

    def sum_all(self, value):
        value = value + self.to_core(value)
        value = value + self.to_y(value)
        value = sum([self.to_x(value, k) for k in range(1, self.nx)], value)
        return sum([self.to_z(value, k) for k in range(1, self.nz)], value)


def after(value, waits):
    return lax.optimization_barrier((value, list(waits)))[0] if waits else value


def vmem():
    return pl.BlockSpec(memory_space=pltpu.VMEM)


def call(body, outs, ins, kinds, scratch=(), flops=0, name=None):
    spec = {
        "v": vmem(),
        "a": pl.BlockSpec(memory_space=pl.ANY),
        "s": pl.BlockSpec(memory_space=pltpu.SMEM),
    }
    moved = sum(v.size * v.dtype.itemsize for v in ins) + sum(math.prod(s) * jnp.dtype(t).itemsize for s, t in outs)
    return pl.pallas_call(
        body,
        out_shape=[jax.ShapeDtypeStruct(s, t) for s, t in outs],
        in_specs=[spec[k] for k in kinds],
        out_specs=[vmem() for _ in outs],
        scratch_shapes=list(scratch),
        compiler_params=pltpu.CompilerParams(vmem_limit_bytes=VMEM_LIMIT),
        cost_estimate=pl.CostEstimate(flops=10**12, bytes_accessed=10**9, transcendentals=0),
        name=name,
    )(*ins)


def dot(a, b):
    return jnp.dot(a, b, preferred_element_type=F32)


def dot_tn(a, b):
    return lax.dot_general(a, b, (((0,), (0,)), ((), ())), preferred_element_type=F32)


def dot_nt(a, b):
    return lax.dot_general(a, b, (((1,), (1,)), ((), ())), preferred_element_type=F32)


def layer_norm(values_in):
    centre = values_in - jnp.mean(values_in, axis=-1, keepdims=True)
    inv_std = lax.rsqrt(jnp.mean(centre * centre, axis=-1, keepdims=True) + 1e-05)
    return (centre * inv_std, inv_std)


def norm_back(grad_normed, normed, inv_std):
    return inv_std * (
        grad_normed
        - jnp.mean(grad_normed, axis=-1, keepdims=True)
        - normed * jnp.mean(grad_normed * normed, axis=-1, keepdims=True)
    )


def aligned(value, step):
    return pl.multiple_of(value, step) if step % 8 == 0 else value


class Load:
    def __init__(self, sem):
        self.sem, self.copies = sem, []

    def copy(self, source, target):
        self.copies.append(pltpu.make_async_copy(source, target, self.sem.at[len(self.copies)]))

    def start(self):
        for copy in self.copies:
            copy.start()

    def wait(self):
        for copy in self.copies:
            copy.wait()

    def blocks(self, info, held, rows, target, col, first=0, base=0):
        nx, nz, cols = len(held), held[0].shape[0], held[0].shape[2]
        for kx, ref in enumerate(held):
            x = lax.rem(info[3] - kx + nx, nx)
            for z in range(nz):
                at = aligned(base + (z * nx + x) * rows, rows)
                self.copy(ref.at[z, pl.ds(first, rows), :], target.at[pl.ds(at, rows), pl.ds(col, cols)])

    def qkv(self, info, pieces, rd, target):
        nx = len(pieces) // 2
        for i in range(2):
            self.blocks(info, pieces[i * nx : (i + 1) * nx], rd, target, i * pieces[0].shape[2])

    def dense(self, info, held, other, rd, target):
        nx, nz, cols = len(held), held[0].shape[0], held[0].shape[2]
        for kx, ref in enumerate(held):
            x = lax.rem(info[3] - kx + nx, nx)
            for j in range(nz // 2):
                rows = pl.ds(aligned((j * nx + x) * rd, rd), rd)
                for core, source in ((info[1], ref.at[info[1] * (nz // 2) + j]), (1 - info[1], other.at[kx, j])):
                    lanes = pl.ds(pl.multiple_of(core * cols, 128), cols)
                    self.copy(source, target.at[rows, lanes])

    def up(self, info, pieces, rd, target):
        nx = len(pieces) // 4
        for i in range(4):
            self.blocks(info, pieces[i * nx : (i + 1) * nx], rd, target, i * pieces[0].shape[2])

    def down(self, info, pieces, quarter, target):
        nx, half = len(pieces) // 3, target.shape[0] // 2
        self.blocks(info, pieces[:nx], quarter, target, 0)
        self.blocks(info, pieces[nx : 2 * nx], quarter, target, 0, base=half)
        for part in range(2):
            base = jnp.bitwise_xor(info[0], part) * half
            self.blocks(info, pieces[2 * nx :], quarter, target, pieces[0].shape[2], part * quarter, base)


def attention_kernel(n, rd, *refs):
    info, slopes, own, other, gain, bias, qv, *rest = refs
    pieces, (nin_ref, qkv_ref, ctx_ref, probs_ref, wq, sem) = rest[:n], rest[n:]
    load = Load(sem)
    load.qkv(info, pieces, rd, wq)
    load.start()
    rows, width = own.shape
    half = width // 2
    for i, ref in enumerate((own, other)):
        normed, _ = layer_norm(ref[...].astype(F32))
        nin_ref[i * rows : (i + 1) * rows, :] = (normed * gain[...] + bias[...]).astype(BF)
    load.wait()
    tile = 256

    @pl.loop(0, 3 * half // tile)
    def _(t):
        cols = pl.ds(pl.multiple_of(t * tile, tile), tile)
        qkv_ref[:, cols] = (dot(nin_ref[...], wq[:, cols]) + qv[:, cols]).astype(BF)

    hd = width // H
    lane = lax.broadcasted_iota(jnp.int32, (rows, 2 * hd), 1)
    first = lane < hd
    q_pos = lax.broadcasted_iota(jnp.int32, (rows, rows), 0)
    k_pos = lax.broadcasted_iota(jnp.int32, (rows, rows), 1)
    distance = (k_pos - q_pos).astype(F32)
    seen = k_pos <= q_pos
    pairs = half // (2 * hd)

    @pl.loop(0, 2 * pairs)
    def _(step):
        seq, pair = step // pairs, step % pairs
        at = pl.ds(pl.multiple_of(seq * rows, rows), rows)
        lanes = [pl.ds(pl.multiple_of(part * half + pair * 2 * hd, 2 * hd), 2 * hd) for part in range(3)]
        q, k, v = (qkv_ref[at, where] for where in lanes)
        out = []
        for i in range(2):
            mine = first if i == 0 else jnp.logical_not(first)
            scores = dot_nt(jnp.where(mine, q, jnp.zeros_like(q)), k) * hd ** (-0.5) + slopes[pair * 2 + i] * distance
            scores = jnp.where(seen, scores, -1e30)
            e = jnp.exp(scores - jnp.max(scores, axis=-1, keepdims=True))
            probs = (e * (1.0 / jnp.sum(e, axis=-1, keepdims=True))).astype(BF)
            probs_ref[step * 2 + i] = probs
            out.append(dot(probs, v))
        ctx_ref[at, lanes[0]] = jnp.where(first, out[0], out[1]).astype(BF)


def dense_kernel(n, rd, *refs):
    info, ctx, *rest = refs
    held, (other, out_ref, wd, sem) = rest[:n], rest[n:]
    load = Load(sem)
    load.dense(info, held, other, rd, wd)
    load.start()
    load.wait()
    out_ref[...] = dot(ctx[...], wd[...])


def middle_kernel(own, other, part, recv, dense_b, gain, bias, res_ref, mid_ref):
    rows = own.shape[0]
    for i, ref in enumerate((own, other)):
        here, there = slice(i * rows, (i + 1) * rows), slice((1 - i) * rows, (2 - i) * rows)
        residual = ref[...].astype(F32) + (part[here, :] + recv[there, :]) + dense_b[...]
        res_ref[here, :] = residual
        normed, _ = layer_norm(residual)
        mid_ref[here, :] = (normed * gain[...] + bias[...]).astype(BF)


def up_kernel(n, rd, *refs):
    info, mid, up_b, *rest = refs
    pieces, (act_ref, slope_ref, wu, sem) = rest[:n], rest[n:]
    load = Load(sem)
    load.up(info, pieces, rd, wu)
    load.start()
    cols = wu.shape[1] // 2
    load.wait()
    tile = 256

    @pl.loop(0, 2 * cols // tile)
    def _(t):
        at = pl.ds(pl.multiple_of(t * tile, tile), tile)
        u = dot(mid[...], wu[:, at]) + up_b[:, at]
        t_ = jnp.tanh(gelu_coef * (u + 0.044715 * u * u * u))
        act_ref[:, at] = (0.5 * u * (1.0 + t_)).astype(BF)
        slope_ref[:, at] = 0.5 * (1.0 + t_) + 0.5 * u * (1.0 - t_ * t_) * gelu_coef * (
            1.0 + 3.0 * 0.044715 * u * u
        )


def feed_back_kernel(n, rd, quarter, *refs):
    info, own, other, slope, *rest = refs
    up_pieces, down_pieces, (gp_ref, gb_ref, gmid_ref, wu, wo, sem, sem2) = rest[:n], rest[n : n + n // 4 * 3], rest[n + n // 4 * 3 :]
    load, load2 = Load(sem), Load(sem2)
    load.down(info, down_pieces, quarter, wo)
    load2.up(info, up_pieces, rd, wu)
    load.start()
    load2.start()
    load.wait()
    cols = wu.shape[1] // 2
    rows = own.shape[0]
    tile = 256

    @pl.loop(0, 2 * cols // tile)
    def _(t):
        at = pl.ds(pl.multiple_of(t * tile, tile), tile)
        total = jnp.zeros((1, tile), F32)
        for i, ref in enumerate((own, other)):
            here = slice(i * rows, (i + 1) * rows)
            grad_pre = dot_nt(ref[...], wo[at, :]) * slope[here, at]
            gp_ref[here, at] = grad_pre.astype(BF)
            total = total + jnp.sum(grad_pre, axis=0, keepdims=True)
        gb_ref[:, at] = total

    width = own.shape[1]
    load2.wait()

    @pl.loop(0, width // tile)
    def _(t):
        at = pl.ds(pl.multiple_of(t * tile, tile), tile)
        gmid_ref[:, at] = dot_nt(gp_ref[...], wu[at, :])


def output_kernel(n, quarter, *refs):
    info, act, *rest = refs
    pieces, (own_ref, other_ref, wo, sem) = rest[:n], rest[n:]
    load = Load(sem)
    load.down(info, pieces, quarter, wo)
    load.start()
    load.wait()
    rows, width = own_ref.shape
    tile = 256

    @pl.loop(0, width // tile)
    def _(t):
        at = pl.ds(pl.multiple_of(t * tile, tile), tile)
        both = dot(act[...], wo[:, at])
        own_ref[:, at] = both[:rows]
        other_ref[:, at] = both[rows:]


def grad_y_kernel(parts, by_y, info, left, *refs):
    right, outs = refs[: -2 * parts], refs[-2 * parts :]
    tokens = right[0].shape[0]
    nz, rows, cols = outs[0].shape
    for which in range(2):
        for p in range(parts):
            out = outs[2 * p + which]
            for z in range(nz):
                total = None
                for i, ref in enumerate(right):
                    here = slice(i * tokens, (i + 1) * tokens)
                    first, start = z * rows, p * cols
                    if by_y:
                        y = info[0] if which == 1 else 1 - info[0]
                        start = pl.multiple_of((y * parts + p) * cols, 128)
                    else:
                        first += (1 - which) * nz * rows
                    term = dot_tn(left[here, first : first + rows], ref[:, pl.ds(start, cols)])
                    total = term if total is None else total + term
                out[z] = total.astype(BF)


def at_x(info, kx, nx, per, value):
    x = lax.rem(info[3] + kx, nx)
    picked = value[:per]
    for v in range(1, nx):
        picked = jnp.where(x == v, value[v * per : (v + 1) * per], picked)
    return picked


def up_grad_kernel(nx, info, left, right, away, mine, *outs):
    nz, per, cols = outs[0].shape
    cols //= 2
    half = right.shape[1] // 2
    for z in range(nz):
        lhs = left[:, z * nx * per : (z + 1) * nx * per]
        for h in range(2):
            value = dot_tn(lhs, right[:, h * half : h * half + cols]).astype(BF)
            lanes = pl.ds(pl.multiple_of(jnp.bitwise_xor(info[0], h) * cols, 128), cols)
            for kx in range(nx):
                outs[kx][z, :, lanes] = at_x(info, kx, nx, per, value)
            out = away if h else mine
            out[z] = dot_tn(lhs, right[:, h * half + cols : (h + 1) * half]).astype(BF)


def fold_y_kernel(nx, info, mine, recv, *outs):
    per = outs[0].shape[1]
    for kx in range(nx):
        x = lax.rem(info[3] + kx, nx)
        at = pl.ds(aligned(x * per, per), per)
        outs[kx][...] = (mine[:, at, :].astype(F32) + recv[:, at, :].astype(F32)).astype(BF)


def dense_grad_kernel(info, left, right, keep, give):
    nz, rows, cols = keep.shape
    for z in range(nz):
        lhs = left[:, z * rows : (z + 1) * rows]
        for out, core in ((keep, info[1]), (give, 1 - info[1])):
            out[z] = dot_tn(lhs, right[:, pl.ds(pl.multiple_of(core * cols, 128), cols)]).astype(BF)


def dense_place_kernel(nx, info, mine, recv, *outs):
    nz, per = outs[0].shape[:2]
    for kx in range(nx):
        x = lax.rem(info[3] + kx, nx)
        at = pl.ds(aligned(x * per, per), per)
        outs[kx][pl.ds(info[1] * (nz // 2), nz // 2)] = mine[:, at, :]
        outs[kx][pl.ds((1 - info[1]) * (nz // 2), nz // 2)] = recv[:, at, :]


def total_kernel(*refs):
    out = refs[-1]
    at = 0
    for ref in refs[:-1]:
        cols = ref.shape[2]
        total = ref[0].astype(F32)
        for z in range(1, ref.shape[0]):
            total = total + ref[z].astype(F32)
        out[:, at : at + cols] = total.astype(BF)
        at += cols


def fold_x_kernel(nx, *refs):
    out = refs[-1]
    cols = refs[0].shape[2]
    for p in range(len(refs) // nx):
        total = refs[p * nx][...].astype(F32)
        for kx in range(1, nx):
            total = total + refs[p * nx + kx][...].astype(F32)
        out[:, :, p * cols : (p + 1) * cols] = total.astype(BF)


def attention_back_kernel(n, rd, *refs):
    info, part, recv, residual, own, other, gain, qkv, probs, *rest = refs
    held, outs = rest[:n], rest[n:]
    other_half, res_ref, resb_ref, sums_ref, dqkv_ref, qvb_ref, wd, gctx, sem = outs
    load = Load(sem)
    load.dense(info, held, other_half, rd, wd)
    load.start()
    rows, width = own.shape
    half = width // 2
    hd = width // H
    for i, ref in enumerate((own, other)):
        here, there = slice(i * rows, (i + 1) * rows), slice((1 - i) * rows, (2 - i) * rows)
        grad_mid = part[here, :] + recv[there, :]
        normed, inv_std = layer_norm(residual[here, :])
        grad_res = ref[...].astype(F32) + norm_back(grad_mid * gain[...], normed, inv_std)
        resb_ref[here, :] = grad_res.astype(BF)
        if i == 0:
            res_ref[...] = grad_res
            sums_ref[0:1, :] = jnp.sum(grad_mid * normed, axis=0, keepdims=True)
            sums_ref[1:2, :] = jnp.sum(grad_mid, axis=0, keepdims=True)
            sums_ref[2:3, :] = jnp.sum(grad_res, axis=0, keepdims=True)
    load.wait()
    gctx[...] = dot_nt(resb_ref[...], wd[...]).astype(BF)

    lane = lax.broadcasted_iota(jnp.int32, (rows, 2 * hd), 1)
    first = lane < hd
    pairs = half // (2 * hd)
    qvb_ref[...] = jnp.zeros_like(qvb_ref)

    @pl.loop(0, 2 * pairs)
    def _(step):
        seq, pair = step // pairs, step % pairs
        at = pl.ds(pl.multiple_of(seq * rows, rows), rows)
        lanes = [pl.ds(pl.multiple_of(p * half + pair * 2 * hd, 2 * hd), 2 * hd) for p in range(3)]
        q, k, v = (qkv[at, where] for where in lanes)
        g = gctx[at, lanes[0]]
        dq, dk, dv = 0.0, 0.0, 0.0
        for i in range(2):
            mine = first if i == 0 else jnp.logical_not(first)
            g_i = jnp.where(mine, g, jnp.zeros_like(g))
            prob = probs[step * 2 + i]
            prob_f = prob.astype(F32)
            grad_probs = dot_nt(g_i, v)
            delta = jnp.sum(prob_f * grad_probs, axis=-1, keepdims=True)
            grad_scores = (prob_f * (grad_probs - delta) * hd ** (-0.5)).astype(BF)
            dq = dq + dot(grad_scores, jnp.where(mine, k, jnp.zeros_like(k)))
            dk = dk + dot_tn(grad_scores, jnp.where(mine, q, jnp.zeros_like(q)))
            dv = dv + dot_tn(prob, g_i)
        for where, value in zip(lanes, (dq, dk, dv)):
            dqkv_ref[at, where] = value.astype(BF)
        for row, value in ((0, dq), (1, dv)):
            qvb_ref[row : row + 1, lanes[0]] = qvb_ref[row : row + 1, lanes[0]] + jnp.sum(value, axis=0, keepdims=True)


def normed_kernel(n, rd, *refs):
    info, dqkv, *rest = refs
    pieces, (own_ref, other_ref, wq, sem) = rest[:n], rest[n:]
    load = Load(sem)
    load.qkv(info, pieces, rd, wq)
    load.start()
    load.wait()
    rows, width = own_ref.shape
    tile = 256

    @pl.loop(0, width // tile)
    def _(t):
        at = pl.ds(pl.multiple_of(t * tile, tile), tile)
        both = dot_nt(dqkv[...], wq[at, :])
        own_ref[:, at] = both[:rows]
        other_ref[:, at] = both[rows:]


def input_kernel(own, recv, hidden, grad_res, gain, in_ref, sums_ref):
    grad_normed = own[...] + recv[...]
    normed, inv_std = layer_norm(hidden[...].astype(F32))
    sums_ref[0:1, :] = jnp.sum(grad_normed * normed, axis=0, keepdims=True)
    sums_ref[1:2, :] = jnp.sum(grad_normed, axis=0, keepdims=True)
    in_ref[...] = grad_res[...] + norm_back(grad_normed * gain[...], normed, inv_std)


def pick(pair_first, pair_second, index):
    flip = index == 1
    return jnp.where(flip, pair_second, pair_first), jnp.where(flip, pair_first, pair_second)


def on_device(
    reps,
    shards,
    hidden_in,
    cotangent,
    ln1_gain,
    ln1_bias,
    w_qkv,
    qv_bias,
    w_dense,
    dense_bias,
    ln2_gain,
    ln2_bias,
    w_up,
    up_bias,
    w_down,
    down_bias,
):
    at = Place(reps, shards)
    info, core, y = at.info, at.core, at.y
    nz, nx, n = at.nz, at.nx, shards
    rows, width = hidden_in.shape
    rd = w_qkv.shape[0]
    ff = w_up.shape[1]
    quarter = ff // shards // 4
    half = width // 2
    heads = H // 2
    hd = width // H
    fq = shards * quarter
    dma = pltpu.SemaphoreType.DMA
    slopes = jnp.asarray(2.0 ** (-8.0 * (np.arange(H) + 1.0) / H), F32)
    slopes = lax.dynamic_slice_in_dim(slopes, core * heads, heads)

    qkv_half = lax.dynamic_index_in_dim(w_qkv.reshape(rd, 3, 2, half), core, 2, keepdims=False)
    qkv_half = qkv_half.reshape(rd, 3 * half)
    cut = 3 * half // 2
    qkv_first = at.gather(qkv_half[:, :cut])
    hidden_other = at.to_core(hidden_in)

    vectors = (ln1_gain, ln1_bias, qv_bias, dense_bias, ln2_gain, ln2_bias, up_bias, down_bias)
    packed = jnp.concatenate(vectors)
    size = packed.shape[0]
    packed = jnp.pad(packed, (0, 16 * cut - size)).reshape(16, cut)
    qkv_second = at.gather(jnp.concatenate([qkv_half[:, cut:], packed]))
    qkv_pieces = qkv_first + qkv_second
    lines = -(-size // cut)
    held = jnp.stack([v[:, rd : rd + lines].reshape(nz, -1)[:, :size] for v in qkv_second])
    held = jnp.stack([lax.dynamic_index_in_dim(held, (at.x - x) % nx, 0, keepdims=False) for x in range(nx)], axis=1)
    packed = held.reshape(n, size).astype(F32)
    whole, start = [], 0
    for v in vectors:
        whole.append(packed[:, start : start + v.shape[0]].reshape(1, -1))
        start += v.shape[0]
    gain1, bias1, qv_b, dense_b, gain2, bias2, up_b, down_b = whole
    qv_half = lax.dynamic_index_in_dim(qv_b.reshape(2, 2, half), core, 1, keepdims=False)
    qkv_bias = jnp.concatenate([qv_half[:1], jnp.zeros((1, half), F32), qv_half[1:]], axis=1)
    up_b4 = lax.dynamic_index_in_dim(up_b.reshape(n, 2, 2, quarter), core, 1, keepdims=False)
    up_halves = jnp.concatenate(pick(up_b4[:, 0].reshape(1, -1), up_b4[:, 1].reshape(1, -1), y), axis=1)

    up_quarter = w_up.reshape(rd, n, 4, quarter)
    up_quarter = lax.dynamic_index_in_dim(up_quarter, core * 2 + y, 2, keepdims=False).reshape(rd, fq)
    up_first = at.gather(up_quarter[:, : fq // 2], True)
    dense_held = at.gather(lax.dynamic_slice_in_dim(w_dense, core * half, half, 1))
    give = jnp.stack([lax.dynamic_slice_in_dim(v, (1 - core) * (nz // 2), nz // 2, 0) for v in dense_held])
    dense_in = dense_held + [at.to_core(give)]
    up_second = at.gather(up_quarter[:, fq // 2 :], True)
    split = width * 5 // 8
    down_half = lax.dynamic_slice_in_dim(w_down, core * 2 * quarter, 2 * quarter, 0)
    down_quarter = lax.dynamic_slice_in_dim(down_half, y * quarter, quarter, 0)
    down_pieces = at.gather(down_quarter[:, :split], True)
    up_pieces = [v for i in range(2) for p in (up_first, up_second) for v in p[i * nx : (i + 1) * nx]]
    down_pieces = down_pieces + at.gather(down_half[:, split:])
    cot_other = at.to_core(cotangent)

    mac = 2 * 2 * rows * width
    nin, qkv, ctx, probs = call(
        functools.partial(attention_kernel, 2 * nx, rd),
        [((2 * rows, width), BF), ((2 * rows, 3 * half), BF), ((2 * rows, half), BF), ((2 * heads, rows, rows), BF)],
        [info, slopes, after(hidden_in, up_first[:1]), hidden_other, gain1, bias1, qkv_bias] + qkv_pieces,
        "ss" + "v" * 5 + "a" * 2 * nx,
        [pltpu.VMEM((width, 3 * half), BF), dma((2 * n,))],
        mac * 4 * half,
        "attn",
    )
    (part,) = call(
        functools.partial(dense_kernel, nx, rd),
        [((2 * rows, width), F32)],
        [info, after(ctx, up_second[:1])] + dense_in,
        "sv" + "a" * (nx + 1),
        [pltpu.VMEM((half, width), BF), dma((n,))],
        mac * half,
        "dense",
    )
    residual, mid = call(
        middle_kernel,
        [((2 * rows, width), F32), ((2 * rows, width), BF)],
        [after(hidden_in, up_second[1:nx] + down_pieces[:1]), hidden_other, part, at.to_core(part), dense_b, gain2, bias2],
        "v" * 7,
        name="middle",
    )
    act, slope = call(
        functools.partial(up_kernel, 4 * nx, rd),
        [((2 * rows, 2 * fq), BF), ((2 * rows, 2 * fq), F32)],
        [info, mid, up_halves] + up_pieces,
        "svv" + "a" * 4 * nx,
        [pltpu.VMEM((width, 2 * fq), BF), dma((4 * n,))],
        mac * 2 * fq,
        "up",
    )

    def scatter_y(left, right, per, cols, by_y, name):
        cols //= 2
        terms = call(
            functools.partial(grad_y_kernel, 2, by_y),
            [((nz, nx * per, cols), BF)] * 4,
            [info, left] + right,
            "sv" + "v" * len(right),
            name=name,
        )
        return [(terms[2 * p + 1], at.to_y(terms[2 * p])) for p in range(2)]

    def fold_y(terms, name):
        nz_, rows_, cols = terms[0].shape
        out = call(
            functools.partial(fold_y_kernel, nx),
            [((nz, rows_ // nx, cols), BF)] * nx,
            [info] + list(terms),
            "svv",
            name=name + "_y",
        )
        return over_x(out)

    def over_x(parts):
        return [parts[0]] + [at.to_x(parts[kx], kx) for kx in range(1, nx)]

    def fold_x(ins, name):
        nz_, per, cols = ins[0].shape
        outs = [((nz, per, cols * len(ins) // nx), BF)]
        return call(functools.partial(fold_x_kernel, nx), outs, ins, "v" * len(ins), name=name + "_x")[0]

    def finish_z(ends, name):
        _, per, cols = ends[0].shape
        total = sum(v.shape[2] for v in ends)
        return call(total_kernel, [((per, total), BF)], ends, "v" * len(ends), name=name + "_z")[0]

    down_terms = scatter_y(act, [cotangent, cot_other], quarter, width, False, "gdown")

    gpre, gpre_sums, gmid = call(
        functools.partial(feed_back_kernel, 4 * nx, rd, quarter),
        [((2 * rows, 2 * fq), BF), ((1, 2 * fq), F32), ((2 * rows, width), F32)],
        [info, cotangent, cot_other, slope] + up_pieces + down_pieces,
        "svvv" + "a" * 7 * nx,
        [pltpu.VMEM((width, 2 * fq), BF), pltpu.VMEM((2 * fq, width), BF), dma((4 * n,)), dma((4 * n,))],
        mac * 4 * fq,
        "feed_back",
    )
    gmid_recv = at.to_core(gmid)
    up_terms = call(
        functools.partial(up_grad_kernel, nx),
        [((nz, nx * rd, fq // 2), BF)] * 2 + [((nz, rd, fq), BF)] * nx,
        [info, mid, gpre],
        "svv",
        name="gup",
    )
    up_first_x = over_x(up_terms[2:])
    up_second_y = (up_terms[1], at.to_y(up_terms[0]))

    grad_res, grad_res_b, sums2, dqkv, qv_sums = call(
        functools.partial(attention_back_kernel, nx, rd),
        [
            ((rows, width), F32),
            ((2 * rows, width), BF),
            ((3, width), F32),
            ((2 * rows, 3 * half), BF),
            ((2, half), F32),
        ],
        [info, gmid, gmid_recv, residual, cotangent, cot_other, gain2, qkv, probs] + dense_in,
        "s" + "v" * 8 + "a" * (nx + 1),
        [pltpu.VMEM((half, width), BF), pltpu.VMEM((2 * rows, half), BF), dma((n,))],
        mac * 3 * half,
        "attn_back",
    )
    qkv_terms = scatter_y(nin, [dqkv], rd, cut, True, "gqkv")
    last = [qkv_terms[0][0]]

    def order(value):
        last[:] = [value[0] if isinstance(value, (list, tuple)) else value]
        return value

    up_sum = order(fold_x(after(up_first_x, last), "gup"))
    end_up = at.swap_z(up_sum)
    down_x = order(fold_y(after(down_terms[0], last), "gdown"))
    down_x = down_x + order(fold_y(after(down_terms[1], last), "gdown"))

    keep, give = call(
        dense_grad_kernel,
        [((nz // 2, nx * rd, half), BF)] * 2,
        [info, after(ctx, last), grad_res_b],
        "svv",
        name="gdense",
    )
    order(keep)
    up2_x = order(fold_y(after(up_second_y, last), "gup2"))
    parts = call(
        functools.partial(dense_place_kernel, nx),
        [((nz, rd, half), BF)] * nx,
        [info, after(keep, last), at.to_core(give)],
        "svv",
        name="gdense_c",
    )
    order(parts)
    dense_x = over_x(parts)
    down_sum = order(fold_x(after(down_x, last), "gdown"))
    end_down = at.swap_z(after(down_sum, [end_up]))
    order(end_up)
    qkv_x = order(fold_y(after(qkv_terms[0], last), "gqkv"))
    qkv_x = qkv_x + order(fold_y(after(qkv_terms[1], last), "gqkv"))
    up2_sum = order(fold_x(after(up2_x, last), "gup2"))
    end_up2 = at.swap_z(after(up2_sum, [end_down]))
    out_own, out_other = order(
        call(
            functools.partial(output_kernel, 3 * nx, quarter),
            [((rows, width), F32), ((rows, width), F32)],
            [info, after(act, last)] + down_pieces,
            "sv" + "a" * 3 * nx,
            [pltpu.VMEM((2 * fq, width), BF), dma((4 * n,))],
            name="output",
        )
    )
    order(end_down)
    dense_sum = order(fold_x(after(dense_x, last), "gdense"))
    end_dense = at.swap_z(after(dense_sum, [end_up2]))
    qkv_sum = order(fold_x(after(qkv_x, last), "gqkv"))
    end_qkv = at.swap_z(after(qkv_sum, [end_dense]))
    order(end_up2)
    norm_own, norm_other = order(
        call(
            functools.partial(normed_kernel, 2 * nx, rd),
            [((rows, width), F32), ((rows, width), F32)],
            [info, after(dqkv, last)] + qkv_pieces,
            "sv" + "a" * 2 * nx,
            [pltpu.VMEM((width, 3 * half), BF), dma((2 * n,))],
            name="gnorm",
        )
    )
    down_own = order(finish_z([after(end_down, last)], "gdown"))
    down_other = at.to_y(down_own)
    order(end_dense)
    up_part = order(finish_z(after([end_up, end_up2], last), "gup"))
    up_recv = at.to_y(up_part)
    dense_part = finish_z([end_dense], "gdense")
    qkv_own = finish_z([end_qkv], "gqkv")
    qkv_other = at.to_y(qkv_own)
    dense_mine = dense_part.astype(F32) + at.to_y(dense_part).astype(F32)
    grad_dense = jnp.concatenate(pick(dense_mine, at.to_core(dense_mine), core), axis=1)

    output = (residual[:rows] + (out_own + at.to_core(out_other)) + down_b).astype(BF)

    input_grad, sums1 = call(
        input_kernel,
        [((rows, width), F32), ((2, width), F32)],
        [norm_own, at.to_core(norm_other), hidden_in, grad_res, gain1],
        "v" * 5,
        name="input_grad",
    )

    down_y = jnp.concatenate(pick(down_own, down_other, y), axis=0)
    grad_down = jnp.concatenate(pick(down_y, at.to_core(down_y), core), axis=0).astype(F32)
    up_total = up_part[:, :fq].astype(F32) + up_recv[:, :fq].astype(F32)
    up_both = [v.astype(F32) for v in pick(up_part[:, fq:], up_recv[:, fq:], y)]
    up_c = jnp.concatenate([up_total] + up_both, axis=1)
    up_c = up_c.reshape(rd, 2, 2, n // 2, quarter).transpose(0, 1, 3, 2, 4).reshape(rd, n, 1, 2 * quarter)
    grad_up = jnp.concatenate(pick(up_c, at.to_core(up_c), core), axis=2).reshape(rd, ff)
    qkv_c = jnp.concatenate(pick(qkv_own, qkv_other, y), axis=1).reshape(rd, 3, 1, half)
    grad_qkv = jnp.concatenate(pick(qkv_c, at.to_core(qkv_c), core), axis=2).reshape(rd, 3 * width).astype(F32)

    grad_down_bias = jnp.sum(cotangent.astype(F32), axis=0)
    up_y = jnp.stack([g.reshape(n, quarter) for g in pick(gpre_sums[0, :fq], gpre_sums[0, fq:], y)], axis=1)
    on_core = jnp.arange(2) == core
    up_bias_all = jnp.where(on_core[None, :, None, None], up_y[:, None], 0.0).reshape(-1)
    qv_all = jnp.where(on_core[None, :, None], qv_sums[:, None], 0.0).reshape(-1)
    feed = jnp.concatenate([sums2.reshape(-1), grad_down_bias, up_bias_all, sums1.reshape(-1), qv_all])
    feed = at.sum_all(feed[None, :])[0]

    def own(start, size):
        per = size // n
        return lax.dynamic_slice_in_dim(feed, start + at.shard * per, per)

    return (
        output,
        input_grad,
        own(4 * width + ff, width),
        own(5 * width + ff, width),
        grad_qkv,
        own(6 * width + ff, 2 * width),
        grad_dense,
        own(2 * width, width),
        own(0, width),
        own(width, width),
        grad_up,
        own(4 * width, ff),
        grad_down,
        own(3 * width, width),
    )


def solution(mesh):
    both, rows, vector = P(("rep", "shard"), None), P("shard", None), P("shard")
    weights = (vector, vector, rows, vector, rows, vector, vector, vector, rows, vector, rows, vector)
    return jax.shard_map(
        functools.partial(on_device, mesh.shape["rep"], mesh.shape["shard"]),
        mesh=mesh,
        in_specs=(both, both) + weights,
        out_specs=(both, both) + weights,
        check_vma=False,
    )
```

time: 497 us -> 462 us (0.930)
  waiting for transfers between devices: 185 us -> 156 us
  starting transfers between devices: 121 us -> 104 us
  other arithmetic: 11.6 us -> 21.3 us
    ppermute x83 -> x47, waiting for transfers between devices: 185 us -> 88.4 us  [_send(): return lax.ppermute(value, AXES, pairs)]
    ppermute x83 -> x47, starting transfers between devices: 121 us -> 52.1 us  [_send(): return lax.ppermute(value, AXES, pairs)]
    all_to_all x0 -> x12, waiting for transfers between devices: none -> 67.6 us  [swap_z(): lax.all_to_all(value, 'shard', 0, 0, axis_index_groups=along, tiled=True)]
    all_to_all x0 -> x12, starting transfers between devices: none -> 51.9 us  [swap_z(): lax.all_to_all(value, 'shard', 0, 0, axis_index_groups=along, tiled=True)]
    unnamed x103 -> x95, local copies, waits for them, and re-layouts: 19.1 us -> 9.41 us
    broadcast_in_dim x1 -> x7, local copies, waits for them, and re-layouts: 0.04 us -> 6.33 us  [gather(): block = jnp.broadcast_to(block[None], (self.nz,) + block.shape)]
  transfers between devices with their start and end apart: 83 -> 59, of which waited for: 27 -> 23; matrix products, arithmetic and copies ran while one was open for 6% -> 9% of each run, Pallas kernels for 23% -> 27%
where the time goes in v3:
time: 462 us; the launch traced here: 460 us
  waiting for transfers between devices  156 us (34%)
  Pallas kernels  139 us (30%)
  starting transfers between devices  104 us (23%)
  local copies, waits for them, and re-layouts  27.7 us (6%)
  other arithmetic  21.3 us (5%)
  between operations  12 us (3%)
    pallas_call x28, Pallas kernels, call(): pl.pallas_call(body, out_shape=[jax.ShapeDtypeStruct(s, t) for s, t in ou...  139 us
    ppermute x47, waiting for transfers between devices, _send(): return lax.ppermute(value, AXES, pairs)  88.4 us
    all_to_all x12, waiting for transfers between devices, swap_z(): lax.all_to_all(value, 'shard', 0, 0, axis_index_groups=along, tiled=True)  67.6 us
    ppermute x47, starting transfers between devices, _send(): return lax.ppermute(value, AXES, pairs)  52.1 us
    all_to_all x12, starting transfers between devices, swap_z(): lax.all_to_all(value, 'shard', 0, 0, axis_index_groups=along, tiled=True)  51.9 us
    unnamed x95, local copies, waits for them, and re-layouts  9.41 us
  transfers between devices with their start and end apart: 59, of which 23 were waited for; matrix products, arithmetic and copies ran while one was open for 9% of the time, Pallas kernels for 27%

profile of v3, /device:TPU:1, one launch (start us, length us, event | category | flops | bytes accessed | tf_op | source)
XLA Modules:
  0.0 459.9 jit_solution(12596907965550817391)
XLA Ops:
  7.2 5.4 %all-to-all-start = ((bf16[4,128,768]{2,1,0:T(8,128)(2,1)}), bf16[4,128,768]{2,1,0:T(8,128)(2,1)}, u32[]{:S(2)}, u32[]{:S(2)}) async-start(bf16[4,128,768]{2,1,0:T(8,128)(2,1)} %broadcast_in_dim.53), calls=%async_computation | async-start | bytes 1572864 | tf_op jit(solution)/shard_map/all_to_all | solution.py:56
  14.9 17.5 %all-to-all-done.refs_7_.refs_2_ = bf16[4,128,768]{2,1,0:T(8,128)(2,1)} async-done(((bf16[4,128,768]{2,1,0:T(8,128)(2,1)}), bf16[4,128,768]{2,1,0:T(8,128)(2,1)}, u32[]{:S(2)}, u32[]{:S(2)}) %all-to-all-start) | async-done | bytes 786464 | tf_op jit(solution)/shard_map/all_to_all | solution.py:56
  33.3 3.5 all-to-all-start.1
  40.2 18.3 %all-to-all-done.1.refs_9_.refs_4_ = bf16[4,144,768]{2,1,0:T(8,128)(2,1)S(1)} async-done(((bf16[4,144,768]{2,1,0:T(8,128)(2,1)}), bf16[4,144,768]{2,1,0:T(8,128)(2,1)S(1)}, u32[]{:S(2)}, u32[]{:S(2)}) %all-to-all-start.1) | async-done | bytes 884768 | tf_op jit(solution)/shard_map/all_to_all | solution.py:56
  60.7 4.1 all-to-all-start.2
  72.1 6.8 %all-to-all-done.2.refs_3_.refs_4_ = bf16[4,128,512]{2,1,0:T(8,128)(2,1)} async-done(((bf16[4,128,512]{2,1,0:T(8,128)(2,1)}), bf16[4,128,512]{2,1,0:T(8,128)(2,1)}, u32[]{:S(2)}, u32[]{:S(2)}) %all-to-all-start.2) | async-done | bytes 524320 | tf_op jit(solution)/shard_map/all_to_all | solution.py:56
  80.1 3.5 all-to-all-start.3
  83.8 13.7 %all-to-all-done.3.refs_2_.refs_9_ = bf16[4,128,512]{2,1,0:T(8,128)(2,1)S(1)} async-done(((bf16[4,128,512]{2,1,0:T(8,128)(2,1)}), bf16[4,128,512]{2,1,0:T(8,128)(2,1)S(1)}, u32[]{:S(2)}, u32[]{:S(2)}) %all-to-all-start.3) | async-done | bytes 524320 | tf_op jit(solution)/shard_map/all_to_all | solution.py:56
  100.8 4.1 all-to-all-start.4
  105.0 4.5 collective-permute-done.4.refs_3_.refs_10_
  112.8 14.9 %attn.1 = (bf16[512,1024]{1,0:T(8,128)(2,1)}, bf16[512,1536]{1,0:T(8,128)(2,1)}, bf16[512,512]{1,0:T(8,128)(2,1)}, bf16[16,256,256]{2,1,0:T(8,128)(2,1)}) custom-call(s32[4]{0:T(128)} %get-tuple-element.245.refs_0_.info, f32[8]{0:T(128)} %dynamic_slice.93.refs_1_, bf16[256,1024]{1,0:T(8,128)(2,1)} %hidden.1, ...), custom_call_target="tpu_custom_call" | custom-call | flops 999999995904 | bytes 1000000000 | tf_op jit(solution)/shard_map/attn/pallas_call | solution.py:95
  127.7 4.4 dense.1.part
  135.4 4.2 all-to-all-start.5
  149.3 9.7 %collective-permute-done.3.refs_6_.refs_7_ = bf16[4,128,512]{2,1,0:T(8,128)(2,1)} collective-permute-done((bf16[4,128,512]{2,1,0:T(8,128)(2,1)}, bf16[4,128,512]{2,1,0:T(8,128)(2,1)}, u32[]{:S(2)}, u32[]{:S(2)}) %collective-permute-start.3) | collective-permute-done | bytes 524320 | tf_op jit(solution)/shard_map/ppermute | solution.py:40
  160.2 4.4 all-to-all-start.6
  165.9 4.6 middle.1
  174.3 4.5 collective-permute-done.13.refs_13_.refs_3_
  180.5 3.5 all-to-all-done.6.refs_16_.refs_6_
  185.3 6.5 %collective-permute-done.11.refs_10_.refs_11_ = bf16[4,128,512]{2,1,0:T(8,128)(2,1)} collective-permute-done((bf16[4,128,512]{2,1,0:T(8,128)(2,1)}, bf16[4,128,512]{2,1,0:T(8,128)(2,1)}, u32[]{:S(2)}, u32[]{:S(2)}) %collective-permute-start.11) | collective-permute-done | bytes 524320 | tf_op jit(solution)/shard_map/ppermute | solution.py:40
  191.8 12.0 %up.1 = (bf16[512,2048]{1,0:T(8,128)(2,1)}, f32[512,2048]{1,0:T(8,128)}) custom-call(s32[4]{0:T(128)} %get-tuple-element.245.refs_0_.info, bf16[512,1024]{1,0:T(8,128)(2,1)} %get-tuple-element.116.refs_1_.left, f32[1,2048]{1,0:T(1,128)} %pad_maximum_fusion.7.refs_2_, bf16[4,128,512]{2,1,0:T(8,128)(2,1)} %all-to-all-done.2.refs_3_.refs_4_, ...), custom_call_target="tpu_custom_call" | custom-call | flops 999999995904 | bytes 1000000000 | tf_op jit(solution)/shard_map/up/pallas_call | solution.py:95
  203.8 5.4 %gdown.1 = (bf16[4,256,512]{2,1,0:T(8,128)(2,1)}, bf16[4,256,512]{2,1,0:T(8,128)(2,1)}, bf16[4,256,512]{2,1,0:T(8,128)(2,1)}, bf16[4,256,512]{2,1,0:T(8,128)(2,1)}) custom-call(s32[4]{0:T(128)} %get-tuple-element.245.refs_0_.info, bf16[512,2048]{1,0:T(8,128)(2,1)} %get-tuple-element.161.left.refs_1_, bf16[256,1024]{1,0:T(8,128)(2,1)} %refs_4_.1, ...), custom_call_target="tpu_custom_call" | custom-call | flops 999999995904 | bytes 1000000000 | tf_op jit(solution)/shard_map/gdown/pallas_call | solution.py:95
  210.7 9.2 %collective-permute-done.15.refs_15_.refs_5_ = bf16[4,128,640]{2,1,0:T(8,128)(2,1)} collective-permute-done((bf16[4,128,640]{2,1,0:T(8,128)(2,1)}, bf16[4,128,640]{2,1,0:T(8,128)(2,1)}, u32[]{:S(2)}, u32[]{:S(2)}) %collective-permute-start.15) | collective-permute-done | bytes 655392 | tf_op jit(solution)/shard_map/ppermute | solution.py:40
  219.9 14.9 %feed_back.1 = (bf16[512,2048]{1,0:T(8,128)(2,1)}, f32[1,2048]{1,0:T(1,128)}, f32[512,1024]{1,0:T(8,128)}) custom-call(s32[4]{0:T(128)} %get-tuple-element.245.refs_0_.info, bf16[256,1024]{1,0:T(8,128)(2,1)} %refs_4_.1, bf16[256,1024]{1,0:T(8,128)(2,1)} %collective-permute-done.12.refs_2_.refs_1_.refs_5_, f32[512,2048]{1,0:T(8,128)} %get-tuple-element.118.refs_3_, ...), custom_call_target="tpu_custom_call" | custom-call | flops 999999995904 | bytes 1000000000 | tf_op jit(solution)/shard_map/feed_back/pallas_call | solution.py:95
  237.2 6.0 %gup.1 = (bf16[4,256,512]{2,1,0:T(8,128)(2,1)}, bf16[4,256,512]{2,1,0:T(8,128)(2,1)}, bf16[4,128,1024]{2,1,0:T(8,128)(2,1)}, bf16[4,128,1024]{2,1,0:T(8,128)(2,1)}) custom-call(s32[4]{0:T(128)} %get-tuple-element.245.refs_0_.info, bf16[512,1024]{1,0:T(8,128)(2,1)} %get-tuple-element.116.refs_1_.left, bf16[512,2048]{1,0:T(8,128)(2,1)} %get-tuple-element.120.right), custom_call_target="tpu_custom_call" | custom-call | flops 999999995904 | bytes 1000000000 | tf_op jit(solution)/shard_map/gup/pallas_call | solution.py:95
  245.6 13.3 %attn_back.1 = (f32[256,1024]{1,0:T(8,128)}, bf16[512,1024]{1,0:T(8,128)(2,1)}, f32[3,1024]{1,0:T(4,128)}, bf16[512,1536]{1,0:T(8,128)(2,1)}, f32[2,512]{1,0:T(2,128)}) custom-call(s32[4]{0:T(128)} %get-tuple-element.245.refs_0_.info, f32[512,1024]{1,0:T(8,128)} %get-tuple-element.130.refs_1_, f32[512,1024]{1,0:T(8,128)} %collective-permute-done.21.refs_2_, ...), custom_call_target="tpu_custom_call" | custom-call | flops 999999995904 | bytes 1000000000 | tf_op jit(solution)/shard_map/attn_back/pallas_call | solution.py:95
  258.9 5.3 %gqkv.1 = (bf16[4,256,384]{2,1,0:T(8,128)(2,1)}, bf16[4,256,384]{2,1,0:T(8,128)(2,1)}, bf16[4,256,384]{2,1,0:T(8,128)(2,1)}, bf16[4,256,384]{2,1,0:T(8,128)(2,1)}) custom-call(s32[4]{0:T(128)} %get-tuple-element.245.refs_0_.info, bf16[512,1024]{1,0:T(8,128)(2,1)} %get-tuple-element.129.left, bf16[512,1536]{1,0:T(8,128)(2,1)} %get-tuple-element.175.refs_0_.refs_1_), custom_call_target="tpu_custom_call" | custom-call | flops 999999995904 | bytes 1000000000 | tf_op jit(solution)/shard_map/gqkv/pallas_call | solution.py:95
  264.2 4.0 collective-permute-done.20.refs_1_
  268.3 2.7 gup_x.1
  271.0 4.8 %all-to-all-start.7 = ((bf16[4,128,1024]{2,1,0:T(8,128)(2,1)}), bf16[4,128,1024]{2,1,0:T(8,128)(2,1)}, u32[]{:S(2)}, u32[]{:S(2)}) async-start(bf16[4,128,1024]{2,1,0:T(8,128)(2,1)} %gup_x.1), calls=%async_computation.7 | async-start | bytes 2097152 | tf_op jit(solution)/shard_map/all_to_all | solution.py:56
  275.8 2.7 gdown_y.2
  278.6 2.7 gdown_y.3
  281.3 3.0 gdense.1
  284.3 3.0 collective-permute-done.17.recv
  297.7 7.4 %collective-permute-done.27.refs_3_ = bf16[4,128,512]{2,1,0:T(8,128)(2,1)} collective-permute-done((bf16[4,128,512]{2,1,0:T(8,128)(2,1)}, bf16[4,128,512]{2,1,0:T(8,128)(2,1)}, u32[]{:S(2)}, u32[]{:S(2)}) %collective-permute-start.27) | collective-permute-done | bytes 524320 | tf_op jit(solution)/shard_map/ppermute | solution.py:40
  305.2 11.2 %collective-permute-done.26.refs_1_ = bf16[4,128,512]{2,1,0:T(8,128)(2,1)} collective-permute-done((bf16[4,128,512]{2,1,0:T(8,128)(2,1)}, bf16[4,128,512]{2,1,0:T(8,128)(2,1)}, u32[]{:S(2)}, u32[]{:S(2)}) %collective-permute-start.26) | collective-permute-done | bytes 524320 | tf_op jit(solution)/shard_map/ppermute | solution.py:40
  316.4 2.7 gdown_x.1
  319.2 4.5 all-to-all-start.8
  333.0 8.5 %output.1 = (f32[256,1024]{1,0:T(8,128)}, f32[256,1024]{1,0:T(8,128)}) custom-call(s32[4]{0:T(128)} %get-tuple-element.245.refs_0_.info, bf16[512,2048]{1,0:T(8,128)(2,1)} %get-tuple-element.161.left.refs_1_, bf16[4,128,640]{2,1,0:T(8,128)(2,1)} %all-to-all-done.5.refs_12_.refs_2_, bf16[4,128,640]{2,1,0:T(8,128)(2,1)} %collective-permute-done.13.refs_13_.refs_3_, ...), custom_call_target="tpu_custom_call" | custom-call | flops 999999995904 | bytes 1000000000 | tf_op jit(solution)/shard_map/output/pallas_call | solution.py:95
  349.0 4.5 all-to-all-start.9
  353.5 4.2 collective-permute-done.38.refs_1_
  359.8 6.3 %collective-permute-done.37.refs_3_ = bf16[4,128,384]{2,1,0:T(8,128)(2,1)} collective-permute-done((bf16[4,128,384]{2,1,0:T(8,128)(2,1)}, bf16[4,128,384]{2,1,0:T(8,128)(2,1)}, u32[]{:S(2)}, u32[]{:S(2)}) %collective-permute-start.37) | collective-permute-done | bytes 393248 | tf_op jit(solution)/shard_map/ppermute | solution.py:40
  366.2 8.4 %collective-permute-done.36.refs_1_ = bf16[4,128,384]{2,1,0:T(8,128)(2,1)} collective-permute-done((bf16[4,128,384]{2,1,0:T(8,128)(2,1)}, bf16[4,128,384]{2,1,0:T(8,128)(2,1)}, u32[]{:S(2)}, u32[]{:S(2)}) %collective-permute-start.36) | collective-permute-done | bytes 393248 | tf_op jit(solution)/shard_map/ppermute | solution.py:40
  374.6 7.2 %gnorm.1 = (f32[256,1024]{1,0:T(8,128)}, f32[256,1024]{1,0:T(8,128)}) custom-call(s32[4]{0:T(128)} %get-tuple-element.245.refs_0_.info, bf16[512,1536]{1,0:T(8,128)(2,1)} %get-tuple-element.175.refs_0_.refs_1_, bf16[4,128,768]{2,1,0:T(8,128)(2,1)} %all-to-all-done.refs_7_.refs_2_, bf16[4,128,768]{2,1,0:T(8,128)(2,1)} %collective-permute-done.refs_8_.refs_3_, ...), custom_call_target="tpu_custom_call" | custom-call | flops 999999995904 | bytes 1000000000 | tf_op jit(solution)/shard_map/gnorm/pallas_call | solution.py:95
  385.1 4.5 all-to-all-start.10
  395.9 7.7 %all-to-all-done.10.refs_0_ = bf16[4,128,512]{2,1,0:T(8,128)(2,1)} async-done(((bf16[4,128,512]{2,1,0:T(8,128)(2,1)}), bf16[4,128,512]{2,1,0:T(8,128)(2,1)}, u32[]{:S(2)}, u32[]{:S(2)}) %all-to-all-start.10) | async-done | bytes 524320 | tf_op jit(solution)/shard_map/all_to_all | solution.py:56
  409.2 4.5 all-to-all-start.11
  416.0 3.9 input_grad.1
  447.9 2.8 collective-permute-done.39
  (282 shorter events, 132.1 us)
Async XLA Ops:
  7.2 25.1 %all-to-all-start = ((bf16[4,128,768]{2,1,0:T(8,128)(2,1)}), bf16[4,128,768]{2,1,0:T(8,128)(2,1)}, u32[]{:S(2)}, u32[]{:S(2)}) async-start(bf16[4,128,768]{2,1,0:T(8,128)(2,1)} %broadcast_in_dim.53), calls=%async_computation | async-start | bytes 1572864 | tf_op jit(solution)/shard_map/all_to_all | solution.py:56
  33.3 25.2 %all-to-all-start.1 = ((bf16[4,144,768]{2,1,0:T(8,128)(2,1)}), bf16[4,144,768]{2,1,0:T(8,128)(2,1)S(1)}, u32[]{:S(2)}, u32[]{:S(2)}) async-start(bf16[4,144,768]{2,1,0:T(8,128)(2,1)} %broadcast_in_dim.61), calls=%async_computation.1 | async-start | bytes 1769472 | tf_op jit(solution)/shard_map/all_to_all | solution.py:56
  36.8 23.0 %collective-permute-start = (bf16[4,128,768]{2,1,0:T(8,128)(2,1)}, bf16[4,128,768]{2,1,0:T(8,128)(2,1)}, u32[]{:S(2)}, u32[]{:S(2)}) collective-permute-start(bf16[4,128,768]{2,1,0:T(8,128)(2,1)} %all-to-all-done.refs_7_.refs_2_), channel_id=1, source_target_pairs={{0,1},{1,0},{2,3},{3,2},{4,5},{5,4},{6,7},{7,6},{8,9},{9,8},{10,11... | collective-permute-start | bytes 2359304 | tf_op jit(solution)/shard_map/ppermute | solution.py:40
  58.5 20.6 %collective-permute-start.2 = (bf16[4,144,768]{2,1,0:T(8,128)(2,1)S(1)}, bf16[4,144,768]{2,1,0:T(8,128)(2,1)S(1)}, u32[]{:S(2)}, u32[]{:S(2)}) collective-permute-start(bf16[4,144,768]{2,1,0:T(8,128)(2,1)S(1)} %all-to-all-done.1.refs_9_.refs_4_), channel_id=1, source_target_pairs={{0,1},{1,0},{2,3},{3,2},{4,5},{5,4},{6,7},{7,6},{8,9},{9,8},{10,11... | collective-permute-start | bytes 2654216 | tf_op jit(solution)/shard_map/ppermute | solution.py:40
  60.7 18.2 %all-to-all-start.2 = ((bf16[4,128,512]{2,1,0:T(8,128)(2,1)}), bf16[4,128,512]{2,1,0:T(8,128)(2,1)}, u32[]{:S(2)}, u32[]{:S(2)}) async-start(bf16[4,128,512]{2,1,0:T(8,128)(2,1)} %broadcast_in_dim.52), calls=%async_computation.2 | async-start | bytes 1048576 | tf_op jit(solution)/shard_map/all_to_all | solution.py:56
  64.9 47.9 %collective-permute-start.5 = (bf16[256,1024]{1,0:T(8,128)(2,1)S(1)}, bf16[256,1024]{1,0:T(8,128)(2,1)}, u32[]{:S(2)}, u32[]{:S(2)}) collective-permute-start(bf16[256,1024]{1,0:T(8,128)(2,1)S(1)} %copy-done.37), channel_id=1, source_target_pairs={{0,8},{1,9},{2,10},{3,11},{4,12},{5,13},{6,14},{7,15},{8,0},{9,1},... | collective-permute-start | bytes 1572872 | tf_op jit(solution)/shard_map/ppermute | solution.py:40
  78.9 21.0 %collective-permute-start.1 = (bf16[4,128,512]{2,1,0:T(8,128)(2,1)}, bf16[4,128,512]{2,1,0:T(8,128)(2,1)}, u32[]{:S(2)}, u32[]{:S(2)}) collective-permute-start(bf16[4,128,512]{2,1,0:T(8,128)(2,1)} %all-to-all-done.2.refs_3_.refs_4_), channel_id=1, source_target_pairs={{0,1},{1,0},{2,3},{3,2},{4,5},{5,4},{6,7},{7,6},{8,9},{9,8},{10,11... | collective-permute-start | bytes 1572872 | tf_op jit(solution)/shard_map/ppermute | solution.py:40
  80.1 17.4 %all-to-all-start.3 = ((bf16[4,128,512]{2,1,0:T(8,128)(2,1)}), bf16[4,128,512]{2,1,0:T(8,128)(2,1)S(1)}, u32[]{:S(2)}, u32[]{:S(2)}) async-start(bf16[4,128,512]{2,1,0:T(8,128)(2,1)} %broadcast_in_dim.96), calls=%async_computation.3 | async-start | bytes 1048576 | tf_op jit(solution)/shard_map/all_to_all | solution.py:56
  97.5 12.0 %collective-permute-start.4 = (bf16[4,128,512]{2,1,0:T(8,128)(2,1)S(1)}, bf16[4,128,512]{2,1,0:T(8,128)(2,1)S(1)}, u32[]{:S(2)}, u32[]{:S(2)}) collective-permute-start(bf16[4,128,512]{2,1,0:T(8,128)(2,1)S(1)} %all-to-all-done.3.refs_2_.refs_9_), channel_id=1, source_target_pairs={{0,1},{1,0},{2,3},{3,2},{4,5},{5,4},{6,7},{7,6},{8,9},{9,8},{10,11... | collective-permute-start | bytes 1572872 | tf_op jit(solution)/shard_map/ppermute | solution.py:40
  100.8 26.9 %all-to-all-start.4 = ((bf16[4,128,512]{2,1,0:T(8,128)(2,1)}), bf16[4,128,512]{2,1,0:T(8,128)(2,1)}, u32[]{:S(2)}, u32[]{:S(2)}) async-start(bf16[4,128,512]{2,1,0:T(8,128)(2,1)} %broadcast_in_dim.51), calls=%async_computation.4 | async-start | bytes 1048576 | tf_op jit(solution)/shard_map/all_to_all | solution.py:56
  110.4 17.3 %collective-permute-start.6 = (bf16[2,2,128,512]{3,2,1,0:T(8,128)(2,1)}, bf16[2,2,128,512]{3,2,1,0:T(8,128)(2,1)}, u32[]{:S(2)}, u32[]{:S(2)}) collective-permute-start(bf16[2,2,128,512]{3,2,1,0:T(8,128)(2,1)} %pad_maximum_fusion.2), channel_id=1, source_target_pairs={{0,8},{1,9},{2,10},{3,11},{4,12},{5,13},{6,14},{7,15},{8,0},{9,1},... | collective-permute-start | bytes 1572872 | tf_op jit(solution)/shard_map/ppermute | solution.py:40
  132.2 32.4 %collective-permute-start.7 = (f32[512,1024]{1,0:T(8,128)}, f32[512,1024]{1,0:T(8,128)S(1)}, u32[]{:S(2)}, u32[]{:S(2)}) collective-permute-start(f32[512,1024]{1,0:T(8,128)} %dense.1.part), channel_id=1, source_target_pairs={{0,8},{1,9},{2,10},{3,11},{4,12},{5,13},{6,14},{7,15},{8,0},{9,1},... | collective-permute-start | bytes 6291464 | tf_op jit(solution)/shard_map/ppermute | solution.py:40
  135.4 23.8 %all-to-all-start.5 = ((bf16[4,128,640]{2,1,0:T(8,128)(2,1)}), bf16[4,128,640]{2,1,0:T(8,128)(2,1)}, u32[]{:S(2)}, u32[]{:S(2)}) async-start(bf16[4,128,640]{2,1,0:T(8,128)(2,1)} %broadcast_in_dim.97), calls=%async_computation.5 | async-start | bytes 1310720 | tf_op jit(solution)/shard_map/all_to_all | solution.py:56
  144.8 25.7 %collective-permute-start.8 = (bf16[4,128,512]{2,1,0:T(8,128)(2,1)}, bf16[4,128,512]{2,1,0:T(8,128)(2,1)}, u32[]{:S(2)}, u32[]{:S(2)}) collective-permute-start(bf16[4,128,512]{2,1,0:T(8,128)(2,1)} %all-to-all-done.2.refs_3_.refs_4_), channel_id=1, source_target_pairs={{0,16},{1,17},{2,18},{3,19},{4,20},{5,21},{6,22},{7,23},{8,24},{9,... | collective-permute-start | bytes 1572872 | tf_op jit(solution)/shard_map/ppermute | solution.py:40
  146.0 13.0 %collective-permute-start.3 = (bf16[4,128,512]{2,1,0:T(8,128)(2,1)}, bf16[4,128,512]{2,1,0:T(8,128)(2,1)}, u32[]{:S(2)}, u32[]{:S(2)}) collective-permute-start(bf16[4,128,512]{2,1,0:T(8,128)(2,1)} %all-to-all-done.4.refs_5_.refs_6_), channel_id=1, source_target_pairs={{0,1},{1,0},{2,3},{3,2},{4,5},{5,4},{6,7},{7,6},{8,9},{9,8},{10,11... | collective-permute-start | bytes 1572872 | tf_op jit(solution)/shard_map/ppermute | solution.py:40
  147.8 25.2 %collective-permute-start.9 = (bf16[4,128,512]{2,1,0:T(8,128)(2,1)}, bf16[4,128,512]{2,1,0:T(8,128)(2,1)}, u32[]{:S(2)}, u32[]{:S(2)}) collective-permute-start(bf16[4,128,512]{2,1,0:T(8,128)(2,1)} %collective-permute-done.1.refs_4_.refs_5_), channel_id=1, source_target_pairs={{0,16},{1,17},{2,18},{3,19},{4,20},{5,21},{6,22},{7,23},{8,24},{9,... | collective-permute-start | bytes 1572872 | tf_op jit(solution)/shard_map/ppermute | solution.py:40
  148.1 32.5 %collective-permute-start.10 = (bf16[4,128,512]{2,1,0:T(8,128)(2,1)}, bf16[4,128,512]{2,1,0:T(8,128)(2,1)}, u32[]{:S(2)}, u32[]{:S(2)}) collective-permute-start(bf16[4,128,512]{2,1,0:T(8,128)(2,1)} %all-to-all-done.4.refs_5_.refs_6_), channel_id=1, source_target_pairs={{0,16},{1,17},{2,18},{3,19},{4,20},{5,21},{6,22},{7,23},{8,24},{9,... | collective-permute-start | bytes 1572872 | tf_op jit(solution)/shard_map/ppermute | solution.py:40
  159.0 32.8 %collective-permute-start.11 = (bf16[4,128,512]{2,1,0:T(8,128)(2,1)}, bf16[4,128,512]{2,1,0:T(8,128)(2,1)}, u32[]{:S(2)}, u32[]{:S(2)}) collective-permute-start(bf16[4,128,512]{2,1,0:T(8,128)(2,1)} %collective-permute-done.3.refs_6_.refs_7_), channel_id=1, source_target_pairs={{0,16},{1,17},{2,18},{3,19},{4,20},{5,21},{6,22},{7,23},{8,24},{9,... | collective-permute-start | bytes 1572872 | tf_op jit(solution)/shard_map/ppermute | solution.py:40
  160.2 23.9 %all-to-all-start.6 = ((bf16[4,256,384]{2,1,0:T(8,128)(2,1)}), bf16[4,256,384]{2,1,0:T(8,128)(2,1)}, u32[]{:S(2)}, u32[]{:S(2)}) async-start(bf16[4,256,384]{2,1,0:T(8,128)(2,1)} %broadcast_in_dim.99), calls=%async_computation.6 | async-start | bytes 1572864 | tf_op jit(solution)/shard_map/all_to_all | solution.py:56
  164.6 14.3 %collective-permute-start.13 = (bf16[4,128,640]{2,1,0:T(8,128)(2,1)}, bf16[4,128,640]{2,1,0:T(8,128)(2,1)}, u32[]{:S(2)}, u32[]{:S(2)}) collective-permute-start(bf16[4,128,640]{2,1,0:T(8,128)(2,1)} %all-to-all-done.5.refs_12_.refs_2_), channel_id=1, source_target_pairs={{0,1},{1,0},{2,3},{3,2},{4,5},{5,4},{6,7},{7,6},{8,9},{9,8},{10,11... | collective-permute-start | bytes 1966088 | tf_op jit(solution)/shard_map/ppermute | solution.py:40
  170.5 33.4 %collective-permute-start.12 = (bf16[256,1024]{1,0:T(8,128)(2,1)}, bf16[256,1024]{1,0:T(8,128)(2,1)}, u32[]{:S(2)}, u32[]{:S(2)}) collective-permute-start(bf16[256,1024]{1,0:T(8,128)(2,1)} %refs_4_.1), channel_id=1, source_target_pairs={{0,8},{1,9},{2,10},{3,11},{4,12},{5,13},{6,14},{7,15},{8,0},{9,1},... | collective-permute-start | bytes 1572872 | tf_op jit(solution)/shard_map/ppermute | solution.py:40
  173.0 37.6 %collective-permute-start.14 = (bf16[4,128,640]{2,1,0:T(8,128)(2,1)}, bf16[4,128,640]{2,1,0:T(8,128)(2,1)}, u32[]{:S(2)}, u32[]{:S(2)}) collective-permute-start(bf16[4,128,640]{2,1,0:T(8,128)(2,1)} %all-to-all-done.5.refs_12_.refs_2_), channel_id=1, source_target_pairs={{0,16},{1,17},{2,18},{3,19},{4,20},{5,21},{6,22},{7,23},{8,24},{9,... | collective-permute-start | bytes 1966088 | tf_op jit(solution)/shard_map/ppermute | solution.py:40
  178.8 41.0 %collective-permute-start.15 = (bf16[4,128,640]{2,1,0:T(8,128)(2,1)}, bf16[4,128,640]{2,1,0:T(8,128)(2,1)}, u32[]{:S(2)}, u32[]{:S(2)}) collective-permute-start(bf16[4,128,640]{2,1,0:T(8,128)(2,1)} %collective-permute-done.13.refs_13_.refs_3_), channel_id=1, source_target_pairs={{0,16},{1,17},{2,18},{3,19},{4,20},{5,21},{6,22},{7,23},{8,24},{9,... | collective-permute-start | bytes 1966088 | tf_op jit(solution)/shard_map/ppermute | solution.py:40
  184.1 35.8 %collective-permute-start.16 = (bf16[4,256,384]{2,1,0:T(8,128)(2,1)}, bf16[4,256,384]{2,1,0:T(8,128)(2,1)}, u32[]{:S(2)}, u32[]{:S(2)}) collective-permute-start(bf16[4,256,384]{2,1,0:T(8,128)(2,1)} %all-to-all-done.6.refs_16_.refs_6_), channel_id=1, source_target_pairs={{0,1},{1,0},{2,3},{3,2},{4,5},{5,4},{6,7},{7,6},{8,9},{9,8},{10,11... | collective-permute-start | bytes 2359304 | tf_op jit(solution)/shard_map/ppermute | solution.py:40
  209.2 66.6 %collective-permute-start.19 = (bf16[4,256,512]{2,1,0:T(8,128)(2,1)}, bf16[4,256,512]{2,1,0:T(8,128)(2,1)}, u32[]{:S(2)}, u32[]{:S(2)}) collective-permute-start(bf16[4,256,512]{2,1,0:T(8,128)(2,1)} %get-tuple-element.126), channel_id=1, source_target_pairs={{0,16},{1,17},{2,18},{3,19},{4,20},{5,21},{6,22},{7,23},{8,24},{9,... | collective-permute-start | bytes 3145736 | tf_op jit(solution)/shard_map/ppermute | solution.py:40
  210.4 68.1 %collective-permute-start.18 = (bf16[4,256,512]{2,1,0:T(8,128)(2,1)}, bf16[4,256,512]{2,1,0:T(8,128)(2,1)}, u32[]{:S(2)}, u32[]{:S(2)}) collective-permute-start(bf16[4,256,512]{2,1,0:T(8,128)(2,1)} %get-tuple-element.124), channel_id=1, source_target_pairs={{0,16},{1,17},{2,18},{3,19},{4,20},{5,21},{6,22},{7,23},{8,24},{9,... | collective-permute-start | bytes 3145736 | tf_op jit(solution)/shard_map/ppermute | solution.py:40
  234.8 10.8 %collective-permute-start.21 = (f32[512,1024]{1,0:T(8,128)}, f32[512,1024]{1,0:T(8,128)}, u32[]{:S(2)}, u32[]{:S(2)}) collective-permute-start(f32[512,1024]{1,0:T(8,128)} %get-tuple-element.130.refs_1_), channel_id=1, source_target_pairs={{0,8},{1,9},{2,10},{3,11},{4,12},{5,13},{6,14},{7,15},{8,0},{9,1},... | collective-permute-start | bytes 6291464 | tf_op jit(solution)/shard_map/ppermute | solution.py:40
  243.2 25.1 %collective-permute-start.20 = (bf16[4,128,1024]{2,1,0:T(8,128)(2,1)}, bf16[4,128,1024]{2,1,0:T(8,128)(2,1)}, u32[]{:S(2)}, u32[]{:S(2)}) collective-permute-start(bf16[4,128,1024]{2,1,0:T(8,128)(2,1)} %get-tuple-element.128), channel_id=1, source_target_pairs={{0,1},{1,0},{2,3},{3,2},{4,5},{5,4},{6,7},{7,6},{8,9},{9,8},{10,11... | collective-permute-start | bytes 3145736 | tf_op jit(solution)/shard_map/ppermute | solution.py:40
  244.4 42.9 %collective-permute-start.17 = (bf16[4,256,512]{2,1,0:T(8,128)(2,1)}, bf16[4,256,512]{2,1,0:T(8,128)(2,1)}, u32[]{:S(2)}, u32[]{:S(2)}) collective-permute-start(bf16[4,256,512]{2,1,0:T(8,128)(2,1)} %get-tuple-element.122), channel_id=1, source_target_pairs={{0,16},{1,17},{2,18},{3,19},{4,20},{5,21},{6,22},{7,23},{8,24},{9,... | collective-permute-start | bytes 3145736 | tf_op jit(solution)/shard_map/ppermute | solution.py:40
  271.0 48.2 %all-to-all-start.7 = ((bf16[4,128,1024]{2,1,0:T(8,128)(2,1)}), bf16[4,128,1024]{2,1,0:T(8,128)(2,1)}, u32[]{:S(2)}, u32[]{:S(2)}) async-start(bf16[4,128,1024]{2,1,0:T(8,128)(2,1)} %gup_x.1), calls=%async_computation.7 | async-start | bytes 2097152 | tf_op jit(solution)/shard_map/all_to_all | solution.py:56
  291.3 13.9 %collective-permute-start.27 = (bf16[4,128,512]{2,1,0:T(8,128)(2,1)}, bf16[4,128,512]{2,1,0:T(8,128)(2,1)}, u32[]{:S(2)}, u32[]{:S(2)}) collective-permute-start(bf16[4,128,512]{2,1,0:T(8,128)(2,1)} %get-tuple-element.165), channel_id=1, source_target_pairs={{0,1},{1,0},{2,3},{3,2},{4,5},{5,4},{6,7},{7,6},{8,9},{9,8},{10,11... | collective-permute-start | bytes 1572872 | tf_op jit(solution)/shard_map/ppermute | solution.py:40
  292.5 23.9 %collective-permute-start.26 = (bf16[4,128,512]{2,1,0:T(8,128)(2,1)}, bf16[4,128,512]{2,1,0:T(8,128)(2,1)}, u32[]{:S(2)}, u32[]{:S(2)}) collective-permute-start(bf16[4,128,512]{2,1,0:T(8,128)(2,1)} %get-tuple-element.164), channel_id=1, source_target_pairs={{0,1},{1,0},{2,3},{3,2},{4,5},{5,4},{6,7},{7,6},{8,9},{9,8},{10,11... | collective-permute-start | bytes 1572872 | tf_op jit(solution)/shard_map/ppermute | solution.py:40
  292.8 30.9 %collective-permute-start.24 = (bf16[4,256,384]{2,1,0:T(8,128)(2,1)}, bf16[4,256,384]{2,1,0:T(8,128)(2,1)}, u32[]{:S(2)}, u32[]{:S(2)}) collective-permute-start(bf16[4,256,384]{2,1,0:T(8,128)(2,1)} %get-tuple-element.152), channel_id=1, source_target_pairs={{0,16},{1,17},{2,18},{3,19},{4,20},{5,21},{6,22},{7,23},{8,24},{9,... | collective-permute-start | bytes 2359304 | tf_op jit(solution)/shard_map/ppermute | solution.py:40
  294.0 34.5 %collective-permute-start.23 = (bf16[4,256,384]{2,1,0:T(8,128)(2,1)}, bf16[4,256,384]{2,1,0:T(8,128)(2,1)}, u32[]{:S(2)}, u32[]{:S(2)}) collective-permute-start(bf16[4,256,384]{2,1,0:T(8,128)(2,1)} %get-tuple-element.151), channel_id=1, source_target_pairs={{0,16},{1,17},{2,18},{3,19},{4,20},{5,21},{6,22},{7,23},{8,24},{9,... | collective-permute-start | bytes 2359304 | tf_op jit(solution)/shard_map/ppermute | solution.py:40
  294.3 36.6 %collective-permute-start.22 = (bf16[4,128,512]{2,1,0:T(8,128)(2,1)}, bf16[4,128,512]{2,1,0:T(8,128)(2,1)}, u32[]{:S(2)}, u32[]{:S(2)}) collective-permute-start(bf16[4,128,512]{2,1,0:T(8,128)(2,1)} %get-tuple-element.149), channel_id=1, source_target_pairs={{0,1},{1,0},{2,3},{3,2},{4,5},{5,4},{6,7},{7,6},{8,9},{9,8},{10,11... | collective-permute-start | bytes 1572872 | tf_op jit(solution)/shard_map/ppermute | solution.py:40
  319.2 29.8 %all-to-all-start.8 = ((bf16[4,128,1024]{2,1,0:T(8,128)(2,1)}), bf16[4,128,1024]{2,1,0:T(8,128)(2,1)}, u32[]{:S(2)}, u32[]{:S(2)}) async-start(bf16[4,128,1024]{2,1,0:T(8,128)(2,1)} %gdown_x.1), calls=%async_computation.8 | async-start | bytes 2097152 | tf_op jit(solution)/shard_map/all_to_all | solution.py:56
  343.9 13.8 %collective-permute-start.38 = (bf16[4,128,512]{2,1,0:T(8,128)(2,1)}, bf16[4,128,512]{2,1,0:T(8,128)(2,1)}, u32[]{:S(2)}, u32[]{:S(2)}) collective-permute-start(bf16[4,128,512]{2,1,0:T(8,128)(2,1)} %get-tuple-element.186), channel_id=1, source_target_pairs={{0,1},{1,0},{2,3},{3,2},{4,5},{5,4},{6,7},{7,6},{8,9},{9,8},{10,11... | collective-permute-start | bytes 1572872 | tf_op jit(solution)/shard_map/ppermute | solution.py:40
  345.1 21.1 %collective-permute-start.37 = (bf16[4,128,384]{2,1,0:T(8,128)(2,1)}, bf16[4,128,384]{2,1,0:T(8,128)(2,1)}, u32[]{:S(2)}, u32[]{:S(2)}) collective-permute-start(bf16[4,128,384]{2,1,0:T(8,128)(2,1)} %get-tuple-element.185), channel_id=1, source_target_pairs={{0,1},{1,0},{2,3},{3,2},{4,5},{5,4},{6,7},{7,6},{8,9},{9,8},{10,11... | collective-permute-start | bytes 1179656 | tf_op jit(solution)/shard_map/ppermute | solution.py:40
  345.4 29.2 %collective-permute-start.36 = (bf16[4,128,384]{2,1,0:T(8,128)(2,1)}, bf16[4,128,384]{2,1,0:T(8,128)(2,1)}, u32[]{:S(2)}, u32[]{:S(2)}) collective-permute-start(bf16[4,128,384]{2,1,0:T(8,128)(2,1)} %get-tuple-element.184), channel_id=1, source_target_pairs={{0,1},{1,0},{2,3},{3,2},{4,5},{5,4},{6,7},{7,6},{8,9},{9,8},{10,11... | collective-permute-start | bytes 1179656 | tf_op jit(solution)/shard_map/ppermute | solution.py:40
  349.0 25.6 %all-to-all-start.9 = ((bf16[4,128,512]{2,1,0:T(8,128)(2,1)}), bf16[4,128,512]{2,1,0:T(8,128)(2,1)}, u32[]{:S(2)}, u32[]{:S(2)}) async-start(bf16[4,128,512]{2,1,0:T(8,128)(2,1)} %gup2_x.1), calls=%async_computation.9 | async-start | bytes 1048576 | tf_op jit(solution)/shard_map/all_to_all | solution.py:56
  383.8 9.6 %collective-permute-start.45 = (bf16[128,1024]{1,0:T(8,128)(2,1)}, bf16[128,1024]{1,0:T(8,128)(2,1)}, u32[]{:S(2)}, u32[]{:S(2)}) collective-permute-start(bf16[128,1024]{1,0:T(8,128)(2,1)} %gdown_z.1), channel_id=1, source_target_pairs={{0,16},{1,17},{2,18},{3,19},{4,20},{5,21},{6,22},{7,23},{8,24},{9,... | collective-permute-start | bytes 786440 | tf_op jit(solution)/shard_map/ppermute | solution.py:40
  385.1 18.6 %all-to-all-start.10 = ((bf16[4,128,512]{2,1,0:T(8,128)(2,1)}), bf16[4,128,512]{2,1,0:T(8,128)(2,1)}, u32[]{:S(2)}, u32[]{:S(2)}) async-start(bf16[4,128,512]{2,1,0:T(8,128)(2,1)} %gdense_x.1), calls=%async_computation.10 | async-start | bytes 1048576 | tf_op jit(solution)/shard_map/all_to_all | solution.py:56
  392.0 24.0 %collective-permute-start.29 = (f32[256,1024]{1,0:T(8,128)}, f32[256,1024]{1,0:T(8,128)}, u32[]{:S(2)}, u32[]{:S(2)}) collective-permute-start(f32[256,1024]{1,0:T(8,128)} %get-tuple-element.177), channel_id=1, source_target_pairs={{0,8},{1,9},{2,10},{3,11},{4,12},{5,13},{6,14},{7,15},{8,0},{9,1},... | collective-permute-start | bytes 3145736 | tf_op jit(solution)/shard_map/ppermute | solution.py:40
  395.9 17.8 %collective-permute-start.46 = (bf16[256,1024]{1,0:T(8,128)(2,1)}, bf16[256,1024]{1,0:T(8,128)(2,1)}, u32[]{:S(2)}, u32[]{:S(2)}) collective-permute-start(bf16[256,1024]{1,0:T(8,128)(2,1)} %pad_maximum_fusion.4), channel_id=1, source_target_pairs={{0,8},{1,9},{2,10},{3,11},{4,12},{5,13},{6,14},{7,15},{8,0},{9,1},... | collective-permute-start | bytes 1572872 | tf_op jit(solution)/shard_map/ppermute | solution.py:40
  406.0 23.1 %collective-permute-start.43 = (bf16[128,1536]{1,0:T(8,128)(2,1)}, bf16[128,1536]{1,0:T(8,128)(2,1)}, u32[]{:S(2)}, u32[]{:S(2)}) collective-permute-start(bf16[128,1536]{1,0:T(8,128)(2,1)} %gup_z.1), channel_id=1, source_target_pairs={{0,16},{1,17},{2,18},{3,19},{4,20},{5,21},{6,22},{7,23},{8,24},{9,... | collective-permute-start | bytes 1179656 | tf_op jit(solution)/shard_map/ppermute | solution.py:40
  408.0 16.6 %collective-permute-start.41 = (bf16[128,512]{1,0:T(8,128)(2,1)}, bf16[128,512]{1,0:T(8,128)(2,1)}, u32[]{:S(2)}, u32[]{:S(2)}) collective-permute-start(bf16[128,512]{1,0:T(8,128)(2,1)} %gdense_z.1), channel_id=1, source_target_pairs={{0,16},{1,17},{2,18},{3,19},{4,20},{5,21},{6,22},{7,23},{8,24},{9,... | collective-permute-start | bytes 393224 | tf_op jit(solution)/shard_map/ppermute | solution.py:40
  409.2 34.1 %all-to-all-start.11 = ((bf16[4,128,768]{2,1,0:T(8,128)(2,1)}), bf16[4,128,768]{2,1,0:T(8,128)(2,1)}, u32[]{:S(2)}, u32[]{:S(2)}) async-start(bf16[4,128,768]{2,1,0:T(8,128)(2,1)} %gqkv_x.1), calls=%async_computation.11 | async-start | bytes 1572864 | tf_op jit(solution)/shard_map/all_to_all | solution.py:56
  433.2 20.8 %collective-permute-start.44 = (f32[128,8,1,256]{0,3,1,2:T(8,128)}, f32[128,8,1,256]{0,3,1,2:T(8,128)}, u32[]{:S(2)}, u32[]{:S(2)}) collective-permute-start(f32[128,8,1,256]{0,3,1,2:T(8,128)} %bitcast.37), channel_id=1, source_target_pairs={{0,8},{1,9},{2,10},{3,11},{4,12},{5,13},{6,14},{7,15},{8,0},{9,1},... | collective-permute-start | bytes 3145736 | tf_op jit(solution)/shard_map/ppermute | solution.py:40
  (51 other events, 547.5 us)

commit v4 on v3

--- a/solution.py
+++ b/solution.py
@@ -15,6 +15,7 @@
 AXES = ("rep", "shard")
 gelu_coef = math.sqrt(2.0 / math.pi)
 VMEM_LIMIT = 60 * 2**20
+COST = {'attn': 1000, 'dense': 1000, 'middle': 1000, 'up': 1000, 'gdown': 13.2, 'feed_back': 1000, 'gup': 16.2, 'attn_back': 1000, 'gqkv': 15.3, 'gdense': 9.0, 'output': 25.2, 'gnorm': 21.6, 'gdense_c': 6.6, 'input_grad': 11.4, 'gup_y': 7.8, 'gup_x': 7.8, 'gdown_x': 7.8, 'gqkv_x': 7.8, 'gqkv_y': 7.8, 'gdense_x': 7.8, 'gup_z': 7.8, 'gdown_z': 7.8, 'gdense_z': 7.8, 'gqkv_z': 7.8}
 
 
 class Place:
@@ -99,7 +100,7 @@
         out_specs=[vmem() for _ in outs],
         scratch_shapes=list(scratch),
         compiler_params=pltpu.CompilerParams(vmem_limit_bytes=VMEM_LIMIT),
-        cost_estimate=pl.CostEstimate(flops=10**12, bytes_accessed=10**9, transcendentals=0),
+        cost_estimate=pl.CostEstimate(flops=int(1153.5e6 * COST.get(name, 2.5)), bytes_accessed=10**6, transcendentals=0),
         name=name,
     )(*ins)
 
@@ -214,7 +215,7 @@
     seen = k_pos <= q_pos
     pairs = half // (2 * hd)
 
-    @pl.loop(0, 2 * pairs)
+    @pl.loop(0, 2 * pairs, unroll=2)
     def _(step):
         seq, pair = step // pairs, step % pairs
         at = pl.ds(pl.multiple_of(seq * rows, rows), rows)
@@ -266,11 +267,12 @@
     def _(t):
         at = pl.ds(pl.multiple_of(t * tile, tile), tile)
         u = dot(mid[...], wu[:, at]) + up_b[:, at]
-        t_ = jnp.tanh(gelu_coef * (u + 0.044715 * u * u * u))
-        act_ref[:, at] = (0.5 * u * (1.0 + t_)).astype(BF)
-        slope_ref[:, at] = 0.5 * (1.0 + t_) + 0.5 * u * (1.0 - t_ * t_) * gelu_coef * (
-            1.0 + 3.0 * 0.044715 * u * u
-        )
+        square = u * u
+        t_ = jnp.tanh(u * (gelu_coef + gelu_coef * 0.044715 * square))
+        gate = 0.5 + 0.5 * t_
+        value = u * gate
+        act_ref[:, at] = value.astype(BF)
+        slope_ref[:, at] = gate + value * (1.0 - t_) * (gelu_coef + 3.0 * 0.044715 * gelu_coef * square)
 
 
 def feed_back_kernel(n, rd, quarter, *refs):
@@ -354,19 +356,29 @@
     return picked
 
 
-def up_grad_kernel(nx, info, left, right, away, mine, *outs):
+def up_grad_kernel(parts, nx, left, right, *outs):
+    nz, rows, cols = outs[0].shape
+    for p in range(parts):
+        for z in range(nz):
+            lhs = left[:, z * rows : (z + 1) * rows]
+            for h in range(2):
+                start = (h * parts + p) * cols
+                outs[2 * p + 1 - h][z] = dot_tn(lhs, right[:, start : start + cols]).astype(BF)
+
+
+def down_grad_kernel(p, nx, info, left, own, other, *outs):
     nz, per, cols = outs[0].shape
-    cols //= 2
-    half = right.shape[1] // 2
+    per //= 2
+    tokens = own.shape[0]
+    half = left.shape[1] // 2
+    here = slice(p * cols, (p + 1) * cols)
     for z in range(nz):
-        lhs = left[:, z * nx * per : (z + 1) * nx * per]
         for h in range(2):
-            value = dot_tn(lhs, right[:, h * half : h * half + cols]).astype(BF)
-            lanes = pl.ds(pl.multiple_of(jnp.bitwise_xor(info[0], h) * cols, 128), cols)
+            lanes = slice(h * half + z * nx * per, h * half + (z + 1) * nx * per)
+            value = dot_tn(left[:tokens, lanes], own[:, here]) + dot_tn(left[tokens:, lanes], other[:, here])
+            rows = pl.ds(aligned(jnp.bitwise_xor(info[0], h) * per, per), per)
             for kx in range(nx):
-                outs[kx][z, :, lanes] = at_x(info, kx, nx, per, value)
-            out = away if h else mine
-            out[z] = dot_tn(lhs, right[:, h * half + cols : (h + 1) * half]).astype(BF)
+                outs[kx][z, rows, :] = at_x(info, kx, nx, per, value).astype(BF)
 
 
 def fold_y_kernel(nx, info, mine, recv, *outs):
@@ -445,7 +457,7 @@
     pairs = half // (2 * hd)
     qvb_ref[...] = jnp.zeros_like(qvb_ref)
 
-    @pl.loop(0, 2 * pairs)
+    @pl.loop(0, 2 * pairs, unroll=2)
     def _(step):
         seq, pair = step // pairs, step % pairs
         at = pl.ds(pl.multiple_of(seq * rows, rows), rows)
@@ -646,7 +658,17 @@
         total = sum(v.shape[2] for v in ends)
         return call(total_kernel, [((per, total), BF)], ends, "v" * len(ends), name=name + "_z")[0]
 
-    down_terms = scatter_y(act, [cotangent, cot_other], quarter, width, False, "gdown")
+    down_x, before = [], []
+    for p in range(2):
+        down_terms = call(
+            functools.partial(down_grad_kernel, p, nx),
+            [((nz, 2 * quarter, width // 2), BF)] * nx,
+            [info, after(act, before), cotangent, cot_other],
+            "svvv",
+            name="gdown",
+        )
+        before = [down_terms[0]]
+        down_x.append(over_x(down_terms))
 
     gpre, gpre_sums, gmid = call(
         functools.partial(feed_back_kernel, 4 * nx, rd, quarter),
@@ -659,14 +681,15 @@
     )
     gmid_recv = at.to_core(gmid)
     up_terms = call(
-        functools.partial(up_grad_kernel, nx),
-        [((nz, nx * rd, fq // 2), BF)] * 2 + [((nz, rd, fq), BF)] * nx,
-        [info, mid, gpre],
-        "svv",
+        functools.partial(up_grad_kernel, 2, nx),
+        [((nz, nx * rd, fq // 2), BF)] * 4,
+        [mid, gpre],
+        "vv",
         name="gup",
     )
-    up_first_x = over_x(up_terms[2:])
-    up_second_y = (up_terms[1], at.to_y(up_terms[0]))
+    up_y = [(up_terms[2 * p + 1], at.to_y(up_terms[2 * p])) for p in range(2)]
+    down_sum = fold_x(after(down_x[0], [up_terms[0]]), "gdown")
+    end_down = [at.swap_z(down_sum)]
 
     grad_res, grad_res_b, sums2, dqkv, qv_sums = call(
         functools.partial(attention_back_kernel, nx, rd),
@@ -677,7 +700,7 @@
             ((2 * rows, 3 * half), BF),
             ((2, half), F32),
         ],
-        [info, gmid, gmid_recv, residual, cotangent, cot_other, gain2, qkv, probs] + dense_in,
+        [info, after(gmid, [down_sum]), gmid_recv, residual, cotangent, cot_other, gain2, qkv, probs] + dense_in,
         "s" + "v" * 8 + "a" * (nx + 1),
         [pltpu.VMEM((half, width), BF), pltpu.VMEM((2 * rows, half), BF), dma((n,))],
         mac * 3 * half,
@@ -690,11 +713,9 @@
         last[:] = [value[0] if isinstance(value, (list, tuple)) else value]
         return value
 
-    up_sum = order(fold_x(after(up_first_x, last), "gup"))
-    end_up = at.swap_z(up_sum)
-    down_x = order(fold_y(after(down_terms[0], last), "gdown"))
-    down_x = down_x + order(fold_y(after(down_terms[1], last), "gdown"))
-
+    down_sum2 = order(fold_x(after(down_x[1], last), "gdown"))
+    end_down.append(at.swap_z(after(down_sum2, end_down)))
+    up_x = order(fold_y(after(up_y[0], last), "gup"))
     keep, give = call(
         dense_grad_kernel,
         [((nz // 2, nx * rd, half), BF)] * 2,
@@ -703,23 +724,6 @@
         name="gdense",
     )
     order(keep)
-    up2_x = order(fold_y(after(up_second_y, last), "gup2"))
-    parts = call(
-        functools.partial(dense_place_kernel, nx),
-        [((nz, rd, half), BF)] * nx,
-        [info, after(keep, last), at.to_core(give)],
-        "svv",
-        name="gdense_c",
-    )
-    order(parts)
-    dense_x = over_x(parts)
-    down_sum = order(fold_x(after(down_x, last), "gdown"))
-    end_down = at.swap_z(after(down_sum, [end_up]))
-    order(end_up)
-    qkv_x = order(fold_y(after(qkv_terms[0], last), "gqkv"))
-    qkv_x = qkv_x + order(fold_y(after(qkv_terms[1], last), "gqkv"))
-    up2_sum = order(fold_x(after(up2_x, last), "gup2"))
-    end_up2 = at.swap_z(after(up2_sum, [end_down]))
     out_own, out_other = order(
         call(
             functools.partial(output_kernel, 3 * nx, quarter),
@@ -730,12 +734,22 @@
             name="output",
         )
     )
-    order(end_down)
-    dense_sum = order(fold_x(after(dense_x, last), "gdense"))
-    end_dense = at.swap_z(after(dense_sum, [end_up2]))
-    qkv_sum = order(fold_x(after(qkv_x, last), "gqkv"))
-    end_qkv = at.swap_z(after(qkv_sum, [end_dense]))
-    order(end_up2)
+    up_x = up_x + order(fold_y(after(up_y[1], last), "gup"))
+    parts = call(
+        functools.partial(dense_place_kernel, nx),
+        [((nz, rd, half), BF)] * nx,
+        [info, after(keep, last), at.to_core(give)],
+        "svv",
+        name="gdense_c",
+    )
+    order(parts)
+    dense_x = over_x(parts)
+    up_sum = order(fold_x(after(up_x, last), "gup"))
+    end_up = at.swap_z(after(up_sum, end_down[1:]))
+    order(end_down[1])
+    qkv_x = order(fold_y(after(qkv_terms[0], last), "gqkv"))
+    qkv_x = qkv_x + order(fold_y(after(qkv_terms[1], last), "gqkv"))
+    order(end_up)
     norm_own, norm_other = order(
         call(
             functools.partial(normed_kernel, 2 * nx, rd),
@@ -746,18 +760,23 @@
             name="gnorm",
         )
     )
-    down_own = order(finish_z([after(end_down, last)], "gdown"))
-    down_other = at.to_y(down_own)
-    order(end_dense)
-    up_part = order(finish_z(after([end_up, end_up2], last), "gup"))
-    up_recv = at.to_y(up_part)
-    dense_part = finish_z([end_dense], "gdense")
-    qkv_own = finish_z([end_qkv], "gqkv")
+    qkv_sum = order(fold_x(after(qkv_x, last), "gqkv"))
+    end_qkv = at.swap_z(after(qkv_sum, [end_up]))
+    order(end_up)
+    down_part = order(finish_z(after(end_down, last), "gdown"))
+    down_recv = at.to_y(down_part)
+    dense_sum = order(fold_x(after(dense_x, last), "gdense"))
+    end_dense = at.swap_z(after(dense_sum, [end_qkv]))
+    up_own = order(finish_z([after(end_up, last)], "gup"))
+    up_other = at.to_y(up_own)
+    order(end_qkv)
+    qkv_own = order(finish_z([after(end_qkv, last)], "gqkv"))
     qkv_other = at.to_y(qkv_own)
+    dense_part = order(finish_z([after(end_dense, last)], "gdense"))
     dense_mine = dense_part.astype(F32) + at.to_y(dense_part).astype(F32)
     grad_dense = jnp.concatenate(pick(dense_mine, at.to_core(dense_mine), core), axis=1)
 
-    output = (residual[:rows] + (out_own + at.to_core(out_other)) + down_b).astype(BF)
+    output = (residual[:rows] + (after(out_own, [dense_part]) + at.to_core(out_other)) + down_b).astype(BF)
 
     input_grad, sums1 = call(
         input_kernel,
@@ -767,13 +786,10 @@
         name="input_grad",
     )
 
-    down_y = jnp.concatenate(pick(down_own, down_other, y), axis=0)
-    grad_down = jnp.concatenate(pick(down_y, at.to_core(down_y), core), axis=0).astype(F32)
-    up_total = up_part[:, :fq].astype(F32) + up_recv[:, :fq].astype(F32)
-    up_both = [v.astype(F32) for v in pick(up_part[:, fq:], up_recv[:, fq:], y)]
-    up_c = jnp.concatenate([up_total] + up_both, axis=1)
-    up_c = up_c.reshape(rd, 2, 2, n // 2, quarter).transpose(0, 1, 3, 2, 4).reshape(rd, n, 1, 2 * quarter)
-    grad_up = jnp.concatenate(pick(up_c, at.to_core(up_c), core), axis=2).reshape(rd, ff)
+    down_c = down_part.astype(F32) + down_recv.astype(F32)
+    grad_down = jnp.concatenate(pick(down_c, at.to_core(down_c), core), axis=0)
+    up_c = jnp.stack([v.reshape(rd, n, quarter) for v in pick(up_own, up_other, y)], axis=2)
+    grad_up = jnp.stack(pick(up_c, at.to_core(up_c), core), axis=2).reshape(rd, ff).astype(F32)
     qkv_c = jnp.concatenate(pick(qkv_own, qkv_other, y), axis=1).reshape(rd, 3, 1, half)
     grad_qkv = jnp.concatenate(pick(qkv_c, at.to_core(qkv_c), core), axis=2).reshape(rd, 3 * width).astype(F32)
 

time: 462 us -> 441 us (0.955); the launches traced: 460 us -> 432 us
  waiting for transfers between devices: 156 us -> 139 us
  other arithmetic: 21.3 us -> 15.3 us
    ppermute x47 -> x46, waiting for transfers between devices: 88.4 us -> 56.2 us  [_send(): return lax.ppermute(value, AXES, pairs)]
    all_to_all x12, waiting for transfers between devices: 67.6 us -> 82.5 us  [swap_z(): lax.all_to_all(value, 'shard', 0, 0, axis_index_groups=along, tiled=True)]
    ppermute x47 -> x46, starting transfers between devices: 52.1 us -> 50.1 us  [_send(): return lax.ppermute(value, AXES, pairs)]
    unnamed x95 -> x101, local copies, waits for them, and re-layouts: 9.41 us -> 10.2 us
  transfers between devices with their start and end apart: 59 -> 58, of which waited for: 23 -> 22; matrix products, arithmetic and copies ran while one was open for 9% -> 8% of each run, Pallas kernels for 27% -> 31%
where the time goes in v4:
time: 441 us; the launch traced here: 432 us
  waiting for transfers between devices  139 us (32%)
  Pallas kernels  137 us (31%)
  starting transfers between devices  99.9 us (23%)
  local copies, waits for them, and re-layouts  29.2 us (7%)
  other arithmetic  15.3 us (3%)
  between operations  12.6 us (3%)
    pallas_call x28, Pallas kernels, call(): pl.pallas_call(body, out_shape=[jax.ShapeDtypeStruct(s, t) for s, t in ou...  137 us
    all_to_all x12, waiting for transfers between devices, swap_z(): lax.all_to_all(value, 'shard', 0, 0, axis_index_groups=along, tiled=True)  82.5 us
    ppermute x46, waiting for transfers between devices, _send(): return lax.ppermute(value, AXES, pairs)  56.2 us
    ppermute x46, starting transfers between devices, _send(): return lax.ppermute(value, AXES, pairs)  50.1 us
    all_to_all x12, starting transfers between devices, swap_z(): lax.all_to_all(value, 'shard', 0, 0, axis_index_groups=along, tiled=True)  49.8 us
    unnamed x101, local copies, waits for them, and re-layouts  10.2 us
  transfers between devices with their start and end apart: 58, of which 22 were waited for; matrix products, arithmetic and copies ran while one was open for 8% of the time, Pallas kernels for 31%

profile of v4, /device:TPU:1, one launch (start us, length us, event | category | flops | bytes accessed | tf_op | source)
XLA Modules:
  0.0 432.5 jit_solution(10056054975645707583)
XLA Ops:
  7.2 5.4 %all-to-all-start = ((bf16[4,128,768]{2,1,0:T(8,128)(2,1)}), bf16[4,128,768]{2,1,0:T(8,128)(2,1)}, u32[]{:S(2)}, u32[]{:S(2)}) async-start(bf16[4,128,768]{2,1,0:T(8,128)(2,1)} %broadcast_in_dim.53), calls=%async_computation | async-start | bytes 1572864 | tf_op jit(solution)/shard_map/all_to_all | solution.py:57
  14.9 17.5 %all-to-all-done.refs_7_.refs_2_ = bf16[4,128,768]{2,1,0:T(8,128)(2,1)} async-done(((bf16[4,128,768]{2,1,0:T(8,128)(2,1)}), bf16[4,128,768]{2,1,0:T(8,128)(2,1)}, u32[]{:S(2)}, u32[]{:S(2)}) %all-to-all-start) | async-done | bytes 786464 | tf_op jit(solution)/shard_map/all_to_all | solution.py:57
  33.3 3.5 all-to-all-start.1
  40.2 18.3 %all-to-all-done.1.refs_9_.refs_4_ = bf16[4,144,768]{2,1,0:T(8,128)(2,1)S(1)} async-done(((bf16[4,144,768]{2,1,0:T(8,128)(2,1)}), bf16[4,144,768]{2,1,0:T(8,128)(2,1)S(1)}, u32[]{:S(2)}, u32[]{:S(2)}) %all-to-all-start.1) | async-done | bytes 884768 | tf_op jit(solution)/shard_map/all_to_all | solution.py:57
  60.7 4.1 all-to-all-start.2
  72.1 6.8 %all-to-all-done.2.refs_3_.refs_4_ = bf16[4,128,512]{2,1,0:T(8,128)(2,1)} async-done(((bf16[4,128,512]{2,1,0:T(8,128)(2,1)}), bf16[4,128,512]{2,1,0:T(8,128)(2,1)}, u32[]{:S(2)}, u32[]{:S(2)}) %all-to-all-start.2) | async-done | bytes 524320 | tf_op jit(solution)/shard_map/all_to_all | solution.py:57
  80.1 3.5 all-to-all-start.3
  83.8 13.7 %all-to-all-done.3.refs_2_.refs_9_ = bf16[4,128,512]{2,1,0:T(8,128)(2,1)S(1)} async-done(((bf16[4,128,512]{2,1,0:T(8,128)(2,1)}), bf16[4,128,512]{2,1,0:T(8,128)(2,1)S(1)}, u32[]{:S(2)}, u32[]{:S(2)}) %all-to-all-start.3) | async-done | bytes 524320 | tf_op jit(solution)/shard_map/all_to_all | solution.py:57
  100.9 4.1 all-to-all-start.4
  105.0 4.4 %collective-permute-done.4.refs_3_.refs_10_ = bf16[4,128,512]{2,1,0:T(8,128)(2,1)S(1)} collective-permute-done((bf16[4,128,512]{2,1,0:T(8,128)(2,1)S(1)}, bf16[4,128,512]{2,1,0:T(8,128)(2,1)S(1)}, u32[]{:S(2)}, u32[]{:S(2)}) %collective-permute-start.4) | collective-permute-done | bytes 524320 | tf_op jit(solution)/shard_map/ppermute | solution.py:41
  112.8 12.4 %attn.1 = (bf16[512,1024]{1,0:T(8,128)(2,1)}, bf16[512,1536]{1,0:T(8,128)(2,1)}, bf16[512,512]{1,0:T(8,128)(2,1)}, bf16[16,256,256]{2,1,0:T(8,128)(2,1)}) custom-call(s32[4]{0:T(128)} %get-tuple-element.245.refs_0_.info, f32[8]{0:T(128)} %dynamic_slice.93.refs_1_, bf16[256,1024]{1,0:T(8,128)(2,1)} %hidden.1, ...), custom_call_target="tpu_custom_call" | custom-call | flops 1153500053504 | bytes 1000000 | tf_op jit(solution)/shard_map/attn/pallas_call | solution.py:96
  125.2 4.4 %dense.1.part = f32[512,1024]{1,0:T(8,128)} custom-call(s32[4]{0:T(128)} %get-tuple-element.245.refs_0_.info, bf16[512,512]{1,0:T(8,128)(2,1)} %get-tuple-element.143.refs_1_.left, bf16[4,128,512]{2,1,0:T(8,128)(2,1)} %copy-done.3, bf16[4,128,512]{2,1,0:T(8,128)(2,1)} %copy-done.13, bf16[2,2,128,512]{3,2,1,0:T(8,128)(2,1)} %collective-permute-done.6.refs_4_.refs_11_), custom_call_target="tpu_custom_call" | custom-call | flops 1153500053504 | bytes 1000000 | tf_op jit(solution)/shard_map/dense/pallas_call | solution.py:96
  133.0 4.1 all-to-all-start.5
  146.9 9.7 %collective-permute-done.3.refs_6_.refs_7_ = bf16[4,128,512]{2,1,0:T(8,128)(2,1)} collective-permute-done((bf16[4,128,512]{2,1,0:T(8,128)(2,1)}, bf16[4,128,512]{2,1,0:T(8,128)(2,1)}, u32[]{:S(2)}, u32[]{:S(2)}) %collective-permute-start.3) | collective-permute-done | bytes 524320 | tf_op jit(solution)/shard_map/ppermute | solution.py:41
  157.7 4.4 %all-to-all-start.6 = ((bf16[4,256,384]{2,1,0:T(8,128)(2,1)}), bf16[4,256,384]{2,1,0:T(8,128)(2,1)}, u32[]{:S(2)}, u32[]{:S(2)}) async-start(bf16[4,256,384]{2,1,0:T(8,128)(2,1)} %broadcast_in_dim.99), calls=%async_computation.6 | async-start | bytes 1572864 | tf_op jit(solution)/shard_map/all_to_all | solution.py:57
  163.5 4.6 %middle.1 = (f32[512,1024]{1,0:T(8,128)}, bf16[512,1024]{1,0:T(8,128)(2,1)}) custom-call(bf16[256,1024]{1,0:T(8,128)(2,1)} %hidden.1, bf16[256,1024]{1,0:T(8,128)(2,1)} %collective-permute-done.5.refs_3_.other, f32[512,1024]{1,0:T(8,128)} %dense.1.part, f32[512,1024]{1,0:T(8,128)} %copy-done.31, f32[1,1024]{1,0:T(1,128)} %bitcast.97, f32[1,1024]{1,0:T(1,128)} %bitcast.94, ...), custom_call_target="tpu_custom_call" | custom-call | flops 1153500053504 | bytes 1000000 | tf_op jit(solution)/shard_map/middle/pallas_call | solution.py:96
  168.1 2.8 collective-permute-start.12
  172.1 4.1 collective-permute-done.13.refs_13_.refs_3_
  178.1 3.7 all-to-all-done.6.refs_16_.refs_6_
  183.0 6.3 %collective-permute-done.11.refs_10_.refs_11_ = bf16[4,128,512]{2,1,0:T(8,128)(2,1)} collective-permute-done((bf16[4,128,512]{2,1,0:T(8,128)(2,1)}, bf16[4,128,512]{2,1,0:T(8,128)(2,1)}, u32[]{:S(2)}, u32[]{:S(2)}) %collective-permute-start.11) | collective-permute-done | bytes 524320 | tf_op jit(solution)/shard_map/ppermute | solution.py:41
  189.3 11.3 %up.1 = (bf16[512,2048]{1,0:T(8,128)(2,1)}, f32[512,2048]{1,0:T(8,128)}) custom-call(s32[4]{0:T(128)} %get-tuple-element.245.refs_0_.info, bf16[512,1024]{1,0:T(8,128)(2,1)} %get-tuple-element.117.refs_1_.left, f32[1,2048]{1,0:T(1,128)} %pad_maximum_fusion.5.refs_2_, bf16[4,128,512]{2,1,0:T(8,128)(2,1)} %all-to-all-done.2.refs_3_.refs_4_, ...), custom_call_target="tpu_custom_call" | custom-call | flops 1153500053504 | bytes 1000000 | tf_op jit(solution)/shard_map/up/pallas_call | solution.py:96
  200.7 4.6 %gdown.2 = (bf16[4,256,512]{2,1,0:T(8,128)(2,1)}, bf16[4,256,512]{2,1,0:T(8,128)(2,1)}) custom-call(s32[4]{0:T(128)} %get-tuple-element.245.refs_0_.info, bf16[512,2048]{1,0:T(8,128)(2,1)} %get-tuple-element.146.left.refs_1_, bf16[256,1024]{1,0:T(8,128)(2,1)} %refs_4_.1, bf16[256,1024]{1,0:T(8,128)(2,1)} %collective-permute-done.12.refs_2_.other.refs_5_), custom_call_target="tpu_custom_call" | custom-call | flops 15226200064 | bytes 1000000 | tf_op jit(solution)/shard_map/gdown/pallas_call | solution.py:96
  206.5 4.5 %gdown.3 = (bf16[4,256,512]{2,1,0:T(8,128)(2,1)}, bf16[4,256,512]{2,1,0:T(8,128)(2,1)}) custom-call(s32[4]{0:T(128)} %get-tuple-element.245.refs_0_.info, bf16[512,2048]{1,0:T(8,128)(2,1)} %get-tuple-element.146.left.refs_1_, bf16[256,1024]{1,0:T(8,128)(2,1)} %refs_4_.1, bf16[256,1024]{1,0:T(8,128)(2,1)} %collective-permute-done.12.refs_2_.other.refs_5_), custom_call_target="tpu_custom_call" | custom-call | flops 15226200064 | bytes 1000000 | tf_op jit(solution)/shard_map/gdown/pallas_call | solution.py:96
  211.2 6.2 %collective-permute-done.15.refs_15_.refs_5_ = bf16[4,128,640]{2,1,0:T(8,128)(2,1)} collective-permute-done((bf16[4,128,640]{2,1,0:T(8,128)(2,1)}, bf16[4,128,640]{2,1,0:T(8,128)(2,1)}, u32[]{:S(2)}, u32[]{:S(2)}) %collective-permute-start.15) | collective-permute-done | bytes 655392 | tf_op jit(solution)/shard_map/ppermute | solution.py:41
  217.4 14.9 %feed_back.1 = (bf16[512,2048]{1,0:T(8,128)(2,1)}, f32[1,2048]{1,0:T(1,128)}, f32[512,1024]{1,0:T(8,128)}) custom-call(s32[4]{0:T(128)} %get-tuple-element.245.refs_0_.info, bf16[256,1024]{1,0:T(8,128)(2,1)} %refs_4_.1, bf16[256,1024]{1,0:T(8,128)(2,1)} %collective-permute-done.12.refs_2_.other.refs_5_, f32[512,2048]{1,0:T(8,128)} %get-tuple-element.119.refs_3_, ...), custom_call_target="tpu_custom_call" | custom-call | flops 1153500053504 | bytes 1000000 | tf_op jit(solution)/shard_map/feed_back/pallas_call | solution.py:96
  233.8 5.5 %gup.1 = (bf16[4,256,512]{2,1,0:T(8,128)(2,1)}, bf16[4,256,512]{2,1,0:T(8,128)(2,1)}, bf16[4,256,512]{2,1,0:T(8,128)(2,1)}, bf16[4,256,512]{2,1,0:T(8,128)(2,1)}) custom-call(bf16[512,1024]{1,0:T(8,128)(2,1)} %get-tuple-element.117.refs_1_.left, bf16[512,2048]{1,0:T(8,128)(2,1)} %get-tuple-element.121.right), custom_call_target="tpu_custom_call" | custom-call | flops 18686699520 | bytes 1000000 | tf_op jit(solution)/shard_map/gup/pallas_call | solution.py:96
  241.5 2.8 gdown_x.2
  244.3 4.7 %all-to-all-start.7 = ((bf16[4,256,512]{2,1,0:T(8,128)(2,1)}), bf16[4,256,512]{2,1,0:T(8,128)(2,1)}, u32[]{:S(2)}, u32[]{:S(2)}) async-start(bf16[4,256,512]{2,1,0:T(8,128)(2,1)} %gdown_x.2), calls=%async_computation.7 | async-start | bytes 2097152 | tf_op jit(solution)/shard_map/all_to_all | solution.py:57
  250.3 12.8 %attn_back.1 = (f32[256,1024]{1,0:T(8,128)}, bf16[512,1024]{1,0:T(8,128)(2,1)}, f32[3,1024]{1,0:T(4,128)}, bf16[512,1536]{1,0:T(8,128)(2,1)}, f32[2,512]{1,0:T(2,128)}) custom-call(s32[4]{0:T(128)} %get-tuple-element.245.refs_0_.info, f32[512,1024]{1,0:T(8,128)} %get-tuple-element.133.refs_1_, f32[512,1024]{1,0:T(8,128)} %copy-done.32, ...), custom_call_target="tpu_custom_call" | custom-call | flops 1153500053504 | bytes 1000000 | tf_op jit(solution)/shard_map/attn_back/pallas_call | solution.py:96
  263.2 5.2 %gqkv.1 = (bf16[4,256,384]{2,1,0:T(8,128)(2,1)}, bf16[4,256,384]{2,1,0:T(8,128)(2,1)}, bf16[4,256,384]{2,1,0:T(8,128)(2,1)}, bf16[4,256,384]{2,1,0:T(8,128)(2,1)}) custom-call(s32[4]{0:T(128)} %get-tuple-element.245.refs_0_.info, bf16[512,1024]{1,0:T(8,128)(2,1)} %get-tuple-element.128.left, bf16[512,1536]{1,0:T(8,128)(2,1)} %get-tuple-element.180.refs_0_.refs_1_), custom_call_target="tpu_custom_call" | custom-call | flops 17648549888 | bytes 1000000 | tf_op jit(solution)/shard_map/gqkv/pallas_call | solution.py:96
  268.4 2.7 gdown_x.3
  271.1 2.7 gup_y.2
  273.8 3.0 gdense.1
  276.8 8.4 %output.1 = (f32[256,1024]{1,0:T(8,128)}, f32[256,1024]{1,0:T(8,128)}) custom-call(s32[4]{0:T(128)} %get-tuple-element.245.refs_0_.info, bf16[512,2048]{1,0:T(8,128)(2,1)} %get-tuple-element.146.left.refs_1_, bf16[4,128,640]{2,1,0:T(8,128)(2,1)} %all-to-all-done.5.refs_12_.refs_2_, bf16[4,128,640]{2,1,0:T(8,128)(2,1)} %collective-permute-done.13.refs_13_.refs_3_, ...), custom_call_target="tpu_custom_call" | custom-call | flops 29068199936 | bytes 1000000 | tf_op jit(solution)/shard_map/output/pallas_call | solution.py:96
  286.9 2.8 gup_y.3
  292.1 4.5 %all-to-all-start.8 = ((bf16[4,256,512]{2,1,0:T(8,128)(2,1)}), bf16[4,256,512]{2,1,0:T(8,128)(2,1)S(1)}, u32[]{:S(2)}, u32[]{:S(2)}) async-start(bf16[4,256,512]{2,1,0:T(8,128)(2,1)} %gdown_x.3), calls=%async_computation.8 | async-start | bytes 2097152 | tf_op jit(solution)/shard_map/all_to_all | solution.py:57
  304.4 11.2 %collective-permute-done.24.refs_1_ = bf16[4,128,512]{2,1,0:T(8,128)(2,1)} collective-permute-done((bf16[4,128,512]{2,1,0:T(8,128)(2,1)S(1)}, bf16[4,128,512]{2,1,0:T(8,128)(2,1)}, u32[]{:S(2)}, u32[]{:S(2)}) %collective-permute-start.24) | collective-permute-done | bytes 524320 | tf_op jit(solution)/shard_map/ppermute | solution.py:41
  316.9 2.7 gup_x.1
  321.8 3.5 all-to-all-start.9
  327.7 4.2 collective-permute-done.28.recv
  335.8 14.7 %all-to-all-done.9.refs_0_ = bf16[4,128,1024]{2,1,0:T(8,128)(2,1)S(1)} async-done(((bf16[4,128,1024]{2,1,0:T(8,128)(2,1)}), bf16[4,128,1024]{2,1,0:T(8,128)(2,1)S(1)}, u32[]{:S(2)}, u32[]{:S(2)}) %all-to-all-start.9) | async-done | bytes 1048608 | tf_op jit(solution)/shard_map/all_to_all | solution.py:57
  350.6 3.0 gdown_z.1
  359.2 7.2 %gnorm.1 = (f32[256,1024]{1,0:T(8,128)}, f32[256,1024]{1,0:T(8,128)}) custom-call(s32[4]{0:T(128)} %get-tuple-element.245.refs_0_.info, bf16[512,1536]{1,0:T(8,128)(2,1)} %get-tuple-element.180.refs_0_.refs_1_, bf16[4,128,768]{2,1,0:T(8,128)(2,1)} %all-to-all-done.refs_7_.refs_2_, bf16[4,128,768]{2,1,0:T(8,128)(2,1)} %collective-permute-done.refs_8_.refs_3_, ...), custom_call_target="tpu_custom_call" | custom-call | flops 24915599360 | bytes 1000000 | tf_op jit(solution)/shard_map/gnorm/pallas_call | solution.py:96
  371.6 4.5 %all-to-all-start.10 = ((bf16[4,128,768]{2,1,0:T(8,128)(2,1)}), bf16[4,128,768]{2,1,0:T(8,128)(2,1)}, u32[]{:S(2)}, u32[]{:S(2)}) async-start(bf16[4,128,768]{2,1,0:T(8,128)(2,1)} %gqkv_x.1), calls=%async_computation.10 | async-start | bytes 1572864 | tf_op jit(solution)/shard_map/all_to_all | solution.py:57
  377.5 3.8 input_grad.1
  392.9 3.5 all-to-all-done.10.refs_0_
  401.7 3.5 all-to-all-start.11
  428.4 2.7 add_convert_fusion
  (283 shorter events, 120.7 us)
Async XLA Ops:
  7.2 25.1 %all-to-all-start = ((bf16[4,128,768]{2,1,0:T(8,128)(2,1)}), bf16[4,128,768]{2,1,0:T(8,128)(2,1)}, u32[]{:S(2)}, u32[]{:S(2)}) async-start(bf16[4,128,768]{2,1,0:T(8,128)(2,1)} %broadcast_in_dim.53), calls=%async_computation | async-start | bytes 1572864 | tf_op jit(solution)/shard_map/all_to_all | solution.py:57
  33.3 25.2 %all-to-all-start.1 = ((bf16[4,144,768]{2,1,0:T(8,128)(2,1)}), bf16[4,144,768]{2,1,0:T(8,128)(2,1)S(1)}, u32[]{:S(2)}, u32[]{:S(2)}) async-start(bf16[4,144,768]{2,1,0:T(8,128)(2,1)} %broadcast_in_dim.61), calls=%async_computation.1 | async-start | bytes 1769472 | tf_op jit(solution)/shard_map/all_to_all | solution.py:57
  36.8 23.0 %collective-permute-start = (bf16[4,128,768]{2,1,0:T(8,128)(2,1)}, bf16[4,128,768]{2,1,0:T(8,128)(2,1)}, u32[]{:S(2)}, u32[]{:S(2)}) collective-permute-start(bf16[4,128,768]{2,1,0:T(8,128)(2,1)} %all-to-all-done.refs_7_.refs_2_), channel_id=1, source_target_pairs={{0,1},{1,0},{2,3},{3,2},{4,5},{5,4},{6,7},{7,6},{8,9},{9,8},{10,11... | collective-permute-start | bytes 2359304 | tf_op jit(solution)/shard_map/ppermute | solution.py:41
  58.5 20.6 %collective-permute-start.2 = (bf16[4,144,768]{2,1,0:T(8,128)(2,1)S(1)}, bf16[4,144,768]{2,1,0:T(8,128)(2,1)S(1)}, u32[]{:S(2)}, u32[]{:S(2)}) collective-permute-start(bf16[4,144,768]{2,1,0:T(8,128)(2,1)S(1)} %all-to-all-done.1.refs_9_.refs_4_), channel_id=1, source_target_pairs={{0,1},{1,0},{2,3},{3,2},{4,5},{5,4},{6,7},{7,6},{8,9},{9,8},{10,11... | collective-permute-start | bytes 2654216 | tf_op jit(solution)/shard_map/ppermute | solution.py:41
  60.7 18.2 %all-to-all-start.2 = ((bf16[4,128,512]{2,1,0:T(8,128)(2,1)}), bf16[4,128,512]{2,1,0:T(8,128)(2,1)}, u32[]{:S(2)}, u32[]{:S(2)}) async-start(bf16[4,128,512]{2,1,0:T(8,128)(2,1)} %broadcast_in_dim.52), calls=%async_computation.2 | async-start | bytes 1048576 | tf_op jit(solution)/shard_map/all_to_all | solution.py:57
  64.9 47.9 %collective-permute-start.5 = (bf16[256,1024]{1,0:T(8,128)(2,1)S(1)}, bf16[256,1024]{1,0:T(8,128)(2,1)}, u32[]{:S(2)}, u32[]{:S(2)}) collective-permute-start(bf16[256,1024]{1,0:T(8,128)(2,1)S(1)} %copy-done.35), channel_id=1, source_target_pairs={{0,8},{1,9},{2,10},{3,11},{4,12},{5,13},{6,14},{7,15},{8,0},{9,1},... | collective-permute-start | bytes 1572872 | tf_op jit(solution)/shard_map/ppermute | solution.py:41
  78.9 21.0 %collective-permute-start.1 = (bf16[4,128,512]{2,1,0:T(8,128)(2,1)}, bf16[4,128,512]{2,1,0:T(8,128)(2,1)}, u32[]{:S(2)}, u32[]{:S(2)}) collective-permute-start(bf16[4,128,512]{2,1,0:T(8,128)(2,1)} %all-to-all-done.2.refs_3_.refs_4_), channel_id=1, source_target_pairs={{0,1},{1,0},{2,3},{3,2},{4,5},{5,4},{6,7},{7,6},{8,9},{9,8},{10,11... | collective-permute-start | bytes 1572872 | tf_op jit(solution)/shard_map/ppermute | solution.py:41
  80.1 17.4 %all-to-all-start.3 = ((bf16[4,128,512]{2,1,0:T(8,128)(2,1)}), bf16[4,128,512]{2,1,0:T(8,128)(2,1)S(1)}, u32[]{:S(2)}, u32[]{:S(2)}) async-start(bf16[4,128,512]{2,1,0:T(8,128)(2,1)} %broadcast_in_dim.96), calls=%async_computation.3 | async-start | bytes 1048576 | tf_op jit(solution)/shard_map/all_to_all | solution.py:57
  97.5 12.0 %collective-permute-start.4 = (bf16[4,128,512]{2,1,0:T(8,128)(2,1)S(1)}, bf16[4,128,512]{2,1,0:T(8,128)(2,1)S(1)}, u32[]{:S(2)}, u32[]{:S(2)}) collective-permute-start(bf16[4,128,512]{2,1,0:T(8,128)(2,1)S(1)} %all-to-all-done.3.refs_2_.refs_9_), channel_id=1, source_target_pairs={{0,1},{1,0},{2,3},{3,2},{4,5},{5,4},{6,7},{7,6},{8,9},{9,8},{10,11... | collective-permute-start | bytes 1572872 | tf_op jit(solution)/shard_map/ppermute | solution.py:41
  100.9 24.4 %all-to-all-start.4 = ((bf16[4,128,512]{2,1,0:T(8,128)(2,1)}), bf16[4,128,512]{2,1,0:T(8,128)(2,1)}, u32[]{:S(2)}, u32[]{:S(2)}) async-start(bf16[4,128,512]{2,1,0:T(8,128)(2,1)} %broadcast_in_dim.51), calls=%async_computation.4 | async-start | bytes 1048576 | tf_op jit(solution)/shard_map/all_to_all | solution.py:57
  110.4 14.9 %collective-permute-start.6 = (bf16[2,2,128,512]{3,2,1,0:T(8,128)(2,1)}, bf16[2,2,128,512]{3,2,1,0:T(8,128)(2,1)}, u32[]{:S(2)}, u32[]{:S(2)}) collective-permute-start(bf16[2,2,128,512]{3,2,1,0:T(8,128)(2,1)} %pad_maximum_fusion.1), channel_id=1, source_target_pairs={{0,8},{1,9},{2,10},{3,11},{4,12},{5,13},{6,14},{7,15},{8,0},{9,1},... | collective-permute-start | bytes 1572872 | tf_op jit(solution)/shard_map/ppermute | solution.py:41
  129.7 32.4 %collective-permute-start.7 = (f32[512,1024]{1,0:T(8,128)}, f32[512,1024]{1,0:T(8,128)S(1)}, u32[]{:S(2)}, u32[]{:S(2)}) collective-permute-start(f32[512,1024]{1,0:T(8,128)} %dense.1.part), channel_id=1, source_target_pairs={{0,8},{1,9},{2,10},{3,11},{4,12},{5,13},{6,14},{7,15},{8,0},{9,1},... | collective-permute-start | bytes 6291464 | tf_op jit(solution)/shard_map/ppermute | solution.py:41
  133.0 23.8 %all-to-all-start.5 = ((bf16[4,128,640]{2,1,0:T(8,128)(2,1)}), bf16[4,128,640]{2,1,0:T(8,128)(2,1)}, u32[]{:S(2)}, u32[]{:S(2)}) async-start(bf16[4,128,640]{2,1,0:T(8,128)(2,1)} %broadcast_in_dim.97), calls=%async_computation.5 | async-start | bytes 1310720 | tf_op jit(solution)/shard_map/all_to_all | solution.py:57
  142.3 25.7 %collective-permute-start.8 = (bf16[4,128,512]{2,1,0:T(8,128)(2,1)}, bf16[4,128,512]{2,1,0:T(8,128)(2,1)}, u32[]{:S(2)}, u32[]{:S(2)}) collective-permute-start(bf16[4,128,512]{2,1,0:T(8,128)(2,1)} %all-to-all-done.2.refs_3_.refs_4_), channel_id=1, source_target_pairs={{0,16},{1,17},{2,18},{3,19},{4,20},{5,21},{6,22},{7,23},{8,24},{9,... | collective-permute-start | bytes 1572872 | tf_op jit(solution)/shard_map/ppermute | solution.py:41
  143.6 13.0 %collective-permute-start.3 = (bf16[4,128,512]{2,1,0:T(8,128)(2,1)}, bf16[4,128,512]{2,1,0:T(8,128)(2,1)}, u32[]{:S(2)}, u32[]{:S(2)}) collective-permute-start(bf16[4,128,512]{2,1,0:T(8,128)(2,1)} %all-to-all-done.4.refs_5_.refs_6_), channel_id=1, source_target_pairs={{0,1},{1,0},{2,3},{3,2},{4,5},{5,4},{6,7},{7,6},{8,9},{9,8},{10,11... | collective-permute-start | bytes 1572872 | tf_op jit(solution)/shard_map/ppermute | solution.py:41
  145.4 25.4 %collective-permute-start.9 = (bf16[4,128,512]{2,1,0:T(8,128)(2,1)}, bf16[4,128,512]{2,1,0:T(8,128)(2,1)}, u32[]{:S(2)}, u32[]{:S(2)}) collective-permute-start(bf16[4,128,512]{2,1,0:T(8,128)(2,1)} %collective-permute-done.1.refs_4_.refs_5_), channel_id=1, source_target_pairs={{0,16},{1,17},{2,18},{3,19},{4,20},{5,21},{6,22},{7,23},{8,24},{9,... | collective-permute-start | bytes 1572872 | tf_op jit(solution)/shard_map/ppermute | solution.py:41
  145.6 32.5 %collective-permute-start.10 = (bf16[4,128,512]{2,1,0:T(8,128)(2,1)}, bf16[4,128,512]{2,1,0:T(8,128)(2,1)}, u32[]{:S(2)}, u32[]{:S(2)}) collective-permute-start(bf16[4,128,512]{2,1,0:T(8,128)(2,1)} %all-to-all-done.4.refs_5_.refs_6_), channel_id=1, source_target_pairs={{0,16},{1,17},{2,18},{3,19},{4,20},{5,21},{6,22},{7,23},{8,24},{9,... | collective-permute-start | bytes 1572872 | tf_op jit(solution)/shard_map/ppermute | solution.py:41
  156.5 32.8 %collective-permute-start.11 = (bf16[4,128,512]{2,1,0:T(8,128)(2,1)}, bf16[4,128,512]{2,1,0:T(8,128)(2,1)}, u32[]{:S(2)}, u32[]{:S(2)}) collective-permute-start(bf16[4,128,512]{2,1,0:T(8,128)(2,1)} %collective-permute-done.3.refs_6_.refs_7_), channel_id=1, source_target_pairs={{0,16},{1,17},{2,18},{3,19},{4,20},{5,21},{6,22},{7,23},{8,24},{9,... | collective-permute-start | bytes 1572872 | tf_op jit(solution)/shard_map/ppermute | solution.py:41
  157.7 24.1 %all-to-all-start.6 = ((bf16[4,256,384]{2,1,0:T(8,128)(2,1)}), bf16[4,256,384]{2,1,0:T(8,128)(2,1)}, u32[]{:S(2)}, u32[]{:S(2)}) async-start(bf16[4,256,384]{2,1,0:T(8,128)(2,1)} %broadcast_in_dim.99), calls=%async_computation.6 | async-start | bytes 1572864 | tf_op jit(solution)/shard_map/all_to_all | solution.py:57
  162.1 14.1 %collective-permute-start.13 = (bf16[4,128,640]{2,1,0:T(8,128)(2,1)}, bf16[4,128,640]{2,1,0:T(8,128)(2,1)}, u32[]{:S(2)}, u32[]{:S(2)}) collective-permute-start(bf16[4,128,640]{2,1,0:T(8,128)(2,1)} %all-to-all-done.5.refs_12_.refs_2_), channel_id=1, source_target_pairs={{0,1},{1,0},{2,3},{3,2},{4,5},{5,4},{6,7},{7,6},{8,9},{9,8},{10,11... | collective-permute-start | bytes 1966088 | tf_op jit(solution)/shard_map/ppermute | solution.py:41
  168.1 32.6 %collective-permute-start.12 = (bf16[256,1024]{1,0:T(8,128)(2,1)}, bf16[256,1024]{1,0:T(8,128)(2,1)}, u32[]{:S(2)}, u32[]{:S(2)}) collective-permute-start(bf16[256,1024]{1,0:T(8,128)(2,1)} %refs_4_.1), channel_id=1, source_target_pairs={{0,8},{1,9},{2,10},{3,11},{4,12},{5,13},{6,14},{7,15},{8,0},{9,1},... | collective-permute-start | bytes 1572872 | tf_op jit(solution)/shard_map/ppermute | solution.py:41
  170.8 40.4 %collective-permute-start.14 = (bf16[4,128,640]{2,1,0:T(8,128)(2,1)}, bf16[4,128,640]{2,1,0:T(8,128)(2,1)}, u32[]{:S(2)}, u32[]{:S(2)}) collective-permute-start(bf16[4,128,640]{2,1,0:T(8,128)(2,1)} %all-to-all-done.5.refs_12_.refs_2_), channel_id=1, source_target_pairs={{0,16},{1,17},{2,18},{3,19},{4,20},{5,21},{6,22},{7,23},{8,24},{9,... | collective-permute-start | bytes 1966088 | tf_op jit(solution)/shard_map/ppermute | solution.py:41
  176.2 41.2 %collective-permute-start.15 = (bf16[4,128,640]{2,1,0:T(8,128)(2,1)}, bf16[4,128,640]{2,1,0:T(8,128)(2,1)}, u32[]{:S(2)}, u32[]{:S(2)}) collective-permute-start(bf16[4,128,640]{2,1,0:T(8,128)(2,1)} %collective-permute-done.13.refs_13_.refs_3_), channel_id=1, source_target_pairs={{0,16},{1,17},{2,18},{3,19},{4,20},{5,21},{6,22},{7,23},{8,24},{9,... | collective-permute-start | bytes 1966088 | tf_op jit(solution)/shard_map/ppermute | solution.py:41
  181.8 35.6 %collective-permute-start.16 = (bf16[4,256,384]{2,1,0:T(8,128)(2,1)}, bf16[4,256,384]{2,1,0:T(8,128)(2,1)}, u32[]{:S(2)}, u32[]{:S(2)}) collective-permute-start(bf16[4,256,384]{2,1,0:T(8,128)(2,1)} %all-to-all-done.6.refs_16_.refs_6_), channel_id=1, source_target_pairs={{0,1},{1,0},{2,3},{3,2},{4,5},{5,4},{6,7},{7,6},{8,9},{9,8},{10,11... | collective-permute-start | bytes 2359304 | tf_op jit(solution)/shard_map/ppermute | solution.py:41
  205.3 36.2 %collective-permute-start.19 = (bf16[4,256,512]{2,1,0:T(8,128)(2,1)}, bf16[4,256,512]{2,1,0:T(8,128)(2,1)}, u32[]{:S(2)}, u32[]{:S(2)}) collective-permute-start(bf16[4,256,512]{2,1,0:T(8,128)(2,1)} %get-tuple-element.130), channel_id=1, source_target_pairs={{0,1},{1,0},{2,3},{3,2},{4,5},{5,4},{6,7},{7,6},{8,9},{9,8},{10,11... | collective-permute-start | bytes 3145736 | tf_op jit(solution)/shard_map/ppermute | solution.py:41
  211.0 57.4 %collective-permute-start.18 = (bf16[4,256,512]{2,1,0:T(8,128)(2,1)}, bf16[4,256,512]{2,1,0:T(8,128)(2,1)}, u32[]{:S(2)}, u32[]{:S(2)}) collective-permute-start(bf16[4,256,512]{2,1,0:T(8,128)(2,1)} %get-tuple-element.127), channel_id=1, source_target_pairs={{0,1},{1,0},{2,3},{3,2},{4,5},{5,4},{6,7},{7,6},{8,9},{9,8},{10,11... | collective-permute-start | bytes 3145736 | tf_op jit(solution)/shard_map/ppermute | solution.py:41
  232.4 16.6 %collective-permute-start.20 = (f32[512,1024]{1,0:T(8,128)}, f32[512,1024]{1,0:T(8,128)S(1)}, u32[]{:S(2)}, u32[]{:S(2)}) collective-permute-start(f32[512,1024]{1,0:T(8,128)} %get-tuple-element.133.refs_1_), channel_id=1, source_target_pairs={{0,8},{1,9},{2,10},{3,11},{4,12},{5,13},{6,14},{7,15},{8,0},{9,1},... | collective-permute-start | bytes 6291464 | tf_op jit(solution)/shard_map/ppermute | solution.py:41
  239.3 31.8 %collective-permute-start.17 = (bf16[4,256,512]{2,1,0:T(8,128)(2,1)}, bf16[4,256,512]{2,1,0:T(8,128)(2,1)}, u32[]{:S(2)}, u32[]{:S(2)}) collective-permute-start(bf16[4,256,512]{2,1,0:T(8,128)(2,1)} %get-tuple-element.123), channel_id=1, source_target_pairs={{0,16},{1,17},{2,18},{3,19},{4,20},{5,21},{6,22},{7,23},{8,24},{9,... | collective-permute-start | bytes 3145736 | tf_op jit(solution)/shard_map/ppermute | solution.py:41
  240.5 46.3 %collective-permute-start.21 = (bf16[4,256,512]{2,1,0:T(8,128)(2,1)}, bf16[4,256,512]{2,1,0:T(8,128)(2,1)}, u32[]{:S(2)}, u32[]{:S(2)}) collective-permute-start(bf16[4,256,512]{2,1,0:T(8,128)(2,1)} %get-tuple-element.149), channel_id=1, source_target_pairs={{0,16},{1,17},{2,18},{3,19},{4,20},{5,21},{6,22},{7,23},{8,24},{9,... | collective-permute-start | bytes 3145736 | tf_op jit(solution)/shard_map/ppermute | solution.py:41
  244.3 47.8 %all-to-all-start.7 = ((bf16[4,256,512]{2,1,0:T(8,128)(2,1)}), bf16[4,256,512]{2,1,0:T(8,128)(2,1)}, u32[]{:S(2)}, u32[]{:S(2)}) async-start(bf16[4,256,512]{2,1,0:T(8,128)(2,1)} %gdown_x.2), calls=%async_computation.7 | async-start | bytes 2097152 | tf_op jit(solution)/shard_map/all_to_all | solution.py:57
  290.6 13.8 %collective-permute-start.25 = (bf16[4,128,512]{2,1,0:T(8,128)(2,1)}, bf16[4,128,512]{2,1,0:T(8,128)(2,1)}, u32[]{:S(2)}, u32[]{:S(2)}) collective-permute-start(bf16[4,128,512]{2,1,0:T(8,128)(2,1)} %get-tuple-element.159), channel_id=1, source_target_pairs={{0,1},{1,0},{2,3},{3,2},{4,5},{5,4},{6,7},{7,6},{8,9},{9,8},{10,11... | collective-permute-start | bytes 1572872 | tf_op jit(solution)/shard_map/ppermute | solution.py:41
  291.9 23.8 %collective-permute-start.24 = (bf16[4,128,512]{2,1,0:T(8,128)(2,1)S(1)}, bf16[4,128,512]{2,1,0:T(8,128)(2,1)}, u32[]{:S(2)}, u32[]{:S(2)}) collective-permute-start(bf16[4,128,512]{2,1,0:T(8,128)(2,1)S(1)} %copy-done.36), channel_id=1, source_target_pairs={{0,1},{1,0},{2,3},{3,2},{4,5},{5,4},{6,7},{7,6},{8,9},{9,8},{10,11... | collective-permute-start | bytes 1572872 | tf_op jit(solution)/shard_map/ppermute | solution.py:41
  292.1 29.7 %all-to-all-start.8 = ((bf16[4,256,512]{2,1,0:T(8,128)(2,1)}), bf16[4,256,512]{2,1,0:T(8,128)(2,1)S(1)}, u32[]{:S(2)}, u32[]{:S(2)}) async-start(bf16[4,256,512]{2,1,0:T(8,128)(2,1)} %gdown_x.3), calls=%async_computation.8 | async-start | bytes 2097152 | tf_op jit(solution)/shard_map/all_to_all | solution.py:57
  296.6 28.8 %collective-permute-start.26 = (bf16[4,256,384]{2,1,0:T(8,128)(2,1)}, bf16[4,256,384]{2,1,0:T(8,128)(2,1)}, u32[]{:S(2)}, u32[]{:S(2)}) collective-permute-start(bf16[4,256,384]{2,1,0:T(8,128)(2,1)} %get-tuple-element.169), channel_id=1, source_target_pairs={{0,16},{1,17},{2,18},{3,19},{4,20},{5,21},{6,22},{7,23},{8,24},{9,... | collective-permute-start | bytes 2359304 | tf_op jit(solution)/shard_map/ppermute | solution.py:41
  297.8 34.1 %collective-permute-start.28 = (bf16[4,256,384]{2,1,0:T(8,128)(2,1)S(1)}, bf16[4,256,384]{2,1,0:T(8,128)(2,1)}, u32[]{:S(2)}, u32[]{:S(2)}) collective-permute-start(bf16[4,256,384]{2,1,0:T(8,128)(2,1)S(1)} %copy-done.34), channel_id=1, source_target_pairs={{0,16},{1,17},{2,18},{3,19},{4,20},{5,21},{6,22},{7,23},{8,24},{9,... | collective-permute-start | bytes 2359304 | tf_op jit(solution)/shard_map/ppermute | solution.py:41
  298.2 130.2 %collective-permute-start.30 = (f32[256,1024]{1,0:T(8,128)}, f32[256,1024]{1,0:T(8,128)}, u32[]{:S(2)}, u32[]{:S(2)}) collective-permute-start(f32[256,1024]{1,0:T(8,128)} %get-tuple-element.191), channel_id=1, source_target_pairs={{0,8},{1,9},{2,10},{3,11},{4,12},{5,13},{6,14},{7,15},{8,0},{9,1},... | collective-permute-start | bytes 3145736 | tf_op jit(solution)/shard_map/ppermute | solution.py:41
  315.7 39.1 %collective-permute-start.23 = (bf16[4,128,512]{2,1,0:T(8,128)(2,1)}, bf16[4,128,512]{2,1,0:T(8,128)(2,1)}, u32[]{:S(2)}, u32[]{:S(2)}) collective-permute-start(bf16[4,128,512]{2,1,0:T(8,128)(2,1)} %get-tuple-element.156), channel_id=1, source_target_pairs={{0,1},{1,0},{2,3},{3,2},{4,5},{5,4},{6,7},{7,6},{8,9},{9,8},{10,11... | collective-permute-start | bytes 1572872 | tf_op jit(solution)/shard_map/ppermute | solution.py:41
  321.8 28.7 %all-to-all-start.9 = ((bf16[4,128,1024]{2,1,0:T(8,128)(2,1)}), bf16[4,128,1024]{2,1,0:T(8,128)(2,1)S(1)}, u32[]{:S(2)}, u32[]{:S(2)}) async-start(bf16[4,128,1024]{2,1,0:T(8,128)(2,1)} %gup_x.1), calls=%async_computation.9 | async-start | bytes 2097152 | tf_op jit(solution)/shard_map/all_to_all | solution.py:57
  334.4 32.0 %collective-permute-start.29 = (bf16[4,128,384]{2,1,0:T(8,128)(2,1)}, bf16[4,128,384]{2,1,0:T(8,128)(2,1)S(1)}, u32[]{:S(2)}, u32[]{:S(2)}) collective-permute-start(bf16[4,128,384]{2,1,0:T(8,128)(2,1)} %get-tuple-element.179), channel_id=1, source_target_pairs={{0,1},{1,0},{2,3},{3,2},{4,5},{5,4},{6,7},{7,6},{8,9},{9,8},{10,11... | collective-permute-start | bytes 1179656 | tf_op jit(solution)/shard_map/ppermute | solution.py:41
  335.6 30.8 %collective-permute-start.27 = (bf16[4,128,384]{2,1,0:T(8,128)(2,1)S(1)}, bf16[4,128,384]{2,1,0:T(8,128)(2,1)}, u32[]{:S(2)}, u32[]{:S(2)}) collective-permute-start(bf16[4,128,384]{2,1,0:T(8,128)(2,1)S(1)} %copy-done.38), channel_id=1, source_target_pairs={{0,1},{1,0},{2,3},{3,2},{4,5},{5,4},{6,7},{7,6},{8,9},{9,8},{10,11... | collective-permute-start | bytes 1179656 | tf_op jit(solution)/shard_map/ppermute | solution.py:41
  353.6 28.9 %collective-permute-start.44 = (bf16[256,1024]{1,0:T(8,128)(2,1)}, bf16[256,1024]{1,0:T(8,128)(2,1)S(1)}, u32[]{:S(2)}, u32[]{:S(2)}) collective-permute-start(bf16[256,1024]{1,0:T(8,128)(2,1)} %gdown_z.1), channel_id=1, source_target_pairs={{0,16},{1,17},{2,18},{3,19},{4,20},{5,21},{6,22},{7,23},{8,24},{9,... | collective-permute-start | bytes 1572872 | tf_op jit(solution)/shard_map/ppermute | solution.py:41
  359.0 17.1 %collective-permute-start.42 = (bf16[128,1024]{1,0:T(8,128)(2,1)}, bf16[128,1024]{1,0:T(8,128)(2,1)S(1)}, u32[]{:S(2)}, u32[]{:S(2)}) collective-permute-start(bf16[128,1024]{1,0:T(8,128)(2,1)} %gup_z.1), channel_id=1, source_target_pairs={{0,16},{1,17},{2,18},{3,19},{4,20},{5,21},{6,22},{7,23},{8,24},{9,... | collective-permute-start | bytes 786440 | tf_op jit(solution)/shard_map/ppermute | solution.py:41
  367.1 9.3 %collective-permute-start.31 = (f32[256,1024]{1,0:T(8,128)}, f32[256,1024]{1,0:T(8,128)S(1)}, u32[]{:S(2)}, u32[]{:S(2)}) collective-permute-start(f32[256,1024]{1,0:T(8,128)} %get-tuple-element.192), channel_id=1, source_target_pairs={{0,8},{1,9},{2,10},{3,11},{4,12},{5,13},{6,14},{7,15},{8,0},{9,1},... | collective-permute-start | bytes 3145736 | tf_op jit(solution)/shard_map/ppermute | solution.py:41
  371.6 24.8 %all-to-all-start.10 = ((bf16[4,128,768]{2,1,0:T(8,128)(2,1)}), bf16[4,128,768]{2,1,0:T(8,128)(2,1)}, u32[]{:S(2)}, u32[]{:S(2)}) async-start(bf16[4,128,768]{2,1,0:T(8,128)(2,1)} %gqkv_x.1), calls=%async_computation.10 | async-start | bytes 1572864 | tf_op jit(solution)/shard_map/all_to_all | solution.py:57
  383.6 30.5 %collective-permute-start.45 = (f32[256,1024]{1,0:T(8,128)}, f32[256,1024]{1,0:T(8,128)}, u32[]{:S(2)}, u32[]{:S(2)}) collective-permute-start(f32[256,1024]{1,0:T(8,128)} %convert_add_fusion), channel_id=1, source_target_pairs={{0,8},{1,9},{2,10},{3,11},{4,12},{5,13},{6,14},{7,15},{8,0},{9,1},... | collective-permute-start | bytes 3145736 | tf_op jit(solution)/shard_map/ppermute | solution.py:41
  387.2 9.2 %collective-permute-start.34 = (f32[1,12288]{1,0:T(1,128)S(1)}, f32[1,12288]{1,0:T(1,128)S(1)}, u32[]{:S(2)}, u32[]{:S(2)}) collective-permute-start(f32[1,12288]{1,0:T(1,128)S(1)} %add.157), channel_id=1, source_target_pairs={{0,1},{1,0},{2,3},{3,2},{4,5},{5,4},{6,7},{7,6},{8,9},{9,8},{10,11... | collective-permute-start | bytes 147464 | tf_op jit(solution)/shard_map/ppermute | solution.py:41
  396.5 10.0 %collective-permute-start.36 = (f32[1,12288]{1,0:T(1,128)S(1)}, f32[1,12288]{1,0:T(1,128)S(1)}, u32[]{:S(2)}, u32[]{:S(2)}) collective-permute-start(f32[1,12288]{1,0:T(1,128)S(1)} %add.158), channel_id=1, source_target_pairs={{0,4},{1,5},{2,6},{3,7},{4,0},{5,1},{6,2},{7,3},{8,12},{9,13},{10,... | collective-permute-start | bytes 147464 | tf_op jit(solution)/shard_map/ppermute | solution.py:41
  401.7 17.4 %all-to-all-start.11 = ((bf16[4,128,512]{2,1,0:T(8,128)(2,1)}), bf16[4,128,512]{2,1,0:T(8,128)(2,1)S(1)}, u32[]{:S(2)}, u32[]{:S(2)}) async-start(bf16[4,128,512]{2,1,0:T(8,128)(2,1)} %gdense_x.1), calls=%async_computation.11 | async-start | bytes 1048576 | tf_op jit(solution)/shard_map/all_to_all | solution.py:57
  (52 other events, 514.6 us)
